TPU v7x, 256 devices: a whole 4x4x8 slice. The times are simulated.
256 devices in a mesh: lat: 8 (over x, y_hi), lon: 32 (over z, y_lo, core).
Axes of the slice: x: 4, y: 4 (y_hi: 2, y_lo: 2; y = y_hi * 2 + y_lo), z: 8, core: 2. Of those that a mesh axis runs over, the one named last changes fastest.
Arguments:
- coarse: bfloat16 [40, 48, 320], P(None, 'lat', 'lon'), may hold values from -6 to 6
- row_map: int32 [384], replicated, may hold values from 0 to 46, as said below
- row_frac: float32 [384], replicated, may hold values from 0 to 1
- col_map: int32 [2560], replicated, may hold values from 0 to 319, as said below
- col_frac: float32 [2560], replicated, may hold values from 0 to 1
- noise_init: float32 [4, 384, 2560], P(None, 'lat', 'lon'), may hold values from -6 to 6
- noise_churn: float32 [4, 384, 2560], P(None, 'lat', 'lon'), may hold values from -6 to 6
- w_state: bfloat16 [128, 36], replicated, may hold values from -1 to 1
- w_cond: bfloat16 [128, 40], replicated, may hold values from -1 to 1
- w_expand: bfloat16 [128, 128], replicated, may hold values from -0.5 to 0.5
- w_project: bfloat16 [128, 128], replicated, may hold values from -0.5 to 0.5
- w_levels: bfloat16 [4, 9, 128, 128], replicated, may hold values from -0.1875 to 0.1875
- w_final: bfloat16 [9, 4, 128], replicated, may hold values from -0.1875 to 0.1875
Outputs:
- final_state: float32 [4, 384, 2560], P(None, 'lat', 'lon')
Inputs may be any that keep to these rules, and one draw needn't show every extreme that they name: |row_map[y] - y // 8| <= 2 for every fine row y, and both +2 and -2 occur. col_map[x] - x // 8, taken modulo 320 into -2 to 2, lies within that range for every fine column x, and both ends occur.
All inputs are finite; a program needn't handle non-finite values.
Results may differ from a plain program's by a relative error of at most 0.014.
Values may be sent and summed in bfloat16 or wider, within the bound.
No kernel may reach another device: no remote copies, remote signals or barrier semaphores. Data moves between devices by JAX's collectives and lax.ppermute only.
A program may use at most 128 MiB of HBM per device.

v0:
```python
import math

import jax
import jax.numpy as jnp
import numpy as np
from jax import lax
from jax.experimental import pallas as pl
from jax.experimental.pallas import tpu as pltpu
from jax.sharding import PartitionSpec as P

MARGIN = 24
TILE_ROWS, TILE_COLS = 48, 80
PATCH_ROWS, PATCH_COLS = 96, 128
CH = 128
ROWS = 4 * PATCH_ROWS
PAIRS = PATCH_ROWS // 2
SIDE = 16
COARSE_SLOTS = 48

sigma_data = 0.5
level_first = 4.0
level_second = 1.0
level_raised = 1.5
level_final = 0.25
epsilon = 1e-06

F32 = jnp.float32
BF16 = jnp.bfloat16


def _constants():
    place = np.arange(128)
    column = 8 * (place % 16) + place // 16
    perm = (column[:, None] == np.arange(128)[None, :]).astype(np.float32)
    back = []
    for shift in range(3):
        one = (column[:, None] == (np.arange(128) + shift - 1)[None, :]).astype(np.float32)
        back += [one, one]
    back = np.concatenate(back, 0)
    pick_in = np.zeros((2, 48, 36), np.float32)
    pick_out = np.zeros((2, 48, 36), np.float32)
    for pi in range(2):
        for dc in range(3):
            for pp in range(4):
                for e in range(4):
                    dr = pp - pi
                    if 0 <= dr <= 2:
                        pick_in[pi, dc * 16 + pp * 4 + e, (3 * dr + dc) * 4 + e] = 1.0
                    dr = pi + 2 - pp
                    if 0 <= dr <= 2:
                        pick_out[pi, dc * 16 + pp * 4 + e, (3 * dr + dc) * 4 + e] = 1.0
    pool = np.zeros((9, 6, 8, 12, 16), np.float32)
    for dr in range(3):
        for dc in range(3):
            for r in range(6):
                for c in range(8):
                    rr, cc = r + dr - 1, c + dc - 1
                    if 0 <= rr < 6 and 0 <= cc < 8:
                        pool[3 * dr + dc, r, c, 2 * rr : 2 * rr + 2, 2 * cc : 2 * cc + 2] = 0.25
    pool = pool.reshape(432, 192)
    grow = np.zeros((12, 16, 6, 8), np.float32)
    for r in range(12):
        for c in range(16):
            grow[r, c, r // 2, c // 2] = 1.0
    grow = grow.reshape(192, 48)
    return perm, back, pick_in, pick_out, pool, grow


PERM, BACK, PICK_IN, PICK_OUT, POOL, GROW = _constants()


def dot_nt(a, b):
    return lax.dot_general(a, b, (((1,), (1,)), ((), ())), preferred_element_type=F32)


def dot_nn(a, b):
    return jnp.dot(a, b, preferred_element_type=F32)


def lanes(shape):
    return lax.broadcasted_iota(jnp.int32, shape, 1)


def roll_lanes(value, amount):
    amount = amount % 128
    return value if amount == 0 else pltpu.roll(value, amount, 1)


def prepare_kernel(
    w_state, w_expand, w_project, w_levels, w_final, eye, pick_in, pick_out,
    first_w, expand_w, project_w, level_w, final_w, flat_final,
):
    unit = eye[...]
    for k in range(9):
        flat_final[4 * k : 4 * k + 4, :] = w_final[k].astype(F32)
    final_rows = flat_final[...].astype(BF16)
    state_rows = w_state[...]
    for pi in range(2):
        part = slice(pi * 128, pi * 128 + 128)
        first_w[:, part] = dot_nn(pick_in[pi], state_rows).astype(BF16)
        final_w[:, part] = dot_nn(pick_out[pi], final_rows).astype(BF16)
    zero = jnp.zeros((128, 128), BF16)
    for source, target, factor in ((w_expand, expand_w, 0.5), (w_project, project_w, 1.0)):
        block = (dot_nt(unit, source[...]) * factor).astype(BF16)
        target[0:128, 0:128] = block
        target[128:256, 128:256] = block
        target[0:128, 128:256] = zero
        target[128:256, 0:128] = zero
    for level in range(4):
        for k in range(9):
            level_w[level, k * 128 : k * 128 + 128, :] = dot_nt(unit, w_levels[level, k]).astype(BF16)


def pack_rows_kernel(noise_init, noise_churn, coarse, to_upper, to_lower, own, own_coarse, padded):
    for which, noise in enumerate((noise_init, noise_churn)):
        for e in range(4):
            padded[which, pl.ds(e, TILE_ROWS, stride=4), 0:TILE_COLS] = noise[e]
    own_coarse[...] = jnp.zeros((96, 128), F32)
    for k in range(10):
        own_coarse[pl.ds(k, 6, stride=16), 0:40] = coarse[k].astype(F32)
    lane = lanes((96, 128))
    placed = roll_lanes(own_coarse[...], 80)
    for which in range(2):
        own[which] = padded[which]
        for target, start in ((to_upper, 0), (to_lower, 96)):
            part = padded[which, start : start + 96, :]
            if which == 0:
                part = jnp.where(lane < 80, part, placed)
            target[which * 96 : which * 96 + 96, :] = part.astype(BF16)


def pack_cols_kernel(from_upper, from_lower, own, own_coarse, to_left, to_right, strip, coarse_strip):
    lane = lanes((192, 128))
    for which in range(2):
        rows = slice(which * 96, which * 96 + 96)
        strip[which, 0:96, :] = roll_lanes(from_upper[rows, :].astype(F32), MARGIN)
        strip[which, 96:288, :] = roll_lanes(own[which], MARGIN)
        strip[which, 288:384, :] = roll_lanes(from_lower[rows, :].astype(F32), MARGIN)
    left = right = None
    for group in range(4):
        part = strip[group // 2, (group % 2) * 192 : (group % 2) * 192 + 192, :]
        for_left = roll_lanes(part, 32 * group - 24)
        for_right = roll_lanes(part, 32 * group - 80)
        inside = (lane >= 32 * group) & (lane < 32 * group + 32)
        left = for_left if group == 0 else jnp.where(inside, for_left, left)
        right = for_right if group == 0 else jnp.where(inside, for_right, right)
    to_left[0:192, :] = left.astype(BF16)
    to_right[0:192, :] = right.astype(BF16)
    narrow = lanes((96, 128))
    above = roll_lanes(from_upper[0:96, :].astype(F32), -80)
    middle = own_coarse[...]
    below = roll_lanes(from_lower[0:96, :].astype(F32), -80)
    for index, part in enumerate((above, middle, below)):
        coarse_strip[index * 96 : index * 96 + 96, :] = jnp.where(narrow < 40, part, 0.0)
    packed = jnp.where(narrow < 40, above, jnp.where(narrow < 80, roll_lanes(middle, 40), roll_lanes(below, 80)))
    to_left[192:288, :] = packed.astype(BF16)
    to_right[192:288, :] = packed.astype(BF16)


def pad_store(target, row, pooled, groups):
    rows = pooled.shape[0]
    place = lax.broadcasted_iota(jnp.int32, (SIDE, 128), 0)
    target[pl.ds(row + 1, rows), SIDE : SIDE + groups * SIDE, :] = pooled.reshape(
        rows, groups * SIDE, 128
    ).astype(BF16)
    for r in range(rows):
        before = pltpu.roll(pooled[r, groups - 1], 1, 0)
        after = pltpu.roll(pooled[r, 0], SIDE - 1, 0)
        target[row + 1 + r, 0:SIDE, :] = jnp.where(place == 0, 0.0, before).astype(BF16)
        target[row + 1 + r, SIDE + groups * SIDE : 2 * SIDE + groups * SIDE, :] = jnp.where(
            place == SIDE - 1, 0.0, after
        ).astype(BF16)


def halve(values, rows, groups):
    grouped = values.reshape(rows // 2, 2, groups // 2, 2, SIDE, 128)
    return 0.25 * (
        (grouped[:, 0, :, 0] + grouped[:, 0, :, 1]) + (grouped[:, 1, :, 0] + grouped[:, 1, :, 1])
    )


def norm_silu(values, mean_w):
    squares = dot_nn((values * values).astype(BF16), mean_w)
    half = values * lax.rsqrt(squares + 4.0 * epsilon)
    return half + half * jnp.tanh(half)


def conv_rows(source, weight, row, rows, groups):
    taps = [
        source[pl.ds(row + dr, rows), dc * SIDE : dc * SIDE + groups * SIDE, :].reshape(
            rows * groups * SIDE, 128
        )
        for dr in range(3)
        for dc in range(3)
    ]
    return dot_nn(jnp.concatenate(taps, axis=1), weight)


CORE_SCRATCH = [
    pltpu.VMEM((3, 400, 128), F32),
    pltpu.VMEM((PAIRS, 128, 256), BF16),
    pltpu.VMEM((50, 96, 128), BF16),
    pltpu.VMEM((26, 64, 128), BF16),
    pltpu.VMEM((14, 48, 128), BF16),
    pltpu.VMEM((48, 64, 128), F32),
    pltpu.VMEM((24, 32, 128), F32),
    pltpu.VMEM((3, 392, 128), F32),
    pltpu.VMEM((3, 400, 128), F32),
]


def denoise(
    state, colmix, coarse_fields, lat, row_map, row_frac, weights, constants, scratch, noise_level, out
):
    first_w, expand_w, project_w, level_w, final_w = weights
    perm, back, mean_w, pool, grow = constants
    scaled, hidden, pooled1, pooled2, pooled3, level1, level2, taps_a, taps_b = scratch
    total_sq = noise_level * noise_level + sigma_data * sigma_data

    for shift in range(3):
        scaled[shift, 0:8, :] = jnp.zeros((8, 128), F32)
        scaled[shift, 384:400, :] = jnp.zeros((16, 128), F32)
        taps_a[shift, 384:392, :] = jnp.zeros((8, 128), F32)
        taps_b[shift, 0:8, :] = jnp.zeros((8, 128), F32)
    base = state[...] * (1.0 / math.sqrt(total_sq))
    lane = lanes((ROWS, 128))
    scaled[0, 4 : 4 + ROWS, :] = jnp.where(lane == 0, 0.0, pltpu.roll(base, 1, 1))
    scaled[1, 4 : 4 + ROWS, :] = base
    scaled[2, 4 : 4 + ROWS, :] = jnp.where(lane == 127, 0.0, pltpu.roll(base, 127, 1))
    for buffer, rows in ((pooled1, 50), (pooled2, 26), (pooled3, 14)):
        blank = jnp.zeros(buffer.shape[1:], BF16)
        buffer[0] = blank
        buffer[rows - 1] = blank

    def coarse_row(p):
        y = lat * TILE_ROWS - MARGIN + p
        inside = (y >= 0) & (y < 8 * TILE_ROWS)
        y = jnp.clip(y, 0, 8 * TILE_ROWS - 1)
        at = jnp.clip(row_map[y] - (lat * 6 - 6), 0, 16)
        fraction = row_frac[y]
        near = jnp.where(inside, 1.0 - fraction, 0.0)
        far = jnp.where(inside, fraction, 0.0)
        return near * coarse_fields[at] + far * coarse_fields[at + 1]

    def first(i, carry):
        row = pl.multiple_of(8 * i, 8)
        columns = [scaled[shift, pl.ds(row, 16), :].astype(BF16) for shift in range(3)]
        turned = dot_nt(perm[...], jnp.concatenate(columns + [colmix[...]], axis=0)).astype(BF16)
        fields = jnp.concatenate([coarse_row(2 * i), coarse_row(2 * i + 1)], axis=1).astype(BF16)
        pre = dot_nn(turned, jnp.concatenate([first_w[...], fields], axis=0))
        act = norm_silu(pre, mean_w[...])
        hidden[i] = act.astype(BF16)
        summed = (act[:, 0:128] + act[:, 128:256]).reshape(4, 2, SIDE, 128)
        pad_store(pooled1, i, (0.25 * (summed[:, 0] + summed[:, 1]))[None], 4)
        return carry

    lax.fori_loop(0, PAIRS, first, 0, unroll=2)

    mean_one = mean_w[0:128, 0:128]

    def one(c, carry):
        act = norm_silu(conv_rows(pooled1, level_w[0], 4 * c, 4, 4), mean_one)
        level1[pl.ds(4 * c, 4)] = act.reshape(4, 64, 128)
        pad_store(pooled2, 2 * c, halve(act, 4, 4), 2)
        return carry

    lax.fori_loop(0, 12, one, 0, unroll=2)

    def two(c, carry):
        act = norm_silu(conv_rows(pooled2, level_w[1], 8 * c, 8, 2), mean_one)
        level2[pl.ds(8 * c, 8)] = act.reshape(8, 32, 128)
        pad_store(pooled3, 4 * c, halve(act, 8, 2), 1)
        return carry

    lax.fori_loop(0, 3, two, 0, unroll=True)

    act3 = norm_silu(conv_rows(pooled3, level_w[2], 0, 12, 1), mean_one)
    shifted = dot_nn(pool[...], act3.astype(BF16)).astype(BF16)
    act4 = norm_silu(
        dot_nn(jnp.concatenate([shifted[48 * k : 48 * k + 48] for k in range(9)], axis=1), level_w[3]),
        mean_one,
    )
    merged3 = act3 + dot_nn(grow[...], act4.astype(BF16))
    merged2 = level2[...].reshape(12, 2, 2, SIDE, 128) + merged3.reshape(12, 1, 1, SIDE, 128)
    level2[...] = merged2.reshape(24, 32, 128)

    def last(i, carry):
        coarse2 = level2[i // 2].reshape(2, 1, SIDE, 128)
        merged1 = level1[i].reshape(2, 2, SIDE, 128) + coarse2
        merged1 = merged1.reshape(4, 1, SIDE, 128)
        merged1 = jnp.concatenate([merged1, merged1], axis=1).reshape(128, 128)
        joined = (hidden[i].astype(F32) + jnp.concatenate([merged1, merged1], axis=1)).astype(BF16)
        half = dot_nn(joined, expand_w[...])
        inner = (half + half * jnp.tanh(half)).astype(BF16)
        mixed = (joined.astype(F32) + dot_nn(inner, project_w[...])).astype(BF16)
        taps = dot_nt(final_w[...], mixed)
        row = pl.multiple_of(8 * i, 8)
        for shift in range(3):
            taps_a[shift, pl.ds(row, 8), :] = taps[16 * shift : 16 * shift + 8]
            taps_b[shift, pl.ds(row + 8, 8), :] = taps[16 * shift + 8 : 16 * shift + 16]
        return carry

    lax.fori_loop(0, PAIRS, last, 0, unroll=2)

    parts = []
    for shift in range(3):
        total = taps_a[shift, 4 : 4 + ROWS, :] + taps_b[shift, 4 : 4 + ROWS, :]
        upper = total.astype(BF16)
        parts += [upper, (total - upper.astype(F32)).astype(BF16)]
    refined = dot_nn(jnp.concatenate(parts, axis=1), back[...])
    skip_scale = sigma_data * sigma_data / total_sq
    out_scale = noise_level * sigma_data / math.sqrt(total_sq)
    out[...] = skip_scale * state[...] + out_scale * refined


def inside_rows(lat):
    row = lax.broadcasted_iota(jnp.int32, (ROWS, 128), 0)
    first = jnp.where(lat == 0, 4 * MARGIN, 0)
    last = jnp.where(lat == 7, ROWS - 4 * MARGIN, ROWS)
    return (row >= first) & (row < last)


def first_kernel(
    place, row_map, row_frac, col_map, col_frac, strip, coarse_strip, from_left, from_right, w_cond,
    first_w, expand_w, project_w, level_w, final_w, perm, back, mean_w, pool, grow,
    den, to_upper, to_lower, state, churn, fields, colmix,
    window, *scratch,
):
    lat, lon = place[0], place[1]
    lane = lanes((192, 128))
    inside = inside_rows(lat)
    for which, target in enumerate((state, churn)):
        for part in range(2):
            group = 2 * which + part
            rows = slice(part * 192, part * 192 + 192)
            left = roll_lanes(from_left[0:192, :].astype(F32), -32 * group)
            right = roll_lanes(from_right[0:192, :].astype(F32), 104 - 32 * group)
            target[rows, :] = jnp.where(lane < 24, left, jnp.where(lane < 104, strip[which, rows, :], right))
    state[...] = jnp.where(inside, level_first * state[...], 0.0)

    narrow = lanes((96, 128))
    for t, source in enumerate((from_left, None, from_right)):
        for part in range(3):
            if source is None:
                rows = coarse_strip[part * 96 : part * 96 + 96, :]
            else:
                rows = roll_lanes(source[192:288, :].astype(F32), -40 * part)
            for j in range(6):
                window[part * 6 + j, t * 16 : t * 16 + 16, :] = rows[j * 16 : j * 16 + 16]
    stacked = window[...].reshape(18 * COARSE_SLOTS, 128)[:, 0:40].astype(BF16)
    fields[...] = dot_nn(stacked, w_cond[...]).reshape(18, COARSE_SLOTS, 128)

    offset = col_map[...] - (10 * lon - 10)
    offset = jnp.where(offset < 0, offset + 320, offset)
    offset = jnp.where(offset >= 320, offset - 320, offset)
    slot = lax.broadcasted_iota(jnp.int32, (COARSE_SLOTS, 128), 0)
    tile = jnp.where(slot >= 32, 2, jnp.where(slot >= 16, 1, 0))
    column = jnp.where(slot - 16 * tile < 10, slot - 6 * tile, -1)
    fraction = col_frac[...]
    mix = jnp.where(column == offset, 1.0 - fraction, 0.0) + jnp.where(column == offset + 1, fraction, 0.0)
    colmix[...] = mix.astype(BF16)

    denoise(
        state, colmix, fields, lat, row_map, row_frac,
        (first_w, expand_w, project_w, level_w, final_w), (perm, back, mean_w, pool, grow),
        scratch, level_first, den,
    )
    to_upper[...] = den[0:192, :].astype(BF16)
    to_lower[...] = den[192:384, :].astype(BF16)


def add_rows_kernel(place, den, from_upper, from_lower, total, to_left, to_right):
    lat = place[0]
    has_upper = jnp.where(lat > 0, 1.0, 0.0)
    has_lower = jnp.where(lat < 7, 1.0, 0.0)
    top = den[0:192, :] + has_upper * from_upper[...].astype(F32)
    bottom = den[192:384, :] + has_lower * from_lower[...].astype(F32)
    total[0:192, :] = top
    total[192:384, :] = bottom
    lane = lanes((192, 128))
    to_left[...] = jnp.where(lane < 64, top, roll_lanes(bottom, 64)).astype(BF16)
    to_right[...] = jnp.where(lane < 64, roll_lanes(top, -80), roll_lanes(bottom, 64 - 80)).astype(BF16)


def second_kernel(
    place, row_map, row_frac, total, from_left, from_right, state, churn, fields, colmix,
    first_w, expand_w, project_w, level_w, final_w, perm, back, mean_w, pool, grow,
    den, to_upper, to_lower, raised,
    *scratch,
):
    lat = place[0]
    lane = lanes((192, 128))
    edge = (lane < 48) | (lane >= 80)
    left = from_left[...].astype(F32)
    right = from_right[...].astype(F32)
    inside = inside_rows(lat)
    for part in range(2):
        rows = slice(part * 192, part * 192 + 192)
        from_l = roll_lanes(left, -64 * part)
        from_r = roll_lanes(right, 80 - 64 * part)
        summed = total[rows, :] + jnp.where(lane < 48, from_l, jnp.where(lane >= 80, from_r, 0.0))
        has = (lat > 0) if part == 0 else (lat < 7)
        blended = summed * (jnp.where(has, 0.5, 1.0) * jnp.where(edge, 0.5, 1.0))
        value = state[rows, :]
        value = value + (level_second - level_first) / level_first * (value - blended)
        value = value + math.sqrt(level_raised * level_raised - level_second * level_second) * churn[rows, :]
        raised[rows, :] = value
    raised[...] = jnp.where(inside, raised[...], 0.0)
    denoise(
        raised, colmix, fields, lat, row_map, row_frac,
        (first_w, expand_w, project_w, level_w, final_w), (perm, back, mean_w, pool, grow),
        scratch, level_raised, den,
    )
    to_upper[...] = den[0:96, :].astype(BF16)
    to_lower[...] = den[288:384, :].astype(BF16)


def add_tile_rows_kernel(place, den, from_upper, from_lower, total, to_left, to_right):
    lat = place[0]
    has_upper = jnp.where(lat > 0, 1.0, 0.0)
    has_lower = jnp.where(lat < 7, 1.0, 0.0)
    top = den[96:192, :] + has_upper * from_upper[...].astype(F32)
    bottom = den[192:288, :] + has_lower * from_lower[...].astype(F32)
    total[0:96, :] = top
    total[96:192, :] = bottom
    lane = lanes((96, 128))
    to_left[...] = jnp.where(lane < 64, top, roll_lanes(bottom, 64)).astype(BF16)
    to_right[...] = jnp.where(lane < 64, roll_lanes(top, -104), roll_lanes(bottom, 64 - 104)).astype(BF16)


def finish_kernel(place, total, from_left, from_right, raised, out, rows_ref):
    lat = place[0]
    lane = lanes((96, 128))
    edge = (lane < 48) | (lane >= 80)
    left = from_left[...].astype(F32)
    right = from_right[...].astype(F32)
    for part in range(2):
        rows = slice(part * 96, part * 96 + 96)
        from_l = roll_lanes(left, 24 - 64 * part)
        from_r = roll_lanes(right, 80 - 64 * part)
        use_l = (lane >= 24) & (lane < 48)
        use_r = (lane >= 80) & (lane < 104)
        summed = total[rows, :] + jnp.where(use_l, from_l, jnp.where(use_r, from_r, 0.0))
        has = (lat > 0) if part == 0 else (lat < 7)
        blended = summed * (jnp.where(has, 0.5, 1.0) * jnp.where(edge, 0.5, 1.0))
        value = raised[96 + part * 96 : 192 + part * 96, :]
        value = value + (level_final - level_raised) / level_raised * (value - blended)
        rows_ref[rows, :] = roll_lanes(value, -24)
    for e in range(4):
        out[e] = rows_ref[pl.ds(e, TILE_ROWS, stride=4), 0:TILE_COLS]


def shape(dims, dtype):
    return jax.ShapeDtypeStruct(dims, dtype)


def call(kernel, operands, outs, scratch=(), scalars=0, cost=(0, 0, 0)):
    smem = pl.BlockSpec(memory_space=pltpu.SMEM)
    vmem = pl.BlockSpec(memory_space=pltpu.VMEM)
    return pl.pallas_call(
        kernel,
        out_shape=outs,
        in_specs=[smem] * scalars + [vmem] * (len(operands) - scalars),
        out_specs=[vmem] * len(outs),
        scratch_shapes=list(scratch),
        compiler_params=pltpu.CompilerParams(vmem_limit_bytes=48 * 1024 * 1024),
        cost_estimate=pl.CostEstimate(flops=cost[0], bytes_accessed=cost[1], transcendentals=cost[2]),
    )(*operands)


def body(
    coarse, row_map, row_frac, col_map, col_frac, noise_init, noise_churn,
    w_state, w_cond, w_expand, w_project, w_levels, w_final,
):
    lat_index = lax.axis_index("lat")
    lon_index = lax.axis_index("lon")
    place = jnp.stack([lat_index, lon_index]).astype(jnp.int32)
    rings = {}
    for axis in ("lat", "lon"):
        size = lax.axis_size(axis)
        rings[axis] = (
            [((i + 1) % size, i) for i in range(size)],
            [(i, (i + 1) % size) for i in range(size)],
        )

    def swap(axis, to_before, to_after):
        down, up = rings[axis]
        from_before = lax.ppermute(to_after, axis, up)
        from_after = lax.ppermute(to_before, axis, down)
        return from_before, from_after

    def columns(values):
        wide = jnp.concatenate([values[-MARGIN:], values, values[:MARGIN]])
        return lax.dynamic_slice(wide, (lon_index * TILE_COLS,), (PATCH_COLS,)).reshape(1, PATCH_COLS)

    msg = shape((192, 128), BF16)
    to_upper, to_lower, own, own_coarse = call(
        pack_rows_kernel,
        (noise_init, noise_churn, coarse.transpose(2, 1, 0)),
        [msg, msg, shape((2, 192, 128), F32), shape((96, 128), F32)],
        [pltpu.VMEM((2, 192, 128), F32)],
    )
    from_upper, from_lower = swap("lat", to_upper, to_lower)
    wide_msg = shape((288, 128), BF16)
    to_left, to_right, strip, coarse_strip = call(
        pack_cols_kernel,
        (from_upper, from_lower, own, own_coarse),
        [wide_msg, wide_msg, shape((2, ROWS, 128), F32), shape((288, 128), F32)],
    )
    from_left, from_right = swap("lon", to_left, to_right)

    weights = call(
        prepare_kernel,
        (
            w_state.T, w_expand, w_project, w_levels, w_final, jnp.asarray(np.eye(128), BF16),
            jnp.asarray(PICK_IN, BF16), jnp.asarray(PICK_OUT, BF16),
        ),
        [
            shape((48, 256), BF16), shape((256, 256), BF16), shape((256, 256), BF16),
            shape((4, 1152, 128), BF16), shape((48, 256), BF16),
        ],
        [pltpu.VMEM((36, 128), F32)],
        cost=(2 * 36 * 128**3, 4 << 20, 0),
    )
    mean_w = np.zeros((256, 256), np.float32)
    mean_w[:128, :128] = mean_w[128:, 128:] = 4.0 / 128.0
    constants = [jnp.asarray(c, BF16) for c in (PERM, BACK, mean_w, POOL, GROW)]
    field = shape((ROWS, 128), F32)
    cost = (5 * 10**9, 8 << 20, 3 * 10**6)
    den, to_upper, to_lower, state, churn, fields, colmix = call(
        first_kernel,
        (
            place, row_map, row_frac, columns(col_map), columns(col_frac),
            strip, coarse_strip, from_left, from_right, w_cond.T, *weights, *constants,
        ),
        [
            field, msg, msg, field, field,
            shape((18, COARSE_SLOTS, 128), F32), shape((COARSE_SLOTS, 128), BF16),
        ],
        [pltpu.VMEM((18, COARSE_SLOTS, 128), F32)] + CORE_SCRATCH,
        scalars=3,
        cost=cost,
    )
    from_upper, from_lower = swap("lat", to_upper, to_lower)
    total, to_left, to_right = call(
        add_rows_kernel, (place, den, from_upper, from_lower), [field, msg, msg], scalars=1
    )
    from_left, from_right = swap("lon", to_left, to_right)
    short_msg = shape((96, 128), BF16)
    den, to_upper, to_lower, raised = call(
        second_kernel,
        (
            place, row_map, row_frac, total, from_left, from_right, state, churn, fields, colmix,
            *weights, *constants,
        ),
        [field, short_msg, short_msg, field],
        CORE_SCRATCH,
        scalars=3,
        cost=cost,
    )
    from_upper, from_lower = swap("lat", to_upper, to_lower)
    total, to_left, to_right = call(
        add_tile_rows_kernel,
        (place, den, from_upper, from_lower),
        [shape((192, 128), F32), short_msg, short_msg],
        scalars=1,
    )
    from_left, from_right = swap("lon", to_left, to_right)
    (final,) = call(
        finish_kernel,
        (place, total, from_left, from_right, raised),
        [shape((4, TILE_ROWS, TILE_COLS), F32)],
        [pltpu.VMEM((192, 128), F32)],
        scalars=1,
    )
    return final


def solution(mesh):
    sharded = P(None, "lat", "lon")
    return jax.shard_map(
        body,
        mesh=mesh,
        in_specs=(sharded, P(), P(), P(), P(), sharded, sharded) + (P(),) * 6,
        out_specs=sharded,
        check_vma=False,
    )
```

profile of v0, /device:TPU:6, one launch (start us, length us, event | category | flops | bytes accessed | tf_op | source)
XLA Modules:
  0.0 126.0 jit_solution(1532412999782360951)
XLA Ops:
  0.0 0.9 copy-done.1
  0.9 0.9 copy-done.2
  1.8 0.7 copy-done.8
  2.5 0.0 copy-start.17
  2.5 0.1 shard_map.199
  2.6 3.3 %collective-permute-start = (bf16[192,128]{1,0:T(8,128)(2,1)S(1)}, bf16[192,128]{1,0:T(8,128)(2,1)S(1)}, u32[]{:S(2)}, u32[]{:S(2)}) collective-permute-start(bf16[192,128]{1,0:T(8,128)(2,1)S(1)} %get-tuple-element.35), channel_id=1, source_target_pairs={{0,32},{32,64},{64,96},{96,128},{128,160},{160,192},{192,224},{224... | collective-permute-start | bytes 147464 | tf_op jit(solution)/shard_map/ppermute | solution.py:488
  5.9 1.2 collective-permute-start.1
  7.1 0.8 fusion.1
  7.9 0.8 fusion
  8.7 0.8 concatenate.7
  9.5 0.1 dynamic-slice_bitcast_fusion.col_frac
  9.5 0.8 concatenate.6
  10.3 0.1 dynamic-slice_bitcast_fusion.1.col_map
  10.4 1.3 %copy-done = bf16[4,9,128,128]{3,2,1,0:T(8,128)(2,1)S(1)} copy-done((bf16[4,9,128,128]{3,2,1,0:T(8,128)(2,1)S(1)}, bf16[4,9,128,128]{3,2,1,0:T(8,128)(2,1)}, u32[]{:S(2)}) %copy-start) | copy-done | bytes 1179672
  11.7 0.8 copy-done.3
  12.4 0.8 copy-done.4
  13.2 0.8 copy-done.5
  14.0 0.7 copy-done.6
  14.7 0.7 copy-done.7
  15.4 0.7 copy-done.9
  16.1 0.7 copy-done.10
  16.8 1.0 shard_map.201
  17.8 0.0 collective-permute-done.from_upper
  17.9 0.3 shard_map.200
  18.2 0.1 collective-permute-start.2
  18.3 5.8 %collective-permute-start.3 = (bf16[288,128]{1,0:T(8,128)(2,1)S(1)}, bf16[288,128]{1,0:T(8,128)(2,1)S(1)}, u32[]{:S(2)}, u32[]{:S(2)}) collective-permute-start(bf16[288,128]{1,0:T(8,128)(2,1)S(1)} %get-tuple-element.42), channel_id=1, source_target_pairs={{1,0},{2,1},{3,2},{4,3},{5,4},{6,5},{7,6},{8,7},{9,8},{10,9},{11,1... | collective-permute-start | bytes 221192 | tf_op jit(solution)/shard_map/ppermute | solution.py:489
  24.1 0.1 pad_add_fusion.place
  24.2 1.9 %collective-permute-done.2.from_left = bf16[288,128]{1,0:T(8,128)(2,1)S(1)} collective-permute-done((bf16[288,128]{1,0:T(8,128)(2,1)S(1)}, bf16[288,128]{1,0:T(8,128)(2,1)S(1)}, u32[]{:S(2)}, u32[]{:S(2)}) %collective-permute-start.2) | collective-permute-done | bytes 73760 | tf_op jit(solution)/shard_map/ppermute | solution.py:488
  26.1 0.0 collective-permute-done.3.from_right
  26.1 34.1 %shard_map.202 = (f32[384,128]{1,0:T(8,128)S(1)}, bf16[192,128]{1,0:T(8,128)(2,1)S(1)}, bf16[192,128]{1,0:T(8,128)(2,1)S(1)}, f32[384,128]{1,0:T(8,128)S(1)}, f3...) custom-call(s32[2]{0:T(128)S(1)} %pad_add_fusion.place, s32[384]{0:T(512)S(1)} %copy-done.12, ...), custom_call_target="tpu_custom_call" | custom-call | flops 5000000000 | bytes 8388608 | tf_op jit(solution)/shard_map/pallas_call | solution.py:460
  60.2 2.1 %collective-permute-start.4 = (bf16[192,128]{1,0:T(8,128)(2,1)S(1)}, bf16[192,128]{1,0:T(8,128)(2,1)S(1)}, u32[]{:S(2)}, u32[]{:S(2)}) collective-permute-start(bf16[192,128]{1,0:T(8,128)(2,1)S(1)} %get-tuple-element.49), channel_id=1, source_target_pairs={{0,32},{32,64},{64,96},{96,128},{128,160},{160,192},{192,224},{224... | collective-permute-start | bytes 147464 | tf_op jit(solution)/shard_map/ppermute | solution.py:488
  62.3 2.4 %collective-permute-start.5 = (bf16[192,128]{1,0:T(8,128)(2,1)S(1)}, bf16[192,128]{1,0:T(8,128)(2,1)S(1)}, u32[]{:S(2)}, u32[]{:S(2)}) collective-permute-start(bf16[192,128]{1,0:T(8,128)(2,1)S(1)} %get-tuple-element.50), channel_id=1, source_target_pairs={{32,0},{64,32},{96,64},{128,96},{160,128},{192,160},{224,192},{0,2... | collective-permute-start | bytes 147464 | tf_op jit(solution)/shard_map/ppermute | solution.py:489
  64.7 2.1 %collective-permute-done.4.from_upper = bf16[192,128]{1,0:T(8,128)(2,1)S(1)} collective-permute-done((bf16[192,128]{1,0:T(8,128)(2,1)S(1)}, bf16[192,128]{1,0:T(8,128)(2,1)S(1)}, u32[]{:S(2)}, u32[]{:S(2)}) %collective-permute-start.4) | collective-permute-done | bytes 49184 | tf_op jit(solution)/shard_map/ppermute | solution.py:488
  66.8 1.1 collective-permute-done.5.from_lower
  67.9 0.7 shard_map.203
  68.6 0.1 collective-permute-start.6
  68.7 3.8 %collective-permute-start.7 = (bf16[192,128]{1,0:T(8,128)(2,1)S(1)}, bf16[192,128]{1,0:T(8,128)(2,1)S(1)}, u32[]{:S(2)}, u32[]{:S(2)}) collective-permute-start(bf16[192,128]{1,0:T(8,128)(2,1)S(1)} %get-tuple-element.53), channel_id=1, source_target_pairs={{1,0},{2,1},{3,2},{4,3},{5,4},{6,5},{7,6},{8,7},{9,8},{10,9},{11,1... | collective-permute-start | bytes 147464 | tf_op jit(solution)/shard_map/ppermute | solution.py:489
  72.5 1.8 %collective-permute-done.6.from_left = bf16[192,128]{1,0:T(8,128)(2,1)S(1)} collective-permute-done((bf16[192,128]{1,0:T(8,128)(2,1)S(1)}, bf16[192,128]{1,0:T(8,128)(2,1)S(1)}, u32[]{:S(2)}, u32[]{:S(2)}) %collective-permute-start.6) | collective-permute-done | bytes 49184 | tf_op jit(solution)/shard_map/ppermute | solution.py:488
  74.3 34.0 %shard_map.204 = (f32[384,128]{1,0:T(8,128)S(1)}, bf16[96,128]{1,0:T(8,128)(2,1)S(1)}, bf16[96,128]{1,0:T(8,128)(2,1)S(1)}, f32[384,128]{1,0:T(8,128)S(1)}) custom-call(s32[2]{0:T(128)S(1)} %pad_add_fusion.place, s32[384]{0:T(512)S(1)} %copy-done.12, f32[384]{0:T(512)S(1)} %copy-done.13, f32[384,128]{1,0:T(8,128)S(1)} %get-tuple-element.51.total, ...), custom_call_target="tpu_custom_call" | custom-call | flops 5000000000 | bytes 8388608 | tf_op jit(solution)/shard_map/pallas_call | solution.py:460
  108.3 4.8 %collective-permute-start.8 = (bf16[96,128]{1,0:T(8,128)(2,1)S(1)}, bf16[96,128]{1,0:T(8,128)(2,1)S(1)}, u32[]{:S(2)}, u32[]{:S(2)}) collective-permute-start(bf16[96,128]{1,0:T(8,128)(2,1)S(1)} %get-tuple-element.59), channel_id=1, source_target_pairs={{0,32},{32,64},{64,96},{96,128},{128,160},{160,192},{192,224},{224... | collective-permute-start | bytes 73736 | tf_op jit(solution)/shard_map/ppermute | solution.py:488
  113.2 1.5 %collective-permute-done.8.from_upper = bf16[96,128]{1,0:T(8,128)(2,1)S(1)} collective-permute-done((bf16[96,128]{1,0:T(8,128)(2,1)S(1)}, bf16[96,128]{1,0:T(8,128)(2,1)S(1)}, u32[]{:S(2)}, u32[]{:S(2)}) %collective-permute-start.8) | collective-permute-done | bytes 24608 | tf_op jit(solution)/shard_map/ppermute | solution.py:488
  114.7 3.8 %collective-permute-done.9.from_lower = bf16[96,128]{1,0:T(8,128)(2,1)S(1)} collective-permute-done((bf16[96,128]{1,0:T(8,128)(2,1)S(1)}, bf16[96,128]{1,0:T(8,128)(2,1)S(1)}, u32[]{:S(2)}, u32[]{:S(2)}) %collective-permute-start.9) | collective-permute-done | bytes 24608 | tf_op jit(solution)/shard_map/ppermute | solution.py:489
  118.5 0.6 shard_map.205
  119.2 0.1 collective-permute-start.10
  119.2 3.8 %collective-permute-start.11 = (bf16[96,128]{1,0:T(8,128)(2,1)S(1)}, bf16[96,128]{1,0:T(8,128)(2,1)S(1)}, u32[]{:S(2)}, u32[]{:S(2)}) collective-permute-start(bf16[96,128]{1,0:T(8,128)(2,1)S(1)} %get-tuple-element.63), channel_id=1, source_target_pairs={{1,0},{2,1},{3,2},{4,3},{5,4},{6,5},{7,6},{8,7},{9,8},{10,9},{11,1... | collective-permute-start | bytes 73736 | tf_op jit(solution)/shard_map/ppermute | solution.py:489
  123.1 1.5 %collective-permute-done.10.from_left = bf16[96,128]{1,0:T(8,128)(2,1)S(1)} collective-permute-done((bf16[96,128]{1,0:T(8,128)(2,1)S(1)}, bf16[96,128]{1,0:T(8,128)(2,1)S(1)}, u32[]{:S(2)}, u32[]{:S(2)}) %collective-permute-start.10) | collective-permute-done | bytes 24608 | tf_op jit(solution)/shard_map/ppermute | solution.py:488
  124.6 0.0 collective-permute-done.11.from_right
  124.6 1.4 %shard_map.206 = f32[4,48,80]{2,1,0:T(8,128)} custom-call(s32[2]{0:T(128)S(1)} %pad_add_fusion.place, f32[192,128]{1,0:T(8,128)S(1)} %get-tuple-element.61.total, bf16[96,128]{1,0:T(8,128)(2,1)S(1)} %collective-permute-done.10.from_left, bf16[96,128]{1,0:T(8,128)(2,1)S(1)} %collective-permute-done.11.from_right, f32[384,128]{1,0:T(8,128)S(1)} %get-tuple-element.64.raised), custom_call_target="tpu_custom_call" | custom-call | tf_op jit(solution)/shard_map/pallas_call | solution.py:460
  (29 shorter events, 0.1 us)
Async XLA Ops:
  0.0 0.9 copy-start.1
  0.9 0.9 copy-start.2
  1.8 0.7 copy-start.8
  2.5 23.6 %copy-start.11 = (bf16[128,40]{0,1:T(8,128)(2,1)S(1)}, bf16[128,40]{0,1:T(8,128)(2,1)}, u32[]{:S(2)}) copy-start(bf16[128,40]{0,1:T(8,128)(2,1)} %param.29) | copy-start | bytes 30724
  2.5 23.6 %copy-start.12 = (s32[384]{0:T(512)S(1)}, s32[384]{0:T(512)}, u32[]{:S(2)}) copy-start(s32[384]{0:T(512)} %row_map.3) | copy-start | bytes 4612
  2.5 23.6 %copy-start.13 = (f32[384]{0:T(512)S(1)}, f32[384]{0:T(512)}, u32[]{:S(2)}) copy-start(f32[384]{0:T(512)} %row_frac.3) | copy-start | bytes 4612
  2.5 23.6 %copy-start.14 = (bf16[432,192]{1,0:T(8,128)(2,1)S(1)}, bf16[432,192]{1,0:T(8,128)(2,1)}, u32[]{:S(2)}) copy-start(bf16[432,192]{1,0:T(8,128)(2,1)} %constant.37.clone.pool) | copy-start | bytes 497668
  2.5 23.6 %copy-start.17 = (bf16[192,48]{1,0:T(8,128)(2,1)S(1)}, bf16[192,48]{1,0:T(8,128)(2,1)}, u32[]{:S(2)}) copy-start(bf16[192,48]{1,0:T(8,128)(2,1)} %constant.38.clone.grow) | copy-start | bytes 55300
  2.6 15.2 %collective-permute-start = (bf16[192,128]{1,0:T(8,128)(2,1)S(1)}, bf16[192,128]{1,0:T(8,128)(2,1)S(1)}, u32[]{:S(2)}, u32[]{:S(2)}) collective-permute-start(bf16[192,128]{1,0:T(8,128)(2,1)S(1)} %get-tuple-element.35), channel_id=1, source_target_pairs={{0,32},{32,64},{64,96},{96,128},{128,160},{160,192},{192,224},{224... | collective-permute-start | bytes 147464 | tf_op jit(solution)/shard_map/ppermute | solution.py:488
  5.9 12.0 %collective-permute-start.1 = (bf16[192,128]{1,0:T(8,128)(2,1)S(1)}, bf16[192,128]{1,0:T(8,128)(2,1)S(1)}, u32[]{:S(2)}, u32[]{:S(2)}) collective-permute-start(bf16[192,128]{1,0:T(8,128)(2,1)S(1)} %get-tuple-element.36), channel_id=1, source_target_pairs={{32,0},{64,32},{96,64},{128,96},{160,128},{192,160},{224,192},{0,2... | collective-permute-start | bytes 147464 | tf_op jit(solution)/shard_map/ppermute | solution.py:489
  10.4 1.3 %copy-start = (bf16[4,9,128,128]{3,2,1,0:T(8,128)(2,1)S(1)}, bf16[4,9,128,128]{3,2,1,0:T(8,128)(2,1)}, u32[]{:S(2)}) copy-start(bf16[4,9,128,128]{3,2,1,0:T(8,128)(2,1)} %w_levels.1) | copy-start | bytes 3538948
  11.7 0.8 copy-start.3
  12.4 0.8 copy-start.4
  13.2 0.8 copy-start.5
  14.0 0.7 copy-start.6
  14.7 0.7 copy-start.7
  15.4 0.7 copy-start.9
  16.1 0.7 copy-start.10
  16.8 9.3 %copy-start.15 = (bf16[768,128]{1,0:T(8,128)(2,1)S(1)}, bf16[768,128]{1,0:T(8,128)(2,1)}, u32[]{:S(2)}) copy-start(bf16[768,128]{1,0:T(8,128)(2,1)} %constant.35.clone.back) | copy-start | bytes 589828
  16.8 9.3 %copy-start.16 = (bf16[256,256]{1,0:T(8,128)(2,1)S(1)}, bf16[256,256]{1,0:T(8,128)(2,1)}, u32[]{:S(2)}) copy-start(bf16[256,256]{1,0:T(8,128)(2,1)} %constant.36.clone.mean_w) | copy-start | bytes 393220
  16.8 9.3 %copy-start.18 = (bf16[128,128]{1,0:T(8,128)(2,1)S(1)}, bf16[128,128]{1,0:T(8,128)(2,1)}, u32[]{:S(2)}) copy-start(bf16[128,128]{1,0:T(8,128)(2,1)} %constant.34.clone.perm) | copy-start | bytes 98308
  18.2 7.9 %collective-permute-start.2 = (bf16[288,128]{1,0:T(8,128)(2,1)S(1)}, bf16[288,128]{1,0:T(8,128)(2,1)S(1)}, u32[]{:S(2)}, u32[]{:S(2)}) collective-permute-start(bf16[288,128]{1,0:T(8,128)(2,1)S(1)} %get-tuple-element.41), channel_id=1, source_target_pairs={{0,1},{1,2},{2,3},{3,4},{4,5},{5,6},{6,7},{7,8},{8,9},{9,10},{10,1... | collective-permute-start | bytes 221192 | tf_op jit(solution)/shard_map/ppermute | solution.py:488
  18.3 7.8 %collective-permute-start.3 = (bf16[288,128]{1,0:T(8,128)(2,1)S(1)}, bf16[288,128]{1,0:T(8,128)(2,1)S(1)}, u32[]{:S(2)}, u32[]{:S(2)}) collective-permute-start(bf16[288,128]{1,0:T(8,128)(2,1)S(1)} %get-tuple-element.42), channel_id=1, source_target_pairs={{1,0},{2,1},{3,2},{4,3},{5,4},{6,5},{7,6},{8,7},{9,8},{10,9},{11,1... | collective-permute-start | bytes 221192 | tf_op jit(solution)/shard_map/ppermute | solution.py:489
  60.2 6.6 %collective-permute-start.4 = (bf16[192,128]{1,0:T(8,128)(2,1)S(1)}, bf16[192,128]{1,0:T(8,128)(2,1)S(1)}, u32[]{:S(2)}, u32[]{:S(2)}) collective-permute-start(bf16[192,128]{1,0:T(8,128)(2,1)S(1)} %get-tuple-element.49), channel_id=1, source_target_pairs={{0,32},{32,64},{64,96},{96,128},{128,160},{160,192},{192,224},{224... | collective-permute-start | bytes 147464 | tf_op jit(solution)/shard_map/ppermute | solution.py:488
  62.3 5.6 %collective-permute-start.5 = (bf16[192,128]{1,0:T(8,128)(2,1)S(1)}, bf16[192,128]{1,0:T(8,128)(2,1)S(1)}, u32[]{:S(2)}, u32[]{:S(2)}) collective-permute-start(bf16[192,128]{1,0:T(8,128)(2,1)S(1)} %get-tuple-element.50), channel_id=1, source_target_pairs={{32,0},{64,32},{96,64},{128,96},{160,128},{192,160},{224,192},{0,2... | collective-permute-start | bytes 147464 | tf_op jit(solution)/shard_map/ppermute | solution.py:489
  68.6 5.7 %collective-permute-start.6 = (bf16[192,128]{1,0:T(8,128)(2,1)S(1)}, bf16[192,128]{1,0:T(8,128)(2,1)S(1)}, u32[]{:S(2)}, u32[]{:S(2)}) collective-permute-start(bf16[192,128]{1,0:T(8,128)(2,1)S(1)} %get-tuple-element.52), channel_id=1, source_target_pairs={{0,1},{1,2},{2,3},{3,4},{4,5},{5,6},{6,7},{7,8},{8,9},{9,10},{10,1... | collective-permute-start | bytes 147464 | tf_op jit(solution)/shard_map/ppermute | solution.py:488
  68.7 5.6 %collective-permute-start.7 = (bf16[192,128]{1,0:T(8,128)(2,1)S(1)}, bf16[192,128]{1,0:T(8,128)(2,1)S(1)}, u32[]{:S(2)}, u32[]{:S(2)}) collective-permute-start(bf16[192,128]{1,0:T(8,128)(2,1)S(1)} %get-tuple-element.53), channel_id=1, source_target_pairs={{1,0},{2,1},{3,2},{4,3},{5,4},{6,5},{7,6},{8,7},{9,8},{10,9},{11,1... | collective-permute-start | bytes 147464 | tf_op jit(solution)/shard_map/ppermute | solution.py:489
  108.3 6.4 %collective-permute-start.8 = (bf16[96,128]{1,0:T(8,128)(2,1)S(1)}, bf16[96,128]{1,0:T(8,128)(2,1)S(1)}, u32[]{:S(2)}, u32[]{:S(2)}) collective-permute-start(bf16[96,128]{1,0:T(8,128)(2,1)S(1)} %get-tuple-element.59), channel_id=1, source_target_pairs={{0,32},{32,64},{64,96},{96,128},{128,160},{160,192},{192,224},{224... | collective-permute-start | bytes 73736 | tf_op jit(solution)/shard_map/ppermute | solution.py:488
  113.2 5.3 %collective-permute-start.9 = (bf16[96,128]{1,0:T(8,128)(2,1)S(1)}, bf16[96,128]{1,0:T(8,128)(2,1)S(1)}, u32[]{:S(2)}, u32[]{:S(2)}) collective-permute-start(bf16[96,128]{1,0:T(8,128)(2,1)S(1)} %get-tuple-element.60), channel_id=1, source_target_pairs={{32,0},{64,32},{96,64},{128,96},{160,128},{192,160},{224,192},{0,2... | collective-permute-start | bytes 73736 | tf_op jit(solution)/shard_map/ppermute | solution.py:489
  119.2 5.4 %collective-permute-start.10 = (bf16[96,128]{1,0:T(8,128)(2,1)S(1)}, bf16[96,128]{1,0:T(8,128)(2,1)S(1)}, u32[]{:S(2)}, u32[]{:S(2)}) collective-permute-start(bf16[96,128]{1,0:T(8,128)(2,1)S(1)} %get-tuple-element.62), channel_id=1, source_target_pairs={{0,1},{1,2},{2,3},{3,4},{4,5},{5,6},{6,7},{7,8},{8,9},{9,10},{10,1... | collective-permute-start | bytes 73736 | tf_op jit(solution)/shard_map/ppermute | solution.py:488
  119.2 5.4 %collective-permute-start.11 = (bf16[96,128]{1,0:T(8,128)(2,1)S(1)}, bf16[96,128]{1,0:T(8,128)(2,1)S(1)}, u32[]{:S(2)}, u32[]{:S(2)}) collective-permute-start(bf16[96,128]{1,0:T(8,128)(2,1)S(1)} %get-tuple-element.63), channel_id=1, source_target_pairs={{1,0},{2,1},{3,2},{4,3},{5,4},{6,5},{7,6},{8,7},{9,8},{10,9},{11,1... | collective-permute-start | bytes 73736 | tf_op jit(solution)/shard_map/ppermute | solution.py:489
where the time goes:
time: 128 us; the launch traced here: 126 us
  Pallas kernels  72.2 us (56%)
  starting transfers between devices  27.6 us (22%)
  waiting for transfers between devices  13.7 us (11%)
  local copies, waits for them, and re-layouts  12.2 us (10%)
    pallas_call x8, Pallas kernels, call(): pl.pallas_call(kernel, out_shape=outs, in_specs=[smem] * scalars + [vmem]...  72.2 us
    ppermute x6, starting transfers between devices, swap(): from_after = lax.ppermute(to_before, axis, down)  17.2 us
    ppermute x6, starting transfers between devices, swap(): from_before = lax.ppermute(to_after, axis, up)  10.4 us
    unnamed x38, local copies, waits for them, and re-layouts  8.96 us
    ppermute x6, waiting for transfers between devices, swap(): from_before = lax.ppermute(to_after, axis, up)  8.73 us
    ppermute x6, waiting for transfers between devices, swap(): from_after = lax.ppermute(to_before, axis, down)  4.97 us
  transfers between devices with their start and end apart: 12, of which 7 were waited for; matrix products, arithmetic and copies ran while one was open for 3% of the time, Pallas kernels for 1%

commit v1 on v0

--- a/solution.py
+++ b/solution.py
@@ -14,6 +14,8 @@
 CH = 128
 ROWS = 4 * PATCH_ROWS
 PAIRS = PATCH_ROWS // 2
+FIRST_BATCH, LAST_BATCH = 16, 24
+LEVEL1_BATCH, LEVEL2_BATCH = 24, 24
 SIDE = 16
 COARSE_SLOTS = 48
 
@@ -242,37 +244,40 @@
         far = jnp.where(inside, fraction, 0.0)
         return near * coarse_fields[at] + far * coarse_fields[at + 1]
 
-    def first(i, carry):
-        row = pl.multiple_of(8 * i, 8)
-        columns = [scaled[shift, pl.ds(row, 16), :].astype(BF16) for shift in range(3)]
-        turned = dot_nt(perm[...], jnp.concatenate(columns + [colmix[...]], axis=0)).astype(BF16)
-        fields = jnp.concatenate([coarse_row(2 * i), coarse_row(2 * i + 1)], axis=1).astype(BF16)
-        pre = dot_nn(turned, jnp.concatenate([first_w[...], fields], axis=0))
-        act = norm_silu(pre, mean_w[...])
-        hidden[i] = act.astype(BF16)
-        summed = (act[:, 0:128] + act[:, 128:256]).reshape(4, 2, SIDE, 128)
-        pad_store(pooled1, i, (0.25 * (summed[:, 0] + summed[:, 1]))[None], 4)
+    def first(c, carry):
+        pre = []
+        for k in range(FIRST_BATCH):
+            i = FIRST_BATCH * c + k
+            row = pl.multiple_of(8 * FIRST_BATCH * c, 8) + 8 * k
+            columns = [scaled[shift, pl.ds(row, 16), :].astype(BF16) for shift in range(3)]
+            turned = dot_nt(perm[...], jnp.concatenate(columns + [colmix[...]], axis=0)).astype(BF16)
+            fields = jnp.concatenate([coarse_row(2 * i), coarse_row(2 * i + 1)], axis=1).astype(BF16)
+            pre.append(dot_nn(turned, jnp.concatenate([first_w[...], fields], axis=0)))
+        act = norm_silu(jnp.concatenate(pre, axis=0), mean_w[...])
+        hidden[pl.ds(FIRST_BATCH * c, FIRST_BATCH)] = act.astype(BF16).reshape(FIRST_BATCH, 128, 256)
+        summed = (act[:, 0:128] + act[:, 128:256]).reshape(FIRST_BATCH, 4, 2, SIDE, 128)
+        pad_store(pooled1, FIRST_BATCH * c, 0.25 * (summed[:, :, 0] + summed[:, :, 1]), 4)
         return carry
 
-    lax.fori_loop(0, PAIRS, first, 0, unroll=2)
+    lax.fori_loop(0, PAIRS // FIRST_BATCH, first, 0)
 
     mean_one = mean_w[0:128, 0:128]
 
     def one(c, carry):
-        act = norm_silu(conv_rows(pooled1, level_w[0], 4 * c, 4, 4), mean_one)
-        level1[pl.ds(4 * c, 4)] = act.reshape(4, 64, 128)
-        pad_store(pooled2, 2 * c, halve(act, 4, 4), 2)
+        act = norm_silu(conv_rows(pooled1, level_w[0], LEVEL1_BATCH * c, LEVEL1_BATCH, 4), mean_one)
+        level1[pl.ds(LEVEL1_BATCH * c, LEVEL1_BATCH)] = act.reshape(LEVEL1_BATCH, 64, 128)
+        pad_store(pooled2, LEVEL1_BATCH // 2 * c, halve(act, LEVEL1_BATCH, 4), 2)
         return carry
 
-    lax.fori_loop(0, 12, one, 0, unroll=2)
+    lax.fori_loop(0, 48 // LEVEL1_BATCH, one, 0)
 
     def two(c, carry):
-        act = norm_silu(conv_rows(pooled2, level_w[1], 8 * c, 8, 2), mean_one)
-        level2[pl.ds(8 * c, 8)] = act.reshape(8, 32, 128)
-        pad_store(pooled3, 4 * c, halve(act, 8, 2), 1)
+        act = norm_silu(conv_rows(pooled2, level_w[1], LEVEL2_BATCH * c, LEVEL2_BATCH, 2), mean_one)
+        level2[pl.ds(LEVEL2_BATCH * c, LEVEL2_BATCH)] = act.reshape(LEVEL2_BATCH, 32, 128)
+        pad_store(pooled3, LEVEL2_BATCH // 2 * c, halve(act, LEVEL2_BATCH, 2), 1)
         return carry
 
-    lax.fori_loop(0, 3, two, 0, unroll=True)
+    lax.fori_loop(0, 24 // LEVEL2_BATCH, two, 0)
 
     act3 = norm_silu(conv_rows(pooled3, level_w[2], 0, 12, 1), mean_one)
     shifted = dot_nn(pool[...], act3.astype(BF16)).astype(BF16)
@@ -284,23 +289,30 @@
     merged2 = level2[...].reshape(12, 2, 2, SIDE, 128) + merged3.reshape(12, 1, 1, SIDE, 128)
     level2[...] = merged2.reshape(24, 32, 128)
 
-    def last(i, carry):
-        coarse2 = level2[i // 2].reshape(2, 1, SIDE, 128)
-        merged1 = level1[i].reshape(2, 2, SIDE, 128) + coarse2
-        merged1 = merged1.reshape(4, 1, SIDE, 128)
-        merged1 = jnp.concatenate([merged1, merged1], axis=1).reshape(128, 128)
-        joined = (hidden[i].astype(F32) + jnp.concatenate([merged1, merged1], axis=1)).astype(BF16)
+    def last(c, carry):
+        merged = []
+        for k in range(LAST_BATCH):
+            i = LAST_BATCH * c + k
+            coarse2 = level2[i // 2].reshape(2, 1, SIDE, 128)
+            merged1 = level1[i].reshape(2, 2, SIDE, 128) + coarse2
+            merged1 = merged1.reshape(4, 1, SIDE, 128)
+            merged1 = jnp.concatenate([merged1, merged1], axis=1).reshape(128, 128)
+            merged.append(jnp.concatenate([merged1, merged1], axis=1))
+        merged = jnp.concatenate(merged, axis=0)
+        before = hidden[pl.ds(LAST_BATCH * c, LAST_BATCH)].reshape(LAST_BATCH * 128, 256)
+        joined = (before.astype(F32) + merged).astype(BF16)
         half = dot_nn(joined, expand_w[...])
         inner = (half + half * jnp.tanh(half)).astype(BF16)
         mixed = (joined.astype(F32) + dot_nn(inner, project_w[...])).astype(BF16)
-        taps = dot_nt(final_w[...], mixed)
-        row = pl.multiple_of(8 * i, 8)
-        for shift in range(3):
-            taps_a[shift, pl.ds(row, 8), :] = taps[16 * shift : 16 * shift + 8]
-            taps_b[shift, pl.ds(row + 8, 8), :] = taps[16 * shift + 8 : 16 * shift + 16]
+        for k in range(LAST_BATCH):
+            taps = dot_nt(final_w[...], mixed[128 * k : 128 * k + 128])
+            row = pl.multiple_of(8 * LAST_BATCH * c, 8) + 8 * k
+            for shift in range(3):
+                taps_a[shift, pl.ds(row, 8), :] = taps[16 * shift : 16 * shift + 8]
+                taps_b[shift, pl.ds(row + 8, 8), :] = taps[16 * shift + 8 : 16 * shift + 16]
         return carry
 
-    lax.fori_loop(0, PAIRS, last, 0, unroll=2)
+    lax.fori_loop(0, PAIRS // LAST_BATCH, last, 0)
 
     parts = []
     for shift in range(3):
@@ -318,6 +330,16 @@
     first = jnp.where(lat == 0, 4 * MARGIN, 0)
     last = jnp.where(lat == 7, ROWS - 4 * MARGIN, ROWS)
     return (row >= first) & (row < last)
+
+
+def send_rows(lat, den, to_upper, to_lower, count):
+    above = jnp.where(lat > 0, 0.5, 0.0)
+    below = jnp.where(lat < 7, 0.5, 0.0)
+    to_upper[...] = (above * den[0:count, :]).astype(BF16)
+    to_lower[...] = (below * den[ROWS - count : ROWS, :]).astype(BF16)
+    half = ROWS // 2
+    den[0:half, :] = (1.0 - above) * den[0:half, :]
+    den[half:ROWS, :] = (1.0 - below) * den[half:ROWS, :]
 
 
 def first_kernel(
@@ -350,13 +372,25 @@
     stacked = window[...].reshape(18 * COARSE_SLOTS, 128)[:, 0:40].astype(BF16)
     fields[...] = dot_nn(stacked, w_cond[...]).reshape(18, COARSE_SLOTS, 128)
 
-    offset = col_map[...] - (10 * lon - 10)
+    begin = lon * TILE_COLS - MARGIN
+    begin = jnp.where(begin < 0, begin + 32 * TILE_COLS, begin)
+    row, skip = begin // 128, begin % 128
+    after = jnp.where(row == 19, 0, row + 1)
+    turn = jnp.where(skip == 0, 0, 128 - skip)
+    front = lanes((1, 128)) < 128 - skip
+
+    def stretch(ref):
+        return jnp.where(
+            front, pltpu.roll(ref[pl.ds(row, 1), :], turn, 1), pltpu.roll(ref[pl.ds(after, 1), :], turn, 1)
+        )
+
+    offset = stretch(col_map) - (10 * lon - 10)
     offset = jnp.where(offset < 0, offset + 320, offset)
     offset = jnp.where(offset >= 320, offset - 320, offset)
     slot = lax.broadcasted_iota(jnp.int32, (COARSE_SLOTS, 128), 0)
     tile = jnp.where(slot >= 32, 2, jnp.where(slot >= 16, 1, 0))
     column = jnp.where(slot - 16 * tile < 10, slot - 6 * tile, -1)
-    fraction = col_frac[...]
+    fraction = stretch(col_frac)
     mix = jnp.where(column == offset, 1.0 - fraction, 0.0) + jnp.where(column == offset + 1, fraction, 0.0)
     colmix[...] = mix.astype(BF16)
 
@@ -365,16 +399,12 @@
         (first_w, expand_w, project_w, level_w, final_w), (perm, back, mean_w, pool, grow),
         scratch, level_first, den,
     )
-    to_upper[...] = den[0:192, :].astype(BF16)
-    to_lower[...] = den[192:384, :].astype(BF16)
-
-
-def add_rows_kernel(place, den, from_upper, from_lower, total, to_left, to_right):
-    lat = place[0]
-    has_upper = jnp.where(lat > 0, 1.0, 0.0)
-    has_lower = jnp.where(lat < 7, 1.0, 0.0)
-    top = den[0:192, :] + has_upper * from_upper[...].astype(F32)
-    bottom = den[192:384, :] + has_lower * from_lower[...].astype(F32)
+    send_rows(lat, den, to_upper, to_lower, 192)
+
+
+def add_rows_kernel(den, from_upper, from_lower, total, to_left, to_right):
+    top = den[0:192, :] + from_upper[...].astype(F32)
+    bottom = den[192:384, :] + from_lower[...].astype(F32)
     total[0:192, :] = top
     total[192:384, :] = bottom
     lane = lanes((192, 128))
@@ -399,8 +429,7 @@
         from_l = roll_lanes(left, -64 * part)
         from_r = roll_lanes(right, 80 - 64 * part)
         summed = total[rows, :] + jnp.where(lane < 48, from_l, jnp.where(lane >= 80, from_r, 0.0))
-        has = (lat > 0) if part == 0 else (lat < 7)
-        blended = summed * (jnp.where(has, 0.5, 1.0) * jnp.where(edge, 0.5, 1.0))
+        blended = summed * jnp.where(edge, 0.5, 1.0)
         value = state[rows, :]
         value = value + (level_second - level_first) / level_first * (value - blended)
         value = value + math.sqrt(level_raised * level_raised - level_second * level_second) * churn[rows, :]
@@ -411,16 +440,12 @@
         (first_w, expand_w, project_w, level_w, final_w), (perm, back, mean_w, pool, grow),
         scratch, level_raised, den,
     )
-    to_upper[...] = den[0:96, :].astype(BF16)
-    to_lower[...] = den[288:384, :].astype(BF16)
-
-
-def add_tile_rows_kernel(place, den, from_upper, from_lower, total, to_left, to_right):
-    lat = place[0]
-    has_upper = jnp.where(lat > 0, 1.0, 0.0)
-    has_lower = jnp.where(lat < 7, 1.0, 0.0)
-    top = den[96:192, :] + has_upper * from_upper[...].astype(F32)
-    bottom = den[192:288, :] + has_lower * from_lower[...].astype(F32)
+    send_rows(lat, den, to_upper, to_lower, 96)
+
+
+def add_tile_rows_kernel(den, from_upper, from_lower, total, to_left, to_right):
+    top = den[96:192, :] + from_upper[...].astype(F32)
+    bottom = den[192:288, :] + from_lower[...].astype(F32)
     total[0:96, :] = top
     total[96:192, :] = bottom
     lane = lanes((96, 128))
@@ -428,8 +453,7 @@
     to_right[...] = jnp.where(lane < 64, roll_lanes(top, -104), roll_lanes(bottom, 64 - 104)).astype(BF16)
 
 
-def finish_kernel(place, total, from_left, from_right, raised, out, rows_ref):
-    lat = place[0]
+def finish_kernel(total, from_left, from_right, raised, out, rows_ref):
     lane = lanes((96, 128))
     edge = (lane < 48) | (lane >= 80)
     left = from_left[...].astype(F32)
@@ -441,8 +465,7 @@
         use_l = (lane >= 24) & (lane < 48)
         use_r = (lane >= 80) & (lane < 104)
         summed = total[rows, :] + jnp.where(use_l, from_l, jnp.where(use_r, from_r, 0.0))
-        has = (lat > 0) if part == 0 else (lat < 7)
-        blended = summed * (jnp.where(has, 0.5, 1.0) * jnp.where(edge, 0.5, 1.0))
+        blended = summed * jnp.where(edge, 0.5, 1.0)
         value = raised[96 + part * 96 : 192 + part * 96, :]
         value = value + (level_final - level_raised) / level_raised * (value - blended)
         rows_ref[rows, :] = roll_lanes(value, -24)
@@ -454,7 +477,7 @@
     return jax.ShapeDtypeStruct(dims, dtype)
 
 
-def call(kernel, operands, outs, scratch=(), scalars=0, cost=(0, 0, 0)):
+def call(kernel, operands, outs, scratch=(), scalars=0, cost=(0, 0, 0), room=40):
     smem = pl.BlockSpec(memory_space=pltpu.SMEM)
     vmem = pl.BlockSpec(memory_space=pltpu.VMEM)
     return pl.pallas_call(
@@ -463,7 +486,7 @@
         in_specs=[smem] * scalars + [vmem] * (len(operands) - scalars),
         out_specs=[vmem] * len(outs),
         scratch_shapes=list(scratch),
-        compiler_params=pltpu.CompilerParams(vmem_limit_bytes=48 * 1024 * 1024),
+        compiler_params=pltpu.CompilerParams(vmem_limit_bytes=room << 20),
         cost_estimate=pl.CostEstimate(flops=cost[0], bytes_accessed=cost[1], transcendentals=cost[2]),
     )(*operands)
 
@@ -489,16 +512,13 @@
         from_after = lax.ppermute(to_before, axis, down)
         return from_before, from_after
 
-    def columns(values):
-        wide = jnp.concatenate([values[-MARGIN:], values, values[:MARGIN]])
-        return lax.dynamic_slice(wide, (lon_index * TILE_COLS,), (PATCH_COLS,)).reshape(1, PATCH_COLS)
-
     msg = shape((192, 128), BF16)
     to_upper, to_lower, own, own_coarse = call(
         pack_rows_kernel,
         (noise_init, noise_churn, coarse.transpose(2, 1, 0)),
         [msg, msg, shape((2, 192, 128), F32), shape((96, 128), F32)],
         [pltpu.VMEM((2, 192, 128), F32)],
+        room=60,
     )
     from_upper, from_lower = swap("lat", to_upper, to_lower)
     wide_msg = shape((288, 128), BF16)
@@ -521,6 +541,7 @@
         ],
         [pltpu.VMEM((36, 128), F32)],
         cost=(2 * 36 * 128**3, 4 << 20, 0),
+        room=60,
     )
     mean_w = np.zeros((256, 256), np.float32)
     mean_w[:128, :128] = mean_w[128:, 128:] = 4.0 / 128.0
@@ -530,7 +551,7 @@
     den, to_upper, to_lower, state, churn, fields, colmix = call(
         first_kernel,
         (
-            place, row_map, row_frac, columns(col_map), columns(col_frac),
+            place, row_map, row_frac, col_map.reshape(20, 128), col_frac.reshape(20, 128),
             strip, coarse_strip, from_left, from_right, w_cond.T, *weights, *constants,
         ),
         [
@@ -543,7 +564,7 @@
     )
     from_upper, from_lower = swap("lat", to_upper, to_lower)
     total, to_left, to_right = call(
-        add_rows_kernel, (place, den, from_upper, from_lower), [field, msg, msg], scalars=1
+        add_rows_kernel, (den, from_upper, from_lower), [field, msg, msg]
     )
     from_left, from_right = swap("lon", to_left, to_right)
     short_msg = shape((96, 128), BF16)
@@ -561,17 +582,15 @@
     from_upper, from_lower = swap("lat", to_upper, to_lower)
     total, to_left, to_right = call(
         add_tile_rows_kernel,
-        (place, den, from_upper, from_lower),
+        (den, from_upper, from_lower),
         [shape((192, 128), F32), short_msg, short_msg],
-        scalars=1,
     )
     from_left, from_right = swap("lon", to_left, to_right)
     (final,) = call(
         finish_kernel,
-        (place, total, from_left, from_right, raised),
+        (total, from_left, from_right, raised),
         [shape((4, TILE_ROWS, TILE_COLS), F32)],
         [pltpu.VMEM((192, 128), F32)],
-        scalars=1,
     )
     return final
 

time: 128 us -> 85.1 us (0.66)
  the two profiles are of different devices: /device:TPU:6 before, /device:TPU:127 now
where the time goes in v1:
time: 85.1 us; the launch traced here: 84.8 us
  Pallas kernels  36.9 us (43%)
  waiting for transfers between devices  27.6 us (32%)
  starting transfers between devices  15.4 us (18%)
  local copies, waits for them, and re-layouts  4.61 us (5%)
    pallas_call x8, Pallas kernels, call(): pl.pallas_call(kernel, out_shape=outs, in_specs=[smem] * scalars + [vmem]...  36.9 us
    ppermute x6, waiting for transfers between devices, swap(): from_after = lax.ppermute(to_before, axis, down)  21.3 us
    ppermute x6, starting transfers between devices, swap(): from_before = lax.ppermute(to_after, axis, up)  10 us
    ppermute x6, waiting for transfers between devices, swap(): from_before = lax.ppermute(to_after, axis, up)  6.33 us
    ppermute x6, starting transfers between devices, swap(): from_after = lax.ppermute(to_before, axis, down)  5.45 us
    unnamed x42, local copies, waits for them, and re-layouts  4.61 us
  transfers between devices with their start and end apart: 12, of which 11 were waited for; matrix products, arithmetic and copies ran while one was open for 0% of the time, Pallas kernels for 4%

profile of v1, /device:TPU:127, one launch (start us, length us, event | category | flops | bytes accessed | tf_op | source)
XLA Modules:
  0.0 84.8 jit_solution(3969646395207851289)
XLA Ops:
  0.0 0.0 copy-start.17
  0.0 0.0 copy-start.20
  0.0 0.0 copy-start.15
  0.0 0.0 copy-start.14
  0.1 0.0 copy-start.13
  0.1 0.0 copy-start.12
  0.1 1.9 %shard_map.199 = (bf16[192,128]{1,0:T(8,128)(2,1)}, bf16[192,128]{1,0:T(8,128)(2,1)}, f32[2,192,128]{2,1,0:T(8,128)}, f32[96,128]{1,0:T(8,128)}) custom-call(f32[4,48,80]{2,1,0:T(8,128)} %noise_init.1, f32[4,48,80]{2,1,0:T(8,128)} %noise_churn.1, bf16[10,6,40]{2,1,0:T(8,128)(2,1)} %bitcast.10), custom_call_target="tpu_custom_call" | custom-call | tf_op jit(solution)/shard_map/pallas_call | solution.py:483
  2.0 0.9 %collective-permute-start = (bf16[192,128]{1,0:T(8,128)(2,1)}, bf16[192,128]{1,0:T(8,128)(2,1)S(1)}, u32[]{:S(2)}, u32[]{:S(2)}) collective-permute-start(bf16[192,128]{1,0:T(8,128)(2,1)} %get-tuple-element.35), channel_id=1, source_target_pairs={{0,32},{32,64},{64,96},{96,128},{128,160},{160,192},{192,224},{224... | collective-permute-start | bytes 147464 | tf_op jit(solution)/shard_map/ppermute | solution.py:511
  2.9 2.1 %collective-permute-start.1 = (bf16[192,128]{1,0:T(8,128)(2,1)}, bf16[192,128]{1,0:T(8,128)(2,1)S(1)}, u32[]{:S(2)}, u32[]{:S(2)}) collective-permute-start(bf16[192,128]{1,0:T(8,128)(2,1)} %get-tuple-element.36), channel_id=1, source_target_pairs={{32,0},{64,32},{96,64},{128,96},{160,128},{192,160},{224,192},{0,2... | collective-permute-start | bytes 147464 | tf_op jit(solution)/shard_map/ppermute | solution.py:512
  5.0 3.4 %shard_map.201 = (bf16[48,256]{1,0:T(8,128)(2,1)}, bf16[256,256]{1,0:T(8,128)(2,1)}, bf16[256,256]{1,0:T(8,128)(2,1)}, bf16[4,1152,128]{2,1,0:T(8,128)(2,1)}, bf16[48,256]{1,0:T(8,128)(2,1)}) custom-call(bf16[36,128]{1,0:T(8,128)(2,1)} %bitcast.11, bf16[128,128]{1,0:T(8,128)(2,1)} %w_expand.1, bf16[128,128]{1,0:T(8,128)(2,1)} %w_project.1, ...), custom_call_target="tpu_custom_call" | custom-call | flops 150994944 | bytes 4194304 | tf_op jit(solution)/shard_map/pallas_call | solution.py:483
  8.3 0.0 collective-permute-done.from_upper
  8.3 1.3 %collective-permute-done.1.from_lower = bf16[192,128]{1,0:T(8,128)(2,1)S(1)} collective-permute-done((bf16[192,128]{1,0:T(8,128)(2,1)}, bf16[192,128]{1,0:T(8,128)(2,1)S(1)}, u32[]{:S(2)}, u32[]{:S(2)}) %collective-permute-start.1) | collective-permute-done | bytes 49184 | tf_op jit(solution)/shard_map/ppermute | solution.py:512
  9.7 0.3 shard_map.200
  10.0 4.2 %collective-permute-start.2 = (bf16[288,128]{1,0:T(8,128)(2,1)S(1)}, bf16[288,128]{1,0:T(8,128)(2,1)S(1)}, u32[]{:S(2)}, u32[]{:S(2)}) collective-permute-start(bf16[288,128]{1,0:T(8,128)(2,1)S(1)} %get-tuple-element.41), channel_id=1, source_target_pairs={{0,1},{1,2},{2,3},{3,4},{4,5},{5,6},{6,7},{7,8},{8,9},{9,10},{10,1... | collective-permute-start | bytes 221192 | tf_op jit(solution)/shard_map/ppermute | solution.py:511
  14.2 0.0 collective-permute-start.3
  14.2 0.1 pad_add_fusion.place
  14.3 1.3 %collective-permute-done.2.from_left = bf16[288,128]{1,0:T(8,128)(2,1)S(1)} collective-permute-done((bf16[288,128]{1,0:T(8,128)(2,1)S(1)}, bf16[288,128]{1,0:T(8,128)(2,1)S(1)}, u32[]{:S(2)}, u32[]{:S(2)}) %collective-permute-start.2) | collective-permute-done | bytes 73760 | tf_op jit(solution)/shard_map/ppermute | solution.py:511
  15.6 4.5 %collective-permute-done.3.from_right = bf16[288,128]{1,0:T(8,128)(2,1)S(1)} collective-permute-done((bf16[288,128]{1,0:T(8,128)(2,1)S(1)}, bf16[288,128]{1,0:T(8,128)(2,1)S(1)}, u32[]{:S(2)}, u32[]{:S(2)}) %collective-permute-start.3) | collective-permute-done | bytes 73760 | tf_op jit(solution)/shard_map/ppermute | solution.py:512
  20.1 0.0 copy-done.19
  20.1 0.0 copy-done.18
  20.2 1.3 %copy-done.2 = bf16[4,1152,128]{2,1,0:T(8,128)(2,1)S(1)} copy-done((bf16[4,1152,128]{2,1,0:T(8,128)(2,1)S(1)}, bf16[4,1152,128]{2,1,0:T(8,128)(2,1)}, u32[]{:S(2)}) %copy-start.2) | copy-done | bytes 1179672
  21.4 0.9 %copy-done.4 = bf16[256,256]{1,0:T(8,128)(2,1)S(1)} copy-done((bf16[256,256]{1,0:T(8,128)(2,1)S(1)}, bf16[256,256]{1,0:T(8,128)(2,1)}, u32[]{:S(2)}) %copy-start.4) | copy-done | bytes 131096
  22.3 0.9 %copy-done.6 = bf16[256,256]{1,0:T(8,128)(2,1)S(1)} copy-done((bf16[256,256]{1,0:T(8,128)(2,1)S(1)}, bf16[256,256]{1,0:T(8,128)(2,1)}, u32[]{:S(2)}) %copy-start.6) | copy-done | bytes 131096
  23.2 0.7 copy-done.7
  24.0 0.7 copy-done.9
  24.7 15.2 %shard_map.202 = (f32[384,128]{1,0:T(8,128)S(1)}, bf16[192,128]{1,0:T(8,128)(2,1)S(1)}, bf16[192,128]{1,0:T(8,128)(2,1)S(1)}, f32[384,128]{1,0:T(8,128)S(1)}, f3...) custom-call(s32[2]{0:T(128)S(1)} %pad_add_fusion.place, s32[384]{0:T(512)S(1)} %copy-done.14, ...), custom_call_target="tpu_custom_call" | custom-call | flops 5000000000 | bytes 8388608 | tf_op jit(solution)/shard_map/pallas_call | solution.py:483
  39.9 1.5 %collective-permute-start.4 = (bf16[192,128]{1,0:T(8,128)(2,1)S(1)}, bf16[192,128]{1,0:T(8,128)(2,1)S(1)}, u32[]{:S(2)}, u32[]{:S(2)}) collective-permute-start(bf16[192,128]{1,0:T(8,128)(2,1)S(1)} %get-tuple-element.49), channel_id=1, source_target_pairs={{0,32},{32,64},{64,96},{96,128},{128,160},{160,192},{192,224},{224... | collective-permute-start | bytes 147464 | tf_op jit(solution)/shard_map/ppermute | solution.py:511
  41.4 1.5 %collective-permute-start.5 = (bf16[192,128]{1,0:T(8,128)(2,1)S(1)}, bf16[192,128]{1,0:T(8,128)(2,1)S(1)}, u32[]{:S(2)}, u32[]{:S(2)}) collective-permute-start(bf16[192,128]{1,0:T(8,128)(2,1)S(1)} %get-tuple-element.50), channel_id=1, source_target_pairs={{32,0},{64,32},{96,64},{128,96},{160,128},{192,160},{224,192},{0,2... | collective-permute-start | bytes 147464 | tf_op jit(solution)/shard_map/ppermute | solution.py:512
  42.9 1.7 %collective-permute-done.4.from_upper = bf16[192,128]{1,0:T(8,128)(2,1)S(1)} collective-permute-done((bf16[192,128]{1,0:T(8,128)(2,1)S(1)}, bf16[192,128]{1,0:T(8,128)(2,1)S(1)}, u32[]{:S(2)}, u32[]{:S(2)}) %collective-permute-start.4) | collective-permute-done | bytes 49184 | tf_op jit(solution)/shard_map/ppermute | solution.py:511
  44.6 3.3 %collective-permute-done.5.from_lower = bf16[192,128]{1,0:T(8,128)(2,1)S(1)} collective-permute-done((bf16[192,128]{1,0:T(8,128)(2,1)S(1)}, bf16[192,128]{1,0:T(8,128)(2,1)S(1)}, u32[]{:S(2)}, u32[]{:S(2)}) %collective-permute-start.5) | collective-permute-done | bytes 49184 | tf_op jit(solution)/shard_map/ppermute | solution.py:512
  47.9 0.1 shard_map.203
  48.1 1.2 %collective-permute-start.6 = (bf16[192,128]{1,0:T(8,128)(2,1)S(1)}, bf16[192,128]{1,0:T(8,128)(2,1)S(1)}, u32[]{:S(2)}, u32[]{:S(2)}) collective-permute-start(bf16[192,128]{1,0:T(8,128)(2,1)S(1)} %get-tuple-element.52), channel_id=1, source_target_pairs={{0,1},{1,2},{2,3},{3,4},{4,5},{5,6},{6,7},{7,8},{8,9},{9,10},{10,1... | collective-permute-start | bytes 147464 | tf_op jit(solution)/shard_map/ppermute | solution.py:511
  49.3 0.0 collective-permute-start.7
  49.3 1.2 %collective-permute-done.6.from_left = bf16[192,128]{1,0:T(8,128)(2,1)S(1)} collective-permute-done((bf16[192,128]{1,0:T(8,128)(2,1)S(1)}, bf16[192,128]{1,0:T(8,128)(2,1)S(1)}, u32[]{:S(2)}, u32[]{:S(2)}) %collective-permute-start.6) | collective-permute-done | bytes 49184 | tf_op jit(solution)/shard_map/ppermute | solution.py:511
  50.5 4.4 %collective-permute-done.7.from_right = bf16[192,128]{1,0:T(8,128)(2,1)S(1)} collective-permute-done((bf16[192,128]{1,0:T(8,128)(2,1)S(1)}, bf16[192,128]{1,0:T(8,128)(2,1)S(1)}, u32[]{:S(2)}, u32[]{:S(2)}) %collective-permute-start.7) | collective-permute-done | bytes 49184 | tf_op jit(solution)/shard_map/ppermute | solution.py:512
  54.9 0.0 copy-done.3
  54.9 0.0 copy-done.8
  54.9 15.1 %shard_map.204 = (f32[384,128]{1,0:T(8,128)S(1)}, bf16[96,128]{1,0:T(8,128)(2,1)S(1)}, bf16[96,128]{1,0:T(8,128)(2,1)S(1)}, f32[384,128]{1,0:T(8,128)S(1)}) custom-call(s32[2]{0:T(128)S(1)} %pad_add_fusion.place, s32[384]{0:T(512)S(1)} %copy-done.14, f32[384]{0:T(512)S(1)} %copy-done.15, f32[384,128]{1,0:T(8,128)S(1)} %get-tuple-element.51.total, ...), custom_call_target="tpu_custom_call" | custom-call | flops 5000000000 | bytes 8388608 | tf_op jit(solution)/shard_map/pallas_call | solution.py:483
  70.1 1.2 %collective-permute-start.8 = (bf16[96,128]{1,0:T(8,128)(2,1)S(1)}, bf16[96,128]{1,0:T(8,128)(2,1)S(1)}, u32[]{:S(2)}, u32[]{:S(2)}) collective-permute-start(bf16[96,128]{1,0:T(8,128)(2,1)S(1)} %get-tuple-element.59), channel_id=1, source_target_pairs={{0,32},{32,64},{64,96},{96,128},{128,160},{160,192},{192,224},{224... | collective-permute-start | bytes 73736 | tf_op jit(solution)/shard_map/ppermute | solution.py:511
  71.3 1.8 %collective-permute-start.9 = (bf16[96,128]{1,0:T(8,128)(2,1)S(1)}, bf16[96,128]{1,0:T(8,128)(2,1)S(1)}, u32[]{:S(2)}, u32[]{:S(2)}) collective-permute-start(bf16[96,128]{1,0:T(8,128)(2,1)S(1)} %get-tuple-element.60), channel_id=1, source_target_pairs={{32,0},{64,32},{96,64},{128,96},{160,128},{192,160},{224,192},{0,2... | collective-permute-start | bytes 73736 | tf_op jit(solution)/shard_map/ppermute | solution.py:512
  73.1 1.2 %collective-permute-done.8.from_upper = bf16[96,128]{1,0:T(8,128)(2,1)S(1)} collective-permute-done((bf16[96,128]{1,0:T(8,128)(2,1)S(1)}, bf16[96,128]{1,0:T(8,128)(2,1)S(1)}, u32[]{:S(2)}, u32[]{:S(2)}) %collective-permute-start.8) | collective-permute-done | bytes 24608 | tf_op jit(solution)/shard_map/ppermute | solution.py:511
  74.3 3.3 %collective-permute-done.9.from_lower = bf16[96,128]{1,0:T(8,128)(2,1)S(1)} collective-permute-done((bf16[96,128]{1,0:T(8,128)(2,1)S(1)}, bf16[96,128]{1,0:T(8,128)(2,1)S(1)}, u32[]{:S(2)}, u32[]{:S(2)}) %collective-permute-start.9) | collective-permute-done | bytes 24608 | tf_op jit(solution)/shard_map/ppermute | solution.py:512
  77.6 0.1 shard_map.205
  77.7 0.9 %collective-permute-start.10 = (bf16[96,128]{1,0:T(8,128)(2,1)S(1)}, bf16[96,128]{1,0:T(8,128)(2,1)S(1)}, u32[]{:S(2)}, u32[]{:S(2)}) collective-permute-start(bf16[96,128]{1,0:T(8,128)(2,1)S(1)} %get-tuple-element.62), channel_id=1, source_target_pairs={{0,1},{1,2},{2,3},{3,4},{4,5},{5,6},{6,7},{7,8},{8,9},{9,10},{10,1... | collective-permute-start | bytes 73736 | tf_op jit(solution)/shard_map/ppermute | solution.py:511
  78.6 0.0 collective-permute-start.11
  78.6 0.9 %collective-permute-done.10.from_left = bf16[96,128]{1,0:T(8,128)(2,1)S(1)} collective-permute-done((bf16[96,128]{1,0:T(8,128)(2,1)S(1)}, bf16[96,128]{1,0:T(8,128)(2,1)S(1)}, u32[]{:S(2)}, u32[]{:S(2)}) %collective-permute-start.10) | collective-permute-done | bytes 24608 | tf_op jit(solution)/shard_map/ppermute | solution.py:511
  79.6 4.4 %collective-permute-done.11.from_right = bf16[96,128]{1,0:T(8,128)(2,1)S(1)} collective-permute-done((bf16[96,128]{1,0:T(8,128)(2,1)S(1)}, bf16[96,128]{1,0:T(8,128)(2,1)S(1)}, u32[]{:S(2)}, u32[]{:S(2)}) %collective-permute-start.11) | collective-permute-done | bytes 24608 | tf_op jit(solution)/shard_map/ppermute | solution.py:512
  84.0 0.8 shard_map.206
  (27 shorter events, 0.0 us)
Async XLA Ops:
  0.0 20.1 %copy-start.19 = (bf16[192,48]{1,0:T(8,128)(2,1)S(1)}, bf16[192,48]{1,0:T(8,128)(2,1)}, u32[]{:S(2)}) copy-start(bf16[192,48]{1,0:T(8,128)(2,1)} %constant.32.clone.grow) | copy-start | bytes 55300
  0.0 20.1 %copy-start.16 = (bf16[432,192]{1,0:T(8,128)(2,1)S(1)}, bf16[432,192]{1,0:T(8,128)(2,1)}, u32[]{:S(2)}) copy-start(bf16[432,192]{1,0:T(8,128)(2,1)} %constant.31.clone.pool) | copy-start | bytes 497668
  0.0 20.1 %copy-start.18 = (bf16[256,256]{1,0:T(8,128)(2,1)S(1)}, bf16[256,256]{1,0:T(8,128)(2,1)}, u32[]{:S(2)}) copy-start(bf16[256,256]{1,0:T(8,128)(2,1)} %constant.30.clone.mean_w) | copy-start | bytes 393220
  0.0 20.1 %copy-start.17 = (bf16[768,128]{1,0:T(8,128)(2,1)S(1)}, bf16[768,128]{1,0:T(8,128)(2,1)}, u32[]{:S(2)}) copy-start(bf16[768,128]{1,0:T(8,128)(2,1)} %constant.29.clone.back) | copy-start | bytes 589828
  0.0 20.1 %copy-start.20 = (bf16[128,128]{1,0:T(8,128)(2,1)S(1)}, bf16[128,128]{1,0:T(8,128)(2,1)}, u32[]{:S(2)}) copy-start(bf16[128,128]{1,0:T(8,128)(2,1)} %constant.28.clone.perm) | copy-start | bytes 98308
  0.0 20.1 %copy-start.15 = (f32[384]{0:T(512)S(1)}, f32[384]{0:T(512)}, u32[]{:S(2)}) copy-start(f32[384]{0:T(512)} %row_frac.3) | copy-start | bytes 4612
  0.0 20.1 %copy-start.14 = (s32[384]{0:T(512)S(1)}, s32[384]{0:T(512)}, u32[]{:S(2)}) copy-start(s32[384]{0:T(512)} %row_map.3) | copy-start | bytes 4612
  0.1 20.1 %copy-start.13 = (bf16[128,40]{0,1:T(8,128)(2,1)S(1)}, bf16[128,40]{0,1:T(8,128)(2,1)}, u32[]{:S(2)}) copy-start(bf16[128,40]{0,1:T(8,128)(2,1)} %param.29) | copy-start | bytes 30724
  0.1 20.1 %copy-start.12 = (f32[2560]{0:T(1024)S(1)}, f32[2560]{0:T(1024)}, u32[]{:S(2)}) copy-start(f32[2560]{0:T(1024)} %param.25) | copy-start | bytes 30724
  0.1 20.1 %copy-start.11 = (s32[2560]{0:T(1024)S(1)}, s32[2560]{0:T(1024)}, u32[]{:S(2)}) copy-start(s32[2560]{0:T(1024)} %param.24) | copy-start | bytes 30724
  2.0 7.7 %copy-start = (f32[2,192,128]{2,1,0:T(8,128)S(1)}, f32[2,192,128]{2,1,0:T(8,128)}, u32[]{:S(2)}) copy-start(f32[2,192,128]{2,1,0:T(8,128)} %get-tuple-element.37.own) | copy-start | bytes 589828
  2.0 7.7 %copy-start.1 = (f32[96,128]{1,0:T(8,128)S(1)}, f32[96,128]{1,0:T(8,128)}, u32[]{:S(2)}) copy-start(f32[96,128]{1,0:T(8,128)} %get-tuple-element.38.own_coarse) | copy-start | bytes 147460
  2.0 6.4 %collective-permute-start = (bf16[192,128]{1,0:T(8,128)(2,1)}, bf16[192,128]{1,0:T(8,128)(2,1)S(1)}, u32[]{:S(2)}, u32[]{:S(2)}) collective-permute-start(bf16[192,128]{1,0:T(8,128)(2,1)} %get-tuple-element.35), channel_id=1, source_target_pairs={{0,32},{32,64},{64,96},{96,128},{128,160},{160,192},{192,224},{224... | collective-permute-start | bytes 147464 | tf_op jit(solution)/shard_map/ppermute | solution.py:511
  2.9 6.8 %collective-permute-start.1 = (bf16[192,128]{1,0:T(8,128)(2,1)}, bf16[192,128]{1,0:T(8,128)(2,1)S(1)}, u32[]{:S(2)}, u32[]{:S(2)}) collective-permute-start(bf16[192,128]{1,0:T(8,128)(2,1)} %get-tuple-element.36), channel_id=1, source_target_pairs={{32,0},{64,32},{96,64},{128,96},{160,128},{192,160},{224,192},{0,2... | collective-permute-start | bytes 147464 | tf_op jit(solution)/shard_map/ppermute | solution.py:512
  10.0 5.6 %collective-permute-start.2 = (bf16[288,128]{1,0:T(8,128)(2,1)S(1)}, bf16[288,128]{1,0:T(8,128)(2,1)S(1)}, u32[]{:S(2)}, u32[]{:S(2)}) collective-permute-start(bf16[288,128]{1,0:T(8,128)(2,1)S(1)} %get-tuple-element.41), channel_id=1, source_target_pairs={{0,1},{1,2},{2,3},{3,4},{4,5},{5,6},{6,7},{7,8},{8,9},{9,10},{10,1... | collective-permute-start | bytes 221192 | tf_op jit(solution)/shard_map/ppermute | solution.py:511
  14.2 5.9 %collective-permute-start.3 = (bf16[288,128]{1,0:T(8,128)(2,1)S(1)}, bf16[288,128]{1,0:T(8,128)(2,1)S(1)}, u32[]{:S(2)}, u32[]{:S(2)}) collective-permute-start(bf16[288,128]{1,0:T(8,128)(2,1)S(1)} %get-tuple-element.42), channel_id=1, source_target_pairs={{1,0},{2,1},{3,2},{4,3},{5,4},{6,5},{7,6},{8,7},{9,8},{10,9},{11,1... | collective-permute-start | bytes 221192 | tf_op jit(solution)/shard_map/ppermute | solution.py:512
  20.1 1.3 %copy-start.2 = (bf16[4,1152,128]{2,1,0:T(8,128)(2,1)S(1)}, bf16[4,1152,128]{2,1,0:T(8,128)(2,1)}, u32[]{:S(2)}) copy-start(bf16[4,1152,128]{2,1,0:T(8,128)(2,1)} %get-tuple-element.46.level_w) | copy-start | bytes 3538948
  21.4 0.9 %copy-start.4 = (bf16[256,256]{1,0:T(8,128)(2,1)S(1)}, bf16[256,256]{1,0:T(8,128)(2,1)}, u32[]{:S(2)}) copy-start(bf16[256,256]{1,0:T(8,128)(2,1)} %get-tuple-element.44.expand_w) | copy-start | bytes 393220
  22.3 0.9 %copy-start.6 = (bf16[256,256]{1,0:T(8,128)(2,1)S(1)}, bf16[256,256]{1,0:T(8,128)(2,1)}, u32[]{:S(2)}) copy-start(bf16[256,256]{1,0:T(8,128)(2,1)} %get-tuple-element.45.project_w) | copy-start | bytes 393220
  23.2 0.7 copy-start.7
  24.0 0.7 copy-start.9
  24.7 30.2 %copy-start.3 = (bf16[4,1152,128]{2,1,0:T(8,128)(2,1)S(1)}, bf16[4,1152,128]{2,1,0:T(8,128)(2,1)}, u32[]{:S(2)}) copy-start(bf16[4,1152,128]{2,1,0:T(8,128)(2,1)} %get-tuple-element.46.level_w) | copy-start | bytes 3538948
  24.7 30.2 %copy-start.5 = (bf16[256,256]{1,0:T(8,128)(2,1)S(1)}, bf16[256,256]{1,0:T(8,128)(2,1)}, u32[]{:S(2)}) copy-start(bf16[256,256]{1,0:T(8,128)(2,1)} %get-tuple-element.44.expand_w) | copy-start | bytes 393220
  24.7 30.2 %copy-start.8 = (bf16[48,256]{1,0:T(8,128)(2,1)S(1)}, bf16[48,256]{1,0:T(8,128)(2,1)}, u32[]{:S(2)}) copy-start(bf16[48,256]{1,0:T(8,128)(2,1)} %get-tuple-element.43.first_w) | copy-start | bytes 73732
  24.7 30.2 %copy-start.10 = (bf16[48,256]{1,0:T(8,128)(2,1)S(1)}, bf16[48,256]{1,0:T(8,128)(2,1)}, u32[]{:S(2)}) copy-start(bf16[48,256]{1,0:T(8,128)(2,1)} %get-tuple-element.47.final_w) | copy-start | bytes 73732
  39.9 4.7 %collective-permute-start.4 = (bf16[192,128]{1,0:T(8,128)(2,1)S(1)}, bf16[192,128]{1,0:T(8,128)(2,1)S(1)}, u32[]{:S(2)}, u32[]{:S(2)}) collective-permute-start(bf16[192,128]{1,0:T(8,128)(2,1)S(1)} %get-tuple-element.49), channel_id=1, source_target_pairs={{0,32},{32,64},{64,96},{96,128},{128,160},{160,192},{192,224},{224... | collective-permute-start | bytes 147464 | tf_op jit(solution)/shard_map/ppermute | solution.py:511
  41.4 6.6 %collective-permute-start.5 = (bf16[192,128]{1,0:T(8,128)(2,1)S(1)}, bf16[192,128]{1,0:T(8,128)(2,1)S(1)}, u32[]{:S(2)}, u32[]{:S(2)}) collective-permute-start(bf16[192,128]{1,0:T(8,128)(2,1)S(1)} %get-tuple-element.50), channel_id=1, source_target_pairs={{32,0},{64,32},{96,64},{128,96},{160,128},{192,160},{224,192},{0,2... | collective-permute-start | bytes 147464 | tf_op jit(solution)/shard_map/ppermute | solution.py:512
  48.1 2.4 %collective-permute-start.6 = (bf16[192,128]{1,0:T(8,128)(2,1)S(1)}, bf16[192,128]{1,0:T(8,128)(2,1)S(1)}, u32[]{:S(2)}, u32[]{:S(2)}) collective-permute-start(bf16[192,128]{1,0:T(8,128)(2,1)S(1)} %get-tuple-element.52), channel_id=1, source_target_pairs={{0,1},{1,2},{2,3},{3,4},{4,5},{5,6},{6,7},{7,8},{8,9},{9,10},{10,1... | collective-permute-start | bytes 147464 | tf_op jit(solution)/shard_map/ppermute | solution.py:511
  49.3 5.6 %collective-permute-start.7 = (bf16[192,128]{1,0:T(8,128)(2,1)S(1)}, bf16[192,128]{1,0:T(8,128)(2,1)S(1)}, u32[]{:S(2)}, u32[]{:S(2)}) collective-permute-start(bf16[192,128]{1,0:T(8,128)(2,1)S(1)} %get-tuple-element.53), channel_id=1, source_target_pairs={{1,0},{2,1},{3,2},{4,3},{5,4},{6,5},{7,6},{8,7},{9,8},{10,9},{11,1... | collective-permute-start | bytes 147464 | tf_op jit(solution)/shard_map/ppermute | solution.py:512
  70.1 4.3 %collective-permute-start.8 = (bf16[96,128]{1,0:T(8,128)(2,1)S(1)}, bf16[96,128]{1,0:T(8,128)(2,1)S(1)}, u32[]{:S(2)}, u32[]{:S(2)}) collective-permute-start(bf16[96,128]{1,0:T(8,128)(2,1)S(1)} %get-tuple-element.59), channel_id=1, source_target_pairs={{0,32},{32,64},{64,96},{96,128},{128,160},{160,192},{192,224},{224... | collective-permute-start | bytes 73736 | tf_op jit(solution)/shard_map/ppermute | solution.py:511
  71.3 6.3 %collective-permute-start.9 = (bf16[96,128]{1,0:T(8,128)(2,1)S(1)}, bf16[96,128]{1,0:T(8,128)(2,1)S(1)}, u32[]{:S(2)}, u32[]{:S(2)}) collective-permute-start(bf16[96,128]{1,0:T(8,128)(2,1)S(1)} %get-tuple-element.60), channel_id=1, source_target_pairs={{32,0},{64,32},{96,64},{128,96},{160,128},{192,160},{224,192},{0,2... | collective-permute-start | bytes 73736 | tf_op jit(solution)/shard_map/ppermute | solution.py:512
  77.7 1.9 %collective-permute-start.10 = (bf16[96,128]{1,0:T(8,128)(2,1)S(1)}, bf16[96,128]{1,0:T(8,128)(2,1)S(1)}, u32[]{:S(2)}, u32[]{:S(2)}) collective-permute-start(bf16[96,128]{1,0:T(8,128)(2,1)S(1)} %get-tuple-element.62), channel_id=1, source_target_pairs={{0,1},{1,2},{2,3},{3,4},{4,5},{5,6},{6,7},{7,8},{8,9},{9,10},{10,1... | collective-permute-start | bytes 73736 | tf_op jit(solution)/shard_map/ppermute | solution.py:511
  78.6 5.4 %collective-permute-start.11 = (bf16[96,128]{1,0:T(8,128)(2,1)S(1)}, bf16[96,128]{1,0:T(8,128)(2,1)S(1)}, u32[]{:S(2)}, u32[]{:S(2)}) collective-permute-start(bf16[96,128]{1,0:T(8,128)(2,1)S(1)} %get-tuple-element.63), channel_id=1, source_target_pairs={{1,0},{2,1},{3,2},{4,3},{5,4},{6,5},{7,6},{8,7},{9,8},{10,9},{11,1... | collective-permute-start | bytes 73736 | tf_op jit(solution)/shard_map/ppermute | solution.py:512

commit v2 on v1

--- a/solution.py
+++ b/solution.py
@@ -15,7 +15,7 @@
 ROWS = 4 * PATCH_ROWS
 PAIRS = PATCH_ROWS // 2
 FIRST_BATCH, LAST_BATCH = 16, 24
-LEVEL1_BATCH, LEVEL2_BATCH = 24, 24
+LEVEL1_BATCH, COND_BATCH = 12, 8
 SIDE = 16
 COARSE_SLOTS = 48
 
@@ -33,15 +33,20 @@
 def _constants():
     place = np.arange(128)
     column = 8 * (place % 16) + place // 16
-    perm = (column[:, None] == np.arange(128)[None, :]).astype(np.float32)
+    shifts = [
+        (np.arange(128)[:, None] == (column + shift - 1)[None, :]).astype(np.float32) for shift in range(3)
+    ]
+    shifts = np.concatenate(shifts, 1)
     back = []
     for shift in range(3):
         one = (column[:, None] == (np.arange(128) + shift - 1)[None, :]).astype(np.float32)
         back += [one, one]
     back = np.concatenate(back, 0)
-    pick_in = np.zeros((2, 48, 36), np.float32)
-    pick_out = np.zeros((2, 48, 36), np.float32)
+    pick_in = np.zeros((2, 48, 128), np.float32)
+    pick_out = np.zeros((2, 48, 128), np.float32)
+    pick_cond = np.zeros((2, 80, 128), np.float32)
     for pi in range(2):
+        pick_cond[pi, pi * 40 + np.arange(40), np.arange(40)] = 1.0
         for dc in range(3):
             for pp in range(4):
                 for e in range(4):
@@ -51,6 +56,7 @@
                     dr = pi + 2 - pp
                     if 0 <= dr <= 2:
                         pick_out[pi, dc * 16 + pp * 4 + e, (3 * dr + dc) * 4 + e] = 1.0
+    picks = np.concatenate([v.reshape(-1, 128) for v in (pick_in, pick_cond, pick_out, np.eye(128))], 0)
     pool = np.zeros((9, 6, 8, 12, 16), np.float32)
     for dr in range(3):
         for dc in range(3):
@@ -59,16 +65,16 @@
                     rr, cc = r + dr - 1, c + dc - 1
                     if 0 <= rr < 6 and 0 <= cc < 8:
                         pool[3 * dr + dc, r, c, 2 * rr : 2 * rr + 2, 2 * cc : 2 * cc + 2] = 0.25
-    pool = pool.reshape(432, 192)
+    pool = pool.reshape(432, 6, 2, 16).transpose(0, 2, 1, 3).reshape(432, 192)
     grow = np.zeros((12, 16, 6, 8), np.float32)
     for r in range(12):
         for c in range(16):
             grow[r, c, r // 2, c // 2] = 1.0
-    grow = grow.reshape(192, 48)
-    return perm, back, pick_in, pick_out, pool, grow
-
-
-PERM, BACK, PICK_IN, PICK_OUT, POOL, GROW = _constants()
+    grow = grow.reshape(6, 2, 16, 48).transpose(1, 0, 2, 3).reshape(192, 48)
+    return shifts, back, picks, pool, grow
+
+
+SHIFTS, BACK, PICKS, POOL, GROW = _constants()
 
 
 def dot_nt(a, b):
@@ -89,18 +95,18 @@
 
 
 def prepare_kernel(
-    w_state, w_expand, w_project, w_levels, w_final, eye, pick_in, pick_out,
-    first_w, expand_w, project_w, level_w, final_w, flat_final,
+    w_state, w_cond, w_expand, w_project, w_levels, w_final, picks,
+    first_w, expand_w, project_w, level_w, last_level_w, final_w, flat_final,
 ):
-    unit = eye[...]
+    unit = picks[352:480, :]
     for k in range(9):
         flat_final[4 * k : 4 * k + 4, :] = w_final[k].astype(F32)
     final_rows = flat_final[...].astype(BF16)
-    state_rows = w_state[...]
     for pi in range(2):
         part = slice(pi * 128, pi * 128 + 128)
-        first_w[:, part] = dot_nn(pick_in[pi], state_rows).astype(BF16)
-        final_w[:, part] = dot_nn(pick_out[pi], final_rows).astype(BF16)
+        first_w[0:48, part] = dot_nn(picks[pi * 48 : pi * 48 + 48, 0:36], w_state[...]).astype(BF16)
+        first_w[48:128, part] = dot_nn(picks[96 + pi * 80 : 176 + pi * 80, 0:40], w_cond[...]).astype(BF16)
+        final_w[:, part] = dot_nn(picks[256 + pi * 48 : 304 + pi * 48, 0:36], final_rows).astype(BF16)
     zero = jnp.zeros((128, 128), BF16)
     for source, target, factor in ((w_expand, expand_w, 0.5), (w_project, project_w, 1.0)):
         block = (dot_nt(unit, source[...]) * factor).astype(BF16)
@@ -108,9 +114,17 @@
         target[128:256, 128:256] = block
         target[0:128, 128:256] = zero
         target[128:256, 0:128] = zero
-    for level in range(4):
-        for k in range(9):
-            level_w[level, k * 128 : k * 128 + 128, :] = dot_nt(unit, w_levels[level, k]).astype(BF16)
+    for level in range(3):
+        for dc in range(3):
+            level_w[level, (9 + dc) * 128 : (10 + dc) * 128, 0:128] = zero
+            level_w[level, dc * 128 : dc * 128 + 128, 128:256] = zero
+            for dr in range(3):
+                block = dot_nt(unit, w_levels[level, 3 * dr + dc]).astype(BF16)
+                for pi in range(2):
+                    start = (3 * (dr + pi) + dc) * 128
+                    level_w[level, start : start + 128, pi * 128 : pi * 128 + 128] = block
+    for k in range(9):
+        last_level_w[k * 128 : k * 128 + 128, :] = dot_nt(unit, w_levels[3, k]).astype(BF16)
 
 
 def pack_rows_kernel(noise_init, noise_churn, coarse, to_upper, to_lower, own, own_coarse, padded):
@@ -174,11 +188,9 @@
         ).astype(BF16)
 
 
-def halve(values, rows, groups):
-    grouped = values.reshape(rows // 2, 2, groups // 2, 2, SIDE, 128)
-    return 0.25 * (
-        (grouped[:, 0, :, 0] + grouped[:, 0, :, 1]) + (grouped[:, 1, :, 0] + grouped[:, 1, :, 1])
-    )
+def halve(values, pairs, groups):
+    summed = (values[:, 0:128] + values[:, 128:256]).reshape(pairs, groups // 2, 2, SIDE, 128)
+    return 0.25 * (summed[:, :, 0] + summed[:, :, 1])
 
 
 def norm_silu(values, mean_w):
@@ -187,12 +199,16 @@
     return half + half * jnp.tanh(half)
 
 
-def conv_rows(source, weight, row, rows, groups):
+def conv_rows(source, weight, pair, pairs, groups):
     taps = [
-        source[pl.ds(row + dr, rows), dc * SIDE : dc * SIDE + groups * SIDE, :].reshape(
-            rows * groups * SIDE, 128
+        jnp.concatenate(
+            [
+                source[2 * (pair + m) + rr, dc * SIDE : dc * SIDE + groups * SIDE, :]
+                for m in range(pairs)
+            ],
+            axis=0,
         )
-        for dr in range(3)
+        for rr in range(4)
         for dc in range(3)
     ]
     return dot_nn(jnp.concatenate(taps, axis=1), weight)
@@ -204,18 +220,16 @@
     pltpu.VMEM((50, 96, 128), BF16),
     pltpu.VMEM((26, 64, 128), BF16),
     pltpu.VMEM((14, 48, 128), BF16),
-    pltpu.VMEM((48, 64, 128), F32),
-    pltpu.VMEM((24, 32, 128), F32),
+    pltpu.VMEM((24, 64, 256), F32),
+    pltpu.VMEM((12, 32, 256), F32),
     pltpu.VMEM((3, 392, 128), F32),
     pltpu.VMEM((3, 400, 128), F32),
 ]
 
 
-def denoise(
-    state, colmix, coarse_fields, lat, row_map, row_frac, weights, constants, scratch, noise_level, out
-):
-    first_w, expand_w, project_w, level_w, final_w = weights
-    perm, back, mean_w, pool, grow = constants
+def denoise(state, cond_rows, weights, constants, scratch, noise_level, out):
+    first_w, expand_w, project_w, level_w, last_level_w, final_w = weights
+    shifts, back, mean_w, pool, grow = constants
     scaled, hidden, pooled1, pooled2, pooled3, level1, level2, taps_a, taps_b = scratch
     total_sq = noise_level * noise_level + sigma_data * sigma_data
 
@@ -224,36 +238,22 @@
         scaled[shift, 384:400, :] = jnp.zeros((16, 128), F32)
         taps_a[shift, 384:392, :] = jnp.zeros((8, 128), F32)
         taps_b[shift, 0:8, :] = jnp.zeros((8, 128), F32)
-    base = state[...] * (1.0 / math.sqrt(total_sq))
-    lane = lanes((ROWS, 128))
-    scaled[0, 4 : 4 + ROWS, :] = jnp.where(lane == 0, 0.0, pltpu.roll(base, 1, 1))
-    scaled[1, 4 : 4 + ROWS, :] = base
-    scaled[2, 4 : 4 + ROWS, :] = jnp.where(lane == 127, 0.0, pltpu.roll(base, 127, 1))
+    base = (state[...] * (1.0 / math.sqrt(total_sq))).astype(BF16)
+    for shift in range(3):
+        scaled[shift, 4 : 4 + ROWS, :] = dot_nn(base, shifts[:, shift * 128 : shift * 128 + 128])
     for buffer, rows in ((pooled1, 50), (pooled2, 26), (pooled3, 14)):
         blank = jnp.zeros(buffer.shape[1:], BF16)
         buffer[0] = blank
         buffer[rows - 1] = blank
 
-    def coarse_row(p):
-        y = lat * TILE_ROWS - MARGIN + p
-        inside = (y >= 0) & (y < 8 * TILE_ROWS)
-        y = jnp.clip(y, 0, 8 * TILE_ROWS - 1)
-        at = jnp.clip(row_map[y] - (lat * 6 - 6), 0, 16)
-        fraction = row_frac[y]
-        near = jnp.where(inside, 1.0 - fraction, 0.0)
-        far = jnp.where(inside, fraction, 0.0)
-        return near * coarse_fields[at] + far * coarse_fields[at + 1]
-
     def first(c, carry):
-        pre = []
+        turned = []
         for k in range(FIRST_BATCH):
-            i = FIRST_BATCH * c + k
             row = pl.multiple_of(8 * FIRST_BATCH * c, 8) + 8 * k
             columns = [scaled[shift, pl.ds(row, 16), :].astype(BF16) for shift in range(3)]
-            turned = dot_nt(perm[...], jnp.concatenate(columns + [colmix[...]], axis=0)).astype(BF16)
-            fields = jnp.concatenate([coarse_row(2 * i), coarse_row(2 * i + 1)], axis=1).astype(BF16)
-            pre.append(dot_nn(turned, jnp.concatenate([first_w[...], fields], axis=0)))
-        act = norm_silu(jnp.concatenate(pre, axis=0), mean_w[...])
+            turned.append(jnp.concatenate(columns + [cond_rows[FIRST_BATCH * c + k]], axis=0).T)
+        pre = dot_nn(jnp.concatenate(turned, axis=0), first_w[...])
+        act = norm_silu(pre, mean_w[...])
         hidden[pl.ds(FIRST_BATCH * c, FIRST_BATCH)] = act.astype(BF16).reshape(FIRST_BATCH, 128, 256)
         summed = (act[:, 0:128] + act[:, 128:256]).reshape(FIRST_BATCH, 4, 2, SIDE, 128)
         pad_store(pooled1, FIRST_BATCH * c, 0.25 * (summed[:, :, 0] + summed[:, :, 1]), 4)
@@ -261,40 +261,39 @@
 
     lax.fori_loop(0, PAIRS // FIRST_BATCH, first, 0)
 
-    mean_one = mean_w[0:128, 0:128]
-
     def one(c, carry):
-        act = norm_silu(conv_rows(pooled1, level_w[0], LEVEL1_BATCH * c, LEVEL1_BATCH, 4), mean_one)
-        level1[pl.ds(LEVEL1_BATCH * c, LEVEL1_BATCH)] = act.reshape(LEVEL1_BATCH, 64, 128)
-        pad_store(pooled2, LEVEL1_BATCH // 2 * c, halve(act, LEVEL1_BATCH, 4), 2)
+        act = norm_silu(conv_rows(pooled1, level_w[0], LEVEL1_BATCH * c, LEVEL1_BATCH, 4), mean_w[...])
+        level1[pl.ds(LEVEL1_BATCH * c, LEVEL1_BATCH)] = act.reshape(LEVEL1_BATCH, 64, 256)
+        pad_store(pooled2, LEVEL1_BATCH * c, halve(act, LEVEL1_BATCH, 4), 2)
         return carry
 
-    lax.fori_loop(0, 48 // LEVEL1_BATCH, one, 0)
-
-    def two(c, carry):
-        act = norm_silu(conv_rows(pooled2, level_w[1], LEVEL2_BATCH * c, LEVEL2_BATCH, 2), mean_one)
-        level2[pl.ds(LEVEL2_BATCH * c, LEVEL2_BATCH)] = act.reshape(LEVEL2_BATCH, 32, 128)
-        pad_store(pooled3, LEVEL2_BATCH // 2 * c, halve(act, LEVEL2_BATCH, 2), 1)
-        return carry
-
-    lax.fori_loop(0, 24 // LEVEL2_BATCH, two, 0)
-
-    act3 = norm_silu(conv_rows(pooled3, level_w[2], 0, 12, 1), mean_one)
+    lax.fori_loop(0, 24 // LEVEL1_BATCH, one, 0)
+
+    act = norm_silu(conv_rows(pooled2, level_w[1], 0, 12, 2), mean_w[...])
+    level2[...] = act.reshape(12, 32, 256)
+    pad_store(pooled3, 0, halve(act, 12, 2), 1)
+
+    act3 = norm_silu(conv_rows(pooled3, level_w[2], 0, 6, 1), mean_w[...])
+    act3 = jnp.concatenate([act3[:, 0:128], act3[:, 128:256]], axis=0)
     shifted = dot_nn(pool[...], act3.astype(BF16)).astype(BF16)
     act4 = norm_silu(
-        dot_nn(jnp.concatenate([shifted[48 * k : 48 * k + 48] for k in range(9)], axis=1), level_w[3]),
-        mean_one,
+        dot_nn(jnp.concatenate([shifted[48 * k : 48 * k + 48] for k in range(9)], axis=1), last_level_w[...]),
+        mean_w[0:128, 0:128],
     )
     merged3 = act3 + dot_nn(grow[...], act4.astype(BF16))
-    merged2 = level2[...].reshape(12, 2, 2, SIDE, 128) + merged3.reshape(12, 1, 1, SIDE, 128)
-    level2[...] = merged2.reshape(24, 32, 128)
+    for a in range(12):
+        start = a % 2 * 96 + a // 2 * SIDE
+        above = merged3[start : start + SIDE]
+        above = jnp.concatenate([above, above], axis=0)
+        level2[a] = level2[a] + jnp.concatenate([above, above], axis=1)
 
     def last(c, carry):
         merged = []
         for k in range(LAST_BATCH):
-            i = LAST_BATCH * c + k
-            coarse2 = level2[i // 2].reshape(2, 1, SIDE, 128)
-            merged1 = level1[i].reshape(2, 2, SIDE, 128) + coarse2
+            half_of = slice(k % 2 * 128, k % 2 * 128 + 128)
+            quarter_of = slice(k // 2 % 2 * 128, k // 2 % 2 * 128 + 128)
+            coarse2 = level2[LAST_BATCH // 4 * c + k // 4, :, quarter_of].reshape(2, 1, SIDE, 128)
+            merged1 = level1[LAST_BATCH // 2 * c + k // 2, :, half_of].reshape(2, 2, SIDE, 128) + coarse2
             merged1 = merged1.reshape(4, 1, SIDE, 128)
             merged1 = jnp.concatenate([merged1, merged1], axis=1).reshape(128, 128)
             merged.append(jnp.concatenate([merged1, merged1], axis=1))
@@ -343,10 +342,10 @@
 
 
 def first_kernel(
-    place, row_map, row_frac, col_map, col_frac, strip, coarse_strip, from_left, from_right, w_cond,
-    first_w, expand_w, project_w, level_w, final_w, perm, back, mean_w, pool, grow,
-    den, to_upper, to_lower, state, churn, fields, colmix,
-    window, *scratch,
+    place, row_map, row_frac, col_map, col_frac, strip, coarse_strip, from_left, from_right,
+    first_w, expand_w, project_w, level_w, last_level_w, final_w, shifts, back, mean_w, pool, grow,
+    den, to_upper, to_lower, state, churn, cond_rows,
+    window, coarse_t, *scratch,
 ):
     lat, lon = place[0], place[1]
     lane = lanes((192, 128))
@@ -369,8 +368,11 @@
                 rows = roll_lanes(source[192:288, :].astype(F32), -40 * part)
             for j in range(6):
                 window[part * 6 + j, t * 16 : t * 16 + 16, :] = rows[j * 16 : j * 16 + 16]
-    stacked = window[...].reshape(18 * COARSE_SLOTS, 128)[:, 0:40].astype(BF16)
-    fields[...] = dot_nn(stacked, w_cond[...]).reshape(18, COARSE_SLOTS, 128)
+    unit = jnp.where(
+        lanes((40, 128)) == lax.broadcasted_iota(jnp.int32, (40, 128), 0), 1.0, 0.0
+    ).astype(BF16)
+    for j in range(18):
+        coarse_t[j] = dot_nt(unit, window[j].astype(BF16))
 
     begin = lon * TILE_COLS - MARGIN
     begin = jnp.where(begin < 0, begin + 32 * TILE_COLS, begin)
@@ -392,12 +394,29 @@
     column = jnp.where(slot - 16 * tile < 10, slot - 6 * tile, -1)
     fraction = stretch(col_frac)
     mix = jnp.where(column == offset, 1.0 - fraction, 0.0) + jnp.where(column == offset + 1, fraction, 0.0)
-    colmix[...] = mix.astype(BF16)
+    mix = dot_nn(mix.astype(BF16), shifts[:, 128:256]).astype(BF16)
+
+    def coarse_row(p):
+        y = lat * TILE_ROWS - MARGIN + p
+        within = (y >= 0) & (y < 8 * TILE_ROWS)
+        y = jnp.clip(y, 0, 8 * TILE_ROWS - 1)
+        at = jnp.clip(row_map[y] - (lat * 6 - 6), 0, 16)
+        weight = row_frac[y]
+        near = jnp.where(within, 1.0 - weight, 0.0)
+        far = jnp.where(within, weight, 0.0)
+        return near * coarse_t[at] + far * coarse_t[at + 1]
+
+    def interpolate(c, carry):
+        rows = [coarse_row(2 * COND_BATCH * c + k) for k in range(2 * COND_BATCH)]
+        fine = dot_nn(jnp.concatenate(rows, axis=0).astype(BF16), mix)
+        cond_rows[pl.ds(COND_BATCH * c, COND_BATCH)] = fine.astype(BF16).reshape(COND_BATCH, 80, 128)
+        return carry
+
+    lax.fori_loop(0, PAIRS // COND_BATCH, interpolate, 0)
 
     denoise(
-        state, colmix, fields, lat, row_map, row_frac,
-        (first_w, expand_w, project_w, level_w, final_w), (perm, back, mean_w, pool, grow),
-        scratch, level_first, den,
+        state, cond_rows, (first_w, expand_w, project_w, level_w, last_level_w, final_w),
+        (shifts, back, mean_w, pool, grow), scratch, level_first, den,
     )
     send_rows(lat, den, to_upper, to_lower, 192)
 
@@ -413,8 +432,8 @@
 
 
 def second_kernel(
-    place, row_map, row_frac, total, from_left, from_right, state, churn, fields, colmix,
-    first_w, expand_w, project_w, level_w, final_w, perm, back, mean_w, pool, grow,
+    place, total, from_left, from_right, state, churn, cond_rows,
+    first_w, expand_w, project_w, level_w, last_level_w, final_w, shifts, back, mean_w, pool, grow,
     den, to_upper, to_lower, raised,
     *scratch,
 ):
@@ -436,9 +455,8 @@
         raised[rows, :] = value
     raised[...] = jnp.where(inside, raised[...], 0.0)
     denoise(
-        raised, colmix, fields, lat, row_map, row_frac,
-        (first_w, expand_w, project_w, level_w, final_w), (perm, back, mean_w, pool, grow),
-        scratch, level_raised, den,
+        raised, cond_rows, (first_w, expand_w, project_w, level_w, last_level_w, final_w),
+        (shifts, back, mean_w, pool, grow), scratch, level_raised, den,
     )
     send_rows(lat, den, to_upper, to_lower, 96)
 
@@ -477,16 +495,18 @@
     return jax.ShapeDtypeStruct(dims, dtype)
 
 
-def call(kernel, operands, outs, scratch=(), scalars=0, cost=(0, 0, 0), room=40):
-    smem = pl.BlockSpec(memory_space=pltpu.SMEM)
-    vmem = pl.BlockSpec(memory_space=pltpu.VMEM)
+def call(kernel, operands, outs, scratch=(), scalars=0, cost=(0, 0, 0), far=()):
+    operands = [
+        pltpu.with_memory_space_constraint(a, pltpu.HBM) if n in far else a for n, a in enumerate(operands)
+    ]
     return pl.pallas_call(
         kernel,
         out_shape=outs,
-        in_specs=[smem] * scalars + [vmem] * (len(operands) - scalars),
-        out_specs=[vmem] * len(outs),
+        in_specs=[pl.BlockSpec(memory_space=pltpu.SMEM)] * scalars
+        + [pl.BlockSpec(memory_space=pltpu.VMEM)] * (len(operands) - scalars),
+        out_specs=[pl.BlockSpec(memory_space=pltpu.VMEM)] * len(outs),
         scratch_shapes=list(scratch),
-        compiler_params=pltpu.CompilerParams(vmem_limit_bytes=room << 20),
+        compiler_params=pltpu.CompilerParams(vmem_limit_bytes=40 << 20),
         cost_estimate=pl.CostEstimate(flops=cost[0], bytes_accessed=cost[1], transcendentals=cost[2]),
     )(*operands)
 
@@ -518,7 +538,7 @@
         (noise_init, noise_churn, coarse.transpose(2, 1, 0)),
         [msg, msg, shape((2, 192, 128), F32), shape((96, 128), F32)],
         [pltpu.VMEM((2, 192, 128), F32)],
-        room=60,
+        far=(0, 1, 2),
     )
     from_upper, from_lower = swap("lat", to_upper, to_lower)
     wide_msg = shape((288, 128), BF16)
@@ -532,35 +552,35 @@
     weights = call(
         prepare_kernel,
         (
-            w_state.T, w_expand, w_project, w_levels, w_final, jnp.asarray(np.eye(128), BF16),
-            jnp.asarray(PICK_IN, BF16), jnp.asarray(PICK_OUT, BF16),
+            w_state.T, w_cond.T, w_expand, w_project, w_levels, w_final, jnp.asarray(PICKS, BF16),
         ),
         [
-            shape((48, 256), BF16), shape((256, 256), BF16), shape((256, 256), BF16),
-            shape((4, 1152, 128), BF16), shape((48, 256), BF16),
+            shape((128, 256), BF16), shape((256, 256), BF16), shape((256, 256), BF16),
+            shape((3, 1536, 256), BF16), shape((1152, 128), BF16), shape((48, 256), BF16),
         ],
         [pltpu.VMEM((36, 128), F32)],
         cost=(2 * 36 * 128**3, 4 << 20, 0),
-        room=60,
+        far=range(7),
     )
     mean_w = np.zeros((256, 256), np.float32)
     mean_w[:128, :128] = mean_w[128:, 128:] = 4.0 / 128.0
-    constants = [jnp.asarray(c, BF16) for c in (PERM, BACK, mean_w, POOL, GROW)]
+    constants = [jnp.asarray(c, BF16) for c in (SHIFTS, BACK, mean_w, POOL, GROW)]
     field = shape((ROWS, 128), F32)
     cost = (5 * 10**9, 8 << 20, 3 * 10**6)
-    den, to_upper, to_lower, state, churn, fields, colmix = call(
+    den, to_upper, to_lower, state, churn, cond_rows = call(
         first_kernel,
         (
             place, row_map, row_frac, col_map.reshape(20, 128), col_frac.reshape(20, 128),
-            strip, coarse_strip, from_left, from_right, w_cond.T, *weights, *constants,
+            strip, coarse_strip, from_left, from_right, *weights, *constants,
         ),
         [
             field, msg, msg, field, field,
-            shape((18, COARSE_SLOTS, 128), F32), shape((COARSE_SLOTS, 128), BF16),
+            shape((PAIRS, 80, 128), BF16),
         ],
-        [pltpu.VMEM((18, COARSE_SLOTS, 128), F32)] + CORE_SCRATCH,
+        [pltpu.VMEM((18, COARSE_SLOTS, 128), F32), pltpu.VMEM((18, 40, COARSE_SLOTS), F32)] + CORE_SCRATCH,
         scalars=3,
         cost=cost,
+        far=(1, 2, 3, 4, 15, 16, 17, 18, 19),
     )
     from_upper, from_lower = swap("lat", to_upper, to_lower)
     total, to_left, to_right = call(
@@ -571,13 +591,14 @@
     den, to_upper, to_lower, raised = call(
         second_kernel,
         (
-            place, row_map, row_frac, total, from_left, from_right, state, churn, fields, colmix,
+            place, total, from_left, from_right, state, churn, cond_rows,
             *weights, *constants,
         ),
         [field, short_msg, short_msg, field],
         CORE_SCRATCH,
-        scalars=3,
+        scalars=1,
         cost=cost,
+        far=(13, 14, 15, 16, 17),
     )
     from_upper, from_lower = swap("lat", to_upper, to_lower)
     total, to_left, to_right = call(

time: 85.1 us -> 73.9 us (0.87)
  the two profiles are of different devices: /device:TPU:127 before, /device:TPU:111 now
where the time goes in v2:
time: 73.9 us; the launch traced here: 73.7 us
  Pallas kernels  30.1 us (41%)
  waiting for transfers between devices  22.1 us (30%)
  starting transfers between devices  21.3 us (29%)
    pallas_call x8, Pallas kernels, call(): pl.pallas_call(kernel, out_shape=outs, in_specs=[pl.BlockSpec(memory_spac...  30.1 us
    ppermute x6, waiting for transfers between devices, swap(): from_after = lax.ppermute(to_before, axis, down)  16 us
    ppermute x6, starting transfers between devices, swap(): from_before = lax.ppermute(to_after, axis, up)  15.4 us
    ppermute x6, waiting for transfers between devices, swap(): from_before = lax.ppermute(to_after, axis, up)  6.14 us
    ppermute x6, starting transfers between devices, swap(): from_after = lax.ppermute(to_before, axis, down)  5.86 us
  transfers between devices with their start and end apart: 12, of which 11 were waited for; matrix products, arithmetic and copies ran while one was open for 0% of the time, Pallas kernels for 3%

profile of v2, /device:TPU:111, one launch (start us, length us, event | category | flops | bytes accessed | tf_op | source)
XLA Modules:
  0.0 73.7 jit_solution(14789562706030124459)
XLA Ops:
  0.0 1.0 %shard_map.181 = (bf16[192,128]{1,0:T(8,128)(2,1)S(1)}, bf16[192,128]{1,0:T(8,128)(2,1)S(1)}, f32[2,192,128]{2,1,0:T(8,128)S(1)}, f32[96,128]{1,0:T(8,128)S(1)}) custom-call(f32[4,48,80]{2,1,0:T(8,128)} %noise_init.1, f32[4,48,80]{2,1,0:T(8,128)} %noise_churn.1, bf16[10,6,40]{2,1,0:T(8,128)(2,1)} %bitcast.7), custom_call_target="tpu_custom_call" | custom-call | tf_op jit(solution)/shard_map/pallas_call | solution.py:502
  1.0 2.1 %collective-permute-start = (bf16[192,128]{1,0:T(8,128)(2,1)S(1)}, bf16[192,128]{1,0:T(8,128)(2,1)S(1)}, u32[]{:S(2)}, u32[]{:S(2)}) collective-permute-start(bf16[192,128]{1,0:T(8,128)(2,1)S(1)} %get-tuple-element.35), channel_id=1, source_target_pairs={{0,32},{32,64},{64,96},{96,128},{128,160},{160,192},{192,224},{224... | collective-permute-start | bytes 147464 | tf_op jit(solution)/shard_map/ppermute | solution.py:531
  3.1 1.9 %collective-permute-start.1 = (bf16[192,128]{1,0:T(8,128)(2,1)S(1)}, bf16[192,128]{1,0:T(8,128)(2,1)S(1)}, u32[]{:S(2)}, u32[]{:S(2)}) collective-permute-start(bf16[192,128]{1,0:T(8,128)(2,1)S(1)} %get-tuple-element.36), channel_id=1, source_target_pairs={{32,0},{64,32},{96,64},{128,96},{160,128},{192,160},{224,192},{0,2... | collective-permute-start | bytes 147464 | tf_op jit(solution)/shard_map/ppermute | solution.py:532
  5.0 2.4 %shard_map.183 = (bf16[128,256]{1,0:T(8,128)(2,1)S(1)}, bf16[256,256]{1,0:T(8,128)(2,1)S(1)}, bf16[256,256]{1,0:T(8,128)(2,1)S(1)}, bf16[3,1536,256]{2,1,0:T(8,1...) custom-call(bf16[36,128]{1,0:T(8,128)(2,1)} %bitcast.8, bf16[40,128]{1,0:T(8,128)(2,1)} %bitcast.9, ...), custom_call_target="tpu_custom_call" | custom-call | flops 150994944 | bytes 4194304 | tf_op jit(solution)/shard_map/pallas_call | solution.py:502
  7.4 0.0 collective-permute-done.from_upper
  7.4 0.7 collective-permute-done.1.from_lower
  8.1 0.3 shard_map.182
  8.4 5.2 %collective-permute-start.2 = (bf16[288,128]{1,0:T(8,128)(2,1)S(1)}, bf16[288,128]{1,0:T(8,128)(2,1)S(1)}, u32[]{:S(2)}, u32[]{:S(2)}) collective-permute-start(bf16[288,128]{1,0:T(8,128)(2,1)S(1)} %get-tuple-element.41), channel_id=1, source_target_pairs={{0,1},{1,2},{2,3},{3,4},{4,5},{5,6},{6,7},{7,8},{8,9},{9,10},{10,1... | collective-permute-start | bytes 221192 | tf_op jit(solution)/shard_map/ppermute | solution.py:531
  13.6 0.0 collective-permute-start.3
  13.6 0.1 pad_add_fusion.place
  13.7 1.3 %collective-permute-done.2.from_left = bf16[288,128]{1,0:T(8,128)(2,1)S(1)} collective-permute-done((bf16[288,128]{1,0:T(8,128)(2,1)S(1)}, bf16[288,128]{1,0:T(8,128)(2,1)S(1)}, u32[]{:S(2)}, u32[]{:S(2)}) %collective-permute-start.2) | collective-permute-done | bytes 73760 | tf_op jit(solution)/shard_map/ppermute | solution.py:531
  15.0 4.5 %collective-permute-done.3.from_right = bf16[288,128]{1,0:T(8,128)(2,1)S(1)} collective-permute-done((bf16[288,128]{1,0:T(8,128)(2,1)S(1)}, bf16[288,128]{1,0:T(8,128)(2,1)S(1)}, u32[]{:S(2)}, u32[]{:S(2)}) %collective-permute-start.3) | collective-permute-done | bytes 73760 | tf_op jit(solution)/shard_map/ppermute | solution.py:532
  19.5 13.4 %shard_map.184 = (f32[384,128]{1,0:T(8,128)S(1)}, bf16[192,128]{1,0:T(8,128)(2,1)S(1)}, bf16[192,128]{1,0:T(8,128)(2,1)S(1)}, f32[384,128]{1,0:T(8,128)S(1)}, f3...) custom-call(s32[2]{0:T(128)S(1)} %pad_add_fusion.place, s32[384]{0:T(512)} %row_map.1, f32[384]{0:T(512)} %row_frac.1, ...), custom_call_target="tpu_custom_call" | custom-call | flops 5000000000 | bytes 8388608 | tf_op jit(solution)/shard_map/pallas_call | solution.py:502
  32.9 1.5 %collective-permute-start.4 = (bf16[192,128]{1,0:T(8,128)(2,1)S(1)}, bf16[192,128]{1,0:T(8,128)(2,1)S(1)}, u32[]{:S(2)}, u32[]{:S(2)}) collective-permute-start(bf16[192,128]{1,0:T(8,128)(2,1)S(1)} %get-tuple-element.50), channel_id=1, source_target_pairs={{0,32},{32,64},{64,96},{96,128},{128,160},{160,192},{192,224},{224... | collective-permute-start | bytes 147464 | tf_op jit(solution)/shard_map/ppermute | solution.py:531
  34.5 2.4 %collective-permute-start.5 = (bf16[192,128]{1,0:T(8,128)(2,1)S(1)}, bf16[192,128]{1,0:T(8,128)(2,1)S(1)}, u32[]{:S(2)}, u32[]{:S(2)}) collective-permute-start(bf16[192,128]{1,0:T(8,128)(2,1)S(1)} %get-tuple-element.51), channel_id=1, source_target_pairs={{32,0},{64,32},{96,64},{128,96},{160,128},{192,160},{224,192},{0,2... | collective-permute-start | bytes 147464 | tf_op jit(solution)/shard_map/ppermute | solution.py:532
  36.9 1.5 %collective-permute-done.4.from_upper = bf16[192,128]{1,0:T(8,128)(2,1)S(1)} collective-permute-done((bf16[192,128]{1,0:T(8,128)(2,1)S(1)}, bf16[192,128]{1,0:T(8,128)(2,1)S(1)}, u32[]{:S(2)}, u32[]{:S(2)}) %collective-permute-start.4) | collective-permute-done | bytes 49184 | tf_op jit(solution)/shard_map/ppermute | solution.py:531
  38.3 0.6 collective-permute-done.5.from_lower
  38.9 0.1 shard_map.185
  39.0 2.2 %collective-permute-start.6 = (bf16[192,128]{1,0:T(8,128)(2,1)S(1)}, bf16[192,128]{1,0:T(8,128)(2,1)S(1)}, u32[]{:S(2)}, u32[]{:S(2)}) collective-permute-start(bf16[192,128]{1,0:T(8,128)(2,1)S(1)} %get-tuple-element.53), channel_id=1, source_target_pairs={{0,1},{1,2},{2,3},{3,4},{4,5},{5,6},{6,7},{7,8},{8,9},{9,10},{10,1... | collective-permute-start | bytes 147464 | tf_op jit(solution)/shard_map/ppermute | solution.py:531
  41.2 0.0 collective-permute-start.7
  41.2 1.2 %collective-permute-done.6.from_left = bf16[192,128]{1,0:T(8,128)(2,1)S(1)} collective-permute-done((bf16[192,128]{1,0:T(8,128)(2,1)S(1)}, bf16[192,128]{1,0:T(8,128)(2,1)S(1)}, u32[]{:S(2)}, u32[]{:S(2)}) %collective-permute-start.6) | collective-permute-done | bytes 49184 | tf_op jit(solution)/shard_map/ppermute | solution.py:531
  42.4 4.4 %collective-permute-done.7.from_right = bf16[192,128]{1,0:T(8,128)(2,1)S(1)} collective-permute-done((bf16[192,128]{1,0:T(8,128)(2,1)S(1)}, bf16[192,128]{1,0:T(8,128)(2,1)S(1)}, u32[]{:S(2)}, u32[]{:S(2)}) %collective-permute-start.7) | collective-permute-done | bytes 49184 | tf_op jit(solution)/shard_map/ppermute | solution.py:532
  46.8 11.9 %shard_map.186 = (f32[384,128]{1,0:T(8,128)S(1)}, bf16[96,128]{1,0:T(8,128)(2,1)S(1)}, bf16[96,128]{1,0:T(8,128)(2,1)S(1)}, f32[384,128]{1,0:T(8,128)S(1)}) custom-call(s32[2]{0:T(128)S(1)} %pad_add_fusion.place, f32[384,128]{1,0:T(8,128)S(1)} %get-tuple-element.52.total, bf16[192,128]{1,0:T(8,128)(2,1)S(1)} %collective-permute-done.6.from_left, ...), custom_call_target="tpu_custom_call" | custom-call | flops 5000000000 | bytes 8388608 | tf_op jit(solution)/shard_map/pallas_call | solution.py:502
  58.7 2.3 %collective-permute-start.8 = (bf16[96,128]{1,0:T(8,128)(2,1)S(1)}, bf16[96,128]{1,0:T(8,128)(2,1)S(1)}, u32[]{:S(2)}, u32[]{:S(2)}) collective-permute-start(bf16[96,128]{1,0:T(8,128)(2,1)S(1)} %get-tuple-element.59), channel_id=1, source_target_pairs={{0,32},{32,64},{64,96},{96,128},{128,160},{160,192},{192,224},{224... | collective-permute-start | bytes 73736 | tf_op jit(solution)/shard_map/ppermute | solution.py:531
  61.1 1.6 %collective-permute-start.9 = (bf16[96,128]{1,0:T(8,128)(2,1)S(1)}, bf16[96,128]{1,0:T(8,128)(2,1)S(1)}, u32[]{:S(2)}, u32[]{:S(2)}) collective-permute-start(bf16[96,128]{1,0:T(8,128)(2,1)S(1)} %get-tuple-element.60), channel_id=1, source_target_pairs={{32,0},{64,32},{96,64},{128,96},{160,128},{192,160},{224,192},{0,2... | collective-permute-start | bytes 73736 | tf_op jit(solution)/shard_map/ppermute | solution.py:532
  62.7 1.2 %collective-permute-done.8.from_upper = bf16[96,128]{1,0:T(8,128)(2,1)S(1)} collective-permute-done((bf16[96,128]{1,0:T(8,128)(2,1)S(1)}, bf16[96,128]{1,0:T(8,128)(2,1)S(1)}, u32[]{:S(2)}, u32[]{:S(2)}) %collective-permute-start.8) | collective-permute-done | bytes 24608 | tf_op jit(solution)/shard_map/ppermute | solution.py:531
  63.9 1.4 %collective-permute-done.9.from_lower = bf16[96,128]{1,0:T(8,128)(2,1)S(1)} collective-permute-done((bf16[96,128]{1,0:T(8,128)(2,1)S(1)}, bf16[96,128]{1,0:T(8,128)(2,1)S(1)}, u32[]{:S(2)}, u32[]{:S(2)}) %collective-permute-start.9) | collective-permute-done | bytes 24608 | tf_op jit(solution)/shard_map/ppermute | solution.py:532
  65.3 0.1 shard_map.187
  65.4 2.1 %collective-permute-start.10 = (bf16[96,128]{1,0:T(8,128)(2,1)S(1)}, bf16[96,128]{1,0:T(8,128)(2,1)S(1)}, u32[]{:S(2)}, u32[]{:S(2)}) collective-permute-start(bf16[96,128]{1,0:T(8,128)(2,1)S(1)} %get-tuple-element.62), channel_id=1, source_target_pairs={{0,1},{1,2},{2,3},{3,4},{4,5},{5,6},{6,7},{7,8},{8,9},{9,10},{10,1... | collective-permute-start | bytes 73736 | tf_op jit(solution)/shard_map/ppermute | solution.py:531
  67.5 0.0 collective-permute-start.11
  67.5 0.9 %collective-permute-done.10.from_left = bf16[96,128]{1,0:T(8,128)(2,1)S(1)} collective-permute-done((bf16[96,128]{1,0:T(8,128)(2,1)S(1)}, bf16[96,128]{1,0:T(8,128)(2,1)S(1)}, u32[]{:S(2)}, u32[]{:S(2)}) %collective-permute-start.10) | collective-permute-done | bytes 24608 | tf_op jit(solution)/shard_map/ppermute | solution.py:531
  68.4 4.4 %collective-permute-done.11.from_right = bf16[96,128]{1,0:T(8,128)(2,1)S(1)} collective-permute-done((bf16[96,128]{1,0:T(8,128)(2,1)S(1)}, bf16[96,128]{1,0:T(8,128)(2,1)S(1)}, u32[]{:S(2)}, u32[]{:S(2)}) %collective-permute-start.11) | collective-permute-done | bytes 24608 | tf_op jit(solution)/shard_map/ppermute | solution.py:532
  72.8 0.8 %shard_map.188 = f32[4,48,80]{2,1,0:T(8,128)} custom-call(f32[192,128]{1,0:T(8,128)S(1)} %get-tuple-element.61.total, bf16[96,128]{1,0:T(8,128)(2,1)S(1)} %collective-permute-done.10.from_left, bf16[96,128]{1,0:T(8,128)(2,1)S(1)} %collective-permute-done.11.from_right, f32[384,128]{1,0:T(8,128)S(1)} %get-tuple-element.64.raised), custom_call_target="tpu_custom_call" | custom-call | tf_op jit(solution)/shard_map/pallas_call | solution.py:502
Async XLA Ops:
  1.0 6.3 %collective-permute-start = (bf16[192,128]{1,0:T(8,128)(2,1)S(1)}, bf16[192,128]{1,0:T(8,128)(2,1)S(1)}, u32[]{:S(2)}, u32[]{:S(2)}) collective-permute-start(bf16[192,128]{1,0:T(8,128)(2,1)S(1)} %get-tuple-element.35), channel_id=1, source_target_pairs={{0,32},{32,64},{64,96},{96,128},{128,160},{160,192},{192,224},{224... | collective-permute-start | bytes 147464 | tf_op jit(solution)/shard_map/ppermute | solution.py:531
  3.1 5.0 %collective-permute-start.1 = (bf16[192,128]{1,0:T(8,128)(2,1)S(1)}, bf16[192,128]{1,0:T(8,128)(2,1)S(1)}, u32[]{:S(2)}, u32[]{:S(2)}) collective-permute-start(bf16[192,128]{1,0:T(8,128)(2,1)S(1)} %get-tuple-element.36), channel_id=1, source_target_pairs={{32,0},{64,32},{96,64},{128,96},{160,128},{192,160},{224,192},{0,2... | collective-permute-start | bytes 147464 | tf_op jit(solution)/shard_map/ppermute | solution.py:532
  8.4 6.6 %collective-permute-start.2 = (bf16[288,128]{1,0:T(8,128)(2,1)S(1)}, bf16[288,128]{1,0:T(8,128)(2,1)S(1)}, u32[]{:S(2)}, u32[]{:S(2)}) collective-permute-start(bf16[288,128]{1,0:T(8,128)(2,1)S(1)} %get-tuple-element.41), channel_id=1, source_target_pairs={{0,1},{1,2},{2,3},{3,4},{4,5},{5,6},{6,7},{7,8},{8,9},{9,10},{10,1... | collective-permute-start | bytes 221192 | tf_op jit(solution)/shard_map/ppermute | solution.py:531
  13.6 5.9 %collective-permute-start.3 = (bf16[288,128]{1,0:T(8,128)(2,1)S(1)}, bf16[288,128]{1,0:T(8,128)(2,1)S(1)}, u32[]{:S(2)}, u32[]{:S(2)}) collective-permute-start(bf16[288,128]{1,0:T(8,128)(2,1)S(1)} %get-tuple-element.42), channel_id=1, source_target_pairs={{1,0},{2,1},{3,2},{4,3},{5,4},{6,5},{7,6},{8,7},{9,8},{10,9},{11,1... | collective-permute-start | bytes 221192 | tf_op jit(solution)/shard_map/ppermute | solution.py:532
  32.9 5.4 %collective-permute-start.4 = (bf16[192,128]{1,0:T(8,128)(2,1)S(1)}, bf16[192,128]{1,0:T(8,128)(2,1)S(1)}, u32[]{:S(2)}, u32[]{:S(2)}) collective-permute-start(bf16[192,128]{1,0:T(8,128)(2,1)S(1)} %get-tuple-element.50), channel_id=1, source_target_pairs={{0,32},{32,64},{64,96},{96,128},{128,160},{160,192},{192,224},{224... | collective-permute-start | bytes 147464 | tf_op jit(solution)/shard_map/ppermute | solution.py:531
  34.5 4.4 %collective-permute-start.5 = (bf16[192,128]{1,0:T(8,128)(2,1)S(1)}, bf16[192,128]{1,0:T(8,128)(2,1)S(1)}, u32[]{:S(2)}, u32[]{:S(2)}) collective-permute-start(bf16[192,128]{1,0:T(8,128)(2,1)S(1)} %get-tuple-element.51), channel_id=1, source_target_pairs={{32,0},{64,32},{96,64},{128,96},{160,128},{192,160},{224,192},{0,2... | collective-permute-start | bytes 147464 | tf_op jit(solution)/shard_map/ppermute | solution.py:532
  39.0 3.3 %collective-permute-start.6 = (bf16[192,128]{1,0:T(8,128)(2,1)S(1)}, bf16[192,128]{1,0:T(8,128)(2,1)S(1)}, u32[]{:S(2)}, u32[]{:S(2)}) collective-permute-start(bf16[192,128]{1,0:T(8,128)(2,1)S(1)} %get-tuple-element.53), channel_id=1, source_target_pairs={{0,1},{1,2},{2,3},{3,4},{4,5},{5,6},{6,7},{7,8},{8,9},{9,10},{10,1... | collective-permute-start | bytes 147464 | tf_op jit(solution)/shard_map/ppermute | solution.py:531
  41.2 5.6 %collective-permute-start.7 = (bf16[192,128]{1,0:T(8,128)(2,1)S(1)}, bf16[192,128]{1,0:T(8,128)(2,1)S(1)}, u32[]{:S(2)}, u32[]{:S(2)}) collective-permute-start(bf16[192,128]{1,0:T(8,128)(2,1)S(1)} %get-tuple-element.54), channel_id=1, source_target_pairs={{1,0},{2,1},{3,2},{4,3},{5,4},{6,5},{7,6},{8,7},{9,8},{10,9},{11,1... | collective-permute-start | bytes 147464 | tf_op jit(solution)/shard_map/ppermute | solution.py:532
  58.7 5.2 %collective-permute-start.8 = (bf16[96,128]{1,0:T(8,128)(2,1)S(1)}, bf16[96,128]{1,0:T(8,128)(2,1)S(1)}, u32[]{:S(2)}, u32[]{:S(2)}) collective-permute-start(bf16[96,128]{1,0:T(8,128)(2,1)S(1)} %get-tuple-element.59), channel_id=1, source_target_pairs={{0,32},{32,64},{64,96},{96,128},{128,160},{160,192},{192,224},{224... | collective-permute-start | bytes 73736 | tf_op jit(solution)/shard_map/ppermute | solution.py:531
  61.1 4.2 %collective-permute-start.9 = (bf16[96,128]{1,0:T(8,128)(2,1)S(1)}, bf16[96,128]{1,0:T(8,128)(2,1)S(1)}, u32[]{:S(2)}, u32[]{:S(2)}) collective-permute-start(bf16[96,128]{1,0:T(8,128)(2,1)S(1)} %get-tuple-element.60), channel_id=1, source_target_pairs={{32,0},{64,32},{96,64},{128,96},{160,128},{192,160},{224,192},{0,2... | collective-permute-start | bytes 73736 | tf_op jit(solution)/shard_map/ppermute | solution.py:532
  65.4 3.1 %collective-permute-start.10 = (bf16[96,128]{1,0:T(8,128)(2,1)S(1)}, bf16[96,128]{1,0:T(8,128)(2,1)S(1)}, u32[]{:S(2)}, u32[]{:S(2)}) collective-permute-start(bf16[96,128]{1,0:T(8,128)(2,1)S(1)} %get-tuple-element.62), channel_id=1, source_target_pairs={{0,1},{1,2},{2,3},{3,4},{4,5},{5,6},{6,7},{7,8},{8,9},{9,10},{10,1... | collective-permute-start | bytes 73736 | tf_op jit(solution)/shard_map/ppermute | solution.py:531
  67.5 5.4 %collective-permute-start.11 = (bf16[96,128]{1,0:T(8,128)(2,1)S(1)}, bf16[96,128]{1,0:T(8,128)(2,1)S(1)}, u32[]{:S(2)}, u32[]{:S(2)}) collective-permute-start(bf16[96,128]{1,0:T(8,128)(2,1)S(1)} %get-tuple-element.63), channel_id=1, source_target_pairs={{1,0},{2,1},{3,2},{4,3},{5,4},{6,5},{7,6},{8,7},{9,8},{10,9},{11,1... | collective-permute-start | bytes 73736 | tf_op jit(solution)/shard_map/ppermute | solution.py:532

commit v3 on v2

--- a/solution.py
+++ b/solution.py
@@ -14,7 +14,7 @@
 CH = 128
 ROWS = 4 * PATCH_ROWS
 PAIRS = PATCH_ROWS // 2
-FIRST_BATCH, LAST_BATCH = 16, 24
+FIRST_BATCH, LAST_BATCH = 48, 48
 LEVEL1_BATCH, COND_BATCH = 12, 8
 SIDE = 16
 COARSE_SLOTS = 48
@@ -89,15 +89,31 @@
     return lax.broadcasted_iota(jnp.int32, shape, 1)
 
 
+def choose(flags, first, second):
+    return jnp.where(flags[2:3, :] > 0.5, first, second)
+
+
 def roll_lanes(value, amount):
     amount = amount % 128
     return value if amount == 0 else pltpu.roll(value, amount, 1)
 
 
 def prepare_kernel(
-    w_state, w_cond, w_expand, w_project, w_levels, w_final, picks,
-    first_w, expand_w, project_w, level_w, last_level_w, final_w, flat_final,
+    w_state, w_cond, w_expand, w_project, w_levels, w_final, picks, shifts, back, mean_w, pool, grow, col_map, col_frac,
+    first_w, expand_w, project_w, level_w, last_level_w, final_w,
+    own_shifts, own_back, own_mean_w, own_pool, own_grow, own_col_map, own_col_frac, flags, flat_final,
 ):
+    for source, target in (
+        (shifts, own_shifts), (back, own_back), (mean_w, own_mean_w), (pool, own_pool), (grow, own_grow),
+        (col_map, own_col_map), (col_frac, own_col_frac),
+    ):
+        target[...] = source[...]
+    lat, lon = lax.axis_index("lat"), lax.axis_index("lon")
+    row = lax.broadcasted_iota(jnp.int32, (8, 128), 0)
+    above = jnp.where(lat > 0, 0.5, 0.0)
+    below = jnp.where(lat < 7, 0.5, 0.0)
+    odd = jnp.where(lon % 2 == 1, 1.0, 0.0)
+    flags[...] = jnp.where(row == 0, above, jnp.where(row == 1, below, odd))
     unit = picks[352:480, :]
     for k in range(9):
         flat_final[4 * k : 4 * k + 4, :] = w_final[k].astype(F32)
@@ -145,7 +161,7 @@
             target[which * 96 : which * 96 + 96, :] = part.astype(BF16)
 
 
-def pack_cols_kernel(from_upper, from_lower, own, own_coarse, to_left, to_right, strip, coarse_strip):
+def pack_cols_kernel(flags, from_upper, from_lower, own, own_coarse, to_far, to_near, strip, coarse_strip):
     lane = lanes((192, 128))
     for which in range(2):
         rows = slice(which * 96, which * 96 + 96)
@@ -160,8 +176,8 @@
         inside = (lane >= 32 * group) & (lane < 32 * group + 32)
         left = for_left if group == 0 else jnp.where(inside, for_left, left)
         right = for_right if group == 0 else jnp.where(inside, for_right, right)
-    to_left[0:192, :] = left.astype(BF16)
-    to_right[0:192, :] = right.astype(BF16)
+    to_near[0:192, :] = choose(flags, left, right).astype(BF16)
+    to_far[0:192, :] = choose(flags, right, left).astype(BF16)
     narrow = lanes((96, 128))
     above = roll_lanes(from_upper[0:96, :].astype(F32), -80)
     middle = own_coarse[...]
@@ -169,8 +185,8 @@
     for index, part in enumerate((above, middle, below)):
         coarse_strip[index * 96 : index * 96 + 96, :] = jnp.where(narrow < 40, part, 0.0)
     packed = jnp.where(narrow < 40, above, jnp.where(narrow < 80, roll_lanes(middle, 40), roll_lanes(below, 80)))
-    to_left[192:288, :] = packed.astype(BF16)
-    to_right[192:288, :] = packed.astype(BF16)
+    to_near[192:288, :] = packed.astype(BF16)
+    to_far[192:288, :] = packed.astype(BF16)
 
 
 def pad_store(target, row, pooled, groups):
@@ -324,16 +340,16 @@
     out[...] = skip_scale * state[...] + out_scale * refined
 
 
-def inside_rows(lat):
+def inside_rows(flags):
     row = lax.broadcasted_iota(jnp.int32, (ROWS, 128), 0)
-    first = jnp.where(lat == 0, 4 * MARGIN, 0)
-    last = jnp.where(lat == 7, ROWS - 4 * MARGIN, ROWS)
-    return (row >= first) & (row < last)
-
-
-def send_rows(lat, den, to_upper, to_lower, count):
-    above = jnp.where(lat > 0, 0.5, 0.0)
-    below = jnp.where(lat < 7, 0.5, 0.0)
+    outside = ((row < 4 * MARGIN) & (flags[0:1, :] < 0.25)) | (
+        (row >= ROWS - 4 * MARGIN) & (flags[1:2, :] < 0.25)
+    )
+    return jnp.logical_not(outside)
+
+
+def send_rows(flags, den, to_upper, to_lower, count):
+    above, below = flags[0:1, :], flags[1:2, :]
     to_upper[...] = (above * den[0:count, :]).astype(BF16)
     to_lower[...] = (below * den[ROWS - count : ROWS, :]).astype(BF16)
     half = ROWS // 2
@@ -342,20 +358,22 @@
 
 
 def first_kernel(
-    place, row_map, row_frac, col_map, col_frac, strip, coarse_strip, from_left, from_right,
+    row_map, row_frac, flags, col_map, col_frac, strip, coarse_strip, from_far, from_near,
     first_w, expand_w, project_w, level_w, last_level_w, final_w, shifts, back, mean_w, pool, grow,
     den, to_upper, to_lower, state, churn, cond_rows,
     window, coarse_t, *scratch,
 ):
-    lat, lon = place[0], place[1]
+    lat, lon = lax.axis_index("lat"), lax.axis_index("lon")
     lane = lanes((192, 128))
-    inside = inside_rows(lat)
+    inside = inside_rows(flags)
+    near, far = from_near[...].astype(F32), from_far[...].astype(F32)
+    from_left, from_right = choose(flags, near, far), choose(flags, far, near)
     for which, target in enumerate((state, churn)):
         for part in range(2):
             group = 2 * which + part
             rows = slice(part * 192, part * 192 + 192)
-            left = roll_lanes(from_left[0:192, :].astype(F32), -32 * group)
-            right = roll_lanes(from_right[0:192, :].astype(F32), 104 - 32 * group)
+            left = roll_lanes(from_left[0:192, :], -32 * group)
+            right = roll_lanes(from_right[0:192, :], 104 - 32 * group)
             target[rows, :] = jnp.where(lane < 24, left, jnp.where(lane < 104, strip[which, rows, :], right))
     state[...] = jnp.where(inside, level_first * state[...], 0.0)
 
@@ -365,7 +383,7 @@
             if source is None:
                 rows = coarse_strip[part * 96 : part * 96 + 96, :]
             else:
-                rows = roll_lanes(source[192:288, :].astype(F32), -40 * part)
+                rows = roll_lanes(source[192:288, :], -40 * part)
             for j in range(6):
                 window[part * 6 + j, t * 16 : t * 16 + 16, :] = rows[j * 16 : j * 16 + 16]
     unit = jnp.where(
@@ -418,31 +436,32 @@
         state, cond_rows, (first_w, expand_w, project_w, level_w, last_level_w, final_w),
         (shifts, back, mean_w, pool, grow), scratch, level_first, den,
     )
-    send_rows(lat, den, to_upper, to_lower, 192)
-
-
-def add_rows_kernel(den, from_upper, from_lower, total, to_left, to_right):
+    send_rows(flags, den, to_upper, to_lower, 192)
+
+
+def add_rows_kernel(flags, den, from_upper, from_lower, total, to_far, to_near):
     top = den[0:192, :] + from_upper[...].astype(F32)
     bottom = den[192:384, :] + from_lower[...].astype(F32)
     total[0:192, :] = top
     total[192:384, :] = bottom
     lane = lanes((192, 128))
-    to_left[...] = jnp.where(lane < 64, top, roll_lanes(bottom, 64)).astype(BF16)
-    to_right[...] = jnp.where(lane < 64, roll_lanes(top, -80), roll_lanes(bottom, 64 - 80)).astype(BF16)
+    left = jnp.where(lane < 64, top, roll_lanes(bottom, 64))
+    right = jnp.where(lane < 64, roll_lanes(top, -80), roll_lanes(bottom, 64 - 80))
+    to_near[...] = choose(flags, left, right).astype(BF16)
+    to_far[...] = choose(flags, right, left).astype(BF16)
 
 
 def second_kernel(
-    place, total, from_left, from_right, state, churn, cond_rows,
+    flags, total, from_far, from_near, state, churn, cond_rows,
     first_w, expand_w, project_w, level_w, last_level_w, final_w, shifts, back, mean_w, pool, grow,
     den, to_upper, to_lower, raised,
     *scratch,
 ):
-    lat = place[0]
     lane = lanes((192, 128))
     edge = (lane < 48) | (lane >= 80)
-    left = from_left[...].astype(F32)
-    right = from_right[...].astype(F32)
-    inside = inside_rows(lat)
+    near, far = from_near[...].astype(F32), from_far[...].astype(F32)
+    left, right = choose(flags, near, far), choose(flags, far, near)
+    inside = inside_rows(flags)
     for part in range(2):
         rows = slice(part * 192, part * 192 + 192)
         from_l = roll_lanes(left, -64 * part)
@@ -458,24 +477,26 @@
         raised, cond_rows, (first_w, expand_w, project_w, level_w, last_level_w, final_w),
         (shifts, back, mean_w, pool, grow), scratch, level_raised, den,
     )
-    send_rows(lat, den, to_upper, to_lower, 96)
-
-
-def add_tile_rows_kernel(den, from_upper, from_lower, total, to_left, to_right):
+    send_rows(flags, den, to_upper, to_lower, 96)
+
+
+def add_tile_rows_kernel(flags, den, from_upper, from_lower, total, to_far, to_near):
     top = den[96:192, :] + from_upper[...].astype(F32)
     bottom = den[192:288, :] + from_lower[...].astype(F32)
     total[0:96, :] = top
     total[96:192, :] = bottom
     lane = lanes((96, 128))
-    to_left[...] = jnp.where(lane < 64, top, roll_lanes(bottom, 64)).astype(BF16)
-    to_right[...] = jnp.where(lane < 64, roll_lanes(top, -104), roll_lanes(bottom, 64 - 104)).astype(BF16)
-
-
-def finish_kernel(total, from_left, from_right, raised, out, rows_ref):
+    left = jnp.where(lane < 64, top, roll_lanes(bottom, 64))
+    right = jnp.where(lane < 64, roll_lanes(top, -104), roll_lanes(bottom, 64 - 104))
+    to_near[...] = choose(flags, left, right).astype(BF16)
+    to_far[...] = choose(flags, right, left).astype(BF16)
+
+
+def finish_kernel(flags, total, from_far, from_near, raised, out, rows_ref):
     lane = lanes((96, 128))
     edge = (lane < 48) | (lane >= 80)
-    left = from_left[...].astype(F32)
-    right = from_right[...].astype(F32)
+    near, far = from_near[...].astype(F32), from_far[...].astype(F32)
+    left, right = choose(flags, near, far), choose(flags, far, near)
     for part in range(2):
         rows = slice(part * 96, part * 96 + 96)
         from_l = roll_lanes(left, 24 - 64 * part)
@@ -515,22 +536,18 @@
     coarse, row_map, row_frac, col_map, col_frac, noise_init, noise_churn,
     w_state, w_cond, w_expand, w_project, w_levels, w_final,
 ):
-    lat_index = lax.axis_index("lat")
-    lon_index = lax.axis_index("lon")
-    place = jnp.stack([lat_index, lon_index]).astype(jnp.int32)
-    rings = {}
-    for axis in ("lat", "lon"):
-        size = lax.axis_size(axis)
-        rings[axis] = (
-            [((i + 1) % size, i) for i in range(size)],
-            [(i, (i + 1) % size) for i in range(size)],
-        )
-
-    def swap(axis, to_before, to_after):
-        down, up = rings[axis]
-        from_before = lax.ppermute(to_after, axis, up)
-        from_after = lax.ppermute(to_before, axis, down)
-        return from_before, from_after
+    lats, lons = lax.axis_size("lat"), lax.axis_size("lon")
+    up = [(i, (i + 1) % lats) for i in range(lats)]
+    down = [((i + 1) % lats, i) for i in range(lats)]
+    near = [(i, i ^ 1) for i in range(lons)]
+    far = [(i, (i + 2 * (i % 2) - 1) % lons) for i in range(lons)]
+
+    def swap_rows(to_upper, to_lower):
+        return lax.ppermute(to_lower, "lat", up), lax.ppermute(to_upper, "lat", down)
+
+    def swap_cols(to_near, to_far):
+        from_far = lax.ppermute(to_far, "lon", far)
+        return from_far, lax.ppermute(to_near, "lon", near)
 
     msg = shape((192, 128), BF16)
     to_upper, to_lower, own, own_coarse = call(
@@ -540,76 +557,77 @@
         [pltpu.VMEM((2, 192, 128), F32)],
         far=(0, 1, 2),
     )
-    from_upper, from_lower = swap("lat", to_upper, to_lower)
-    wide_msg = shape((288, 128), BF16)
-    to_left, to_right, strip, coarse_strip = call(
-        pack_cols_kernel,
-        (from_upper, from_lower, own, own_coarse),
-        [wide_msg, wide_msg, shape((2, ROWS, 128), F32), shape((288, 128), F32)],
-    )
-    from_left, from_right = swap("lon", to_left, to_right)
-
-    weights = call(
+    from_upper, from_lower = swap_rows(to_upper, to_lower)
+    mean_w = np.zeros((256, 256), np.float32)
+    mean_w[:128, :128] = mean_w[128:, 128:] = 4.0 / 128.0
+    constants = [jnp.asarray(c, BF16) for c in (SHIFTS, BACK, mean_w, POOL, GROW)]
+    prepared = call(
         prepare_kernel,
         (
-            w_state.T, w_cond.T, w_expand, w_project, w_levels, w_final, jnp.asarray(PICKS, BF16),
+            w_state.T, w_cond.T, w_expand, w_project, w_levels, w_final, jnp.asarray(PICKS, BF16), *constants, col_map.reshape(20, 128), col_frac.reshape(20, 128),
         ),
         [
             shape((128, 256), BF16), shape((256, 256), BF16), shape((256, 256), BF16),
             shape((3, 1536, 256), BF16), shape((1152, 128), BF16), shape((48, 256), BF16),
+            *[shape(c.shape, BF16) for c in constants],
+            shape((20, 128), jnp.int32), shape((20, 128), F32), shape((8, 128), F32),
         ],
         [pltpu.VMEM((36, 128), F32)],
         cost=(2 * 36 * 128**3, 4 << 20, 0),
-        far=range(7),
-    )
-    mean_w = np.zeros((256, 256), np.float32)
-    mean_w[:128, :128] = mean_w[128:, 128:] = 4.0 / 128.0
-    constants = [jnp.asarray(c, BF16) for c in (SHIFTS, BACK, mean_w, POOL, GROW)]
+        far=range(14),
+    )
+    weights, constants, (col_map, col_frac, flags) = prepared[:6], prepared[6:11], prepared[11:]
+    wide_msg = shape((288, 128), BF16)
+    to_far, to_near, strip, coarse_strip = call(
+        pack_cols_kernel,
+        (flags, from_upper, from_lower, own, own_coarse),
+        [wide_msg, wide_msg, shape((2, ROWS, 128), F32), shape((288, 128), F32)],
+    )
+    from_far, from_near = swap_cols(to_near, to_far)
+
     field = shape((ROWS, 128), F32)
     cost = (5 * 10**9, 8 << 20, 3 * 10**6)
     den, to_upper, to_lower, state, churn, cond_rows = call(
         first_kernel,
         (
-            place, row_map, row_frac, col_map.reshape(20, 128), col_frac.reshape(20, 128),
-            strip, coarse_strip, from_left, from_right, *weights, *constants,
+            row_map, row_frac, flags, col_map, col_frac,
+            strip, coarse_strip, from_far, from_near, *weights, *constants,
         ),
         [
             field, msg, msg, field, field,
             shape((PAIRS, 80, 128), BF16),
         ],
         [pltpu.VMEM((18, COARSE_SLOTS, 128), F32), pltpu.VMEM((18, 40, COARSE_SLOTS), F32)] + CORE_SCRATCH,
-        scalars=3,
+        scalars=2,
         cost=cost,
-        far=(1, 2, 3, 4, 15, 16, 17, 18, 19),
-    )
-    from_upper, from_lower = swap("lat", to_upper, to_lower)
-    total, to_left, to_right = call(
-        add_rows_kernel, (den, from_upper, from_lower), [field, msg, msg]
-    )
-    from_left, from_right = swap("lon", to_left, to_right)
+        far=(0, 1),
+    )
+    from_upper, from_lower = swap_rows(to_upper, to_lower)
+    total, to_far, to_near = call(
+        add_rows_kernel, (flags, den, from_upper, from_lower), [field, msg, msg]
+    )
+    from_far, from_near = swap_cols(to_near, to_far)
     short_msg = shape((96, 128), BF16)
     den, to_upper, to_lower, raised = call(
         second_kernel,
         (
-            place, total, from_left, from_right, state, churn, cond_rows,
+            flags, total, from_far, from_near, state, churn, cond_rows,
             *weights, *constants,
         ),
         [field, short_msg, short_msg, field],
         CORE_SCRATCH,
-        scalars=1,
         cost=cost,
-        far=(13, 14, 15, 16, 17),
-    )
-    from_upper, from_lower = swap("lat", to_upper, to_lower)
-    total, to_left, to_right = call(
+    )
+    from_upper, from_lower = swap_rows(to_upper, to_lower)
+    total, to_far, to_near = call(
         add_tile_rows_kernel,
-        (den, from_upper, from_lower),
+        (flags, den, from_upper, from_lower),
         [shape((192, 128), F32), short_msg, short_msg],
     )
-    from_left, from_right = swap("lon", to_left, to_right)
+    from_far, from_near = swap_cols(to_near, to_far)
     (final,) = call(
         finish_kernel,
-        (total, from_left, from_right, raised),
+        (flags, total, from_far, from_near, raised),
         [shape((4, TILE_ROWS, TILE_COLS), F32)],
         [pltpu.VMEM((192, 128), F32)],
     )

time: 73.9 us -> 69.2 us (0.936)
  the two profiles are of different devices: /device:TPU:111 before, /device:TPU:6 now
where the time goes in v3:
time: 69.2 us; the launch traced here: 69.1 us
  Pallas kernels  27.4 us (40%)
  starting transfers between devices  21.8 us (32%)
  waiting for transfers between devices  19.8 us (29%)
    pallas_call x8, Pallas kernels, call(): pl.pallas_call(kernel, out_shape=outs, in_specs=[pl.BlockSpec(memory_spac...  27.4 us
    ppermute x3, starting transfers between devices, swap_rows(): lax.ppermute(to_lower, 'lat', up)  10 us
    ppermute x3, waiting for transfers between devices, swap_cols(): from_far = lax.ppermute(to_far, 'lon', far)  9.66 us
    ppermute x3, starting transfers between devices, swap_cols(): from_far = lax.ppermute(to_far, 'lon', far)  8.12 us
    ppermute x3, waiting for transfers between devices, swap_rows(): lax.ppermute(to_upper, 'lat', down)  6.21 us
    ppermute x3, waiting for transfers between devices, swap_rows(): lax.ppermute(to_lower, 'lat', up)  3.88 us
    ppermute x3, starting transfers between devices, swap_rows(): lax.ppermute(to_upper, 'lat', down)  3.69 us
  transfers between devices with their start and end apart: 12, of which 8 were waited for; matrix products, arithmetic and copies ran while one was open for 0% of the time, Pallas kernels for 4%

profile of v3, /device:TPU:6, one launch (start us, length us, event | category | flops | bytes accessed | tf_op | source)
XLA Modules:
  0.0 69.1 jit_solution(11470625441225635479)
XLA Ops:
  0.0 1.0 %shard_map.182 = (bf16[192,128]{1,0:T(8,128)(2,1)S(1)}, bf16[192,128]{1,0:T(8,128)(2,1)S(1)}, f32[2,192,128]{2,1,0:T(8,128)S(1)}, f32[96,128]{1,0:T(8,128)S(1)}) custom-call(f32[4,48,80]{2,1,0:T(8,128)} %noise_init.1, f32[4,48,80]{2,1,0:T(8,128)} %noise_churn.1, bf16[10,6,40]{2,1,0:T(8,128)(2,1)} %bitcast.5), custom_call_target="tpu_custom_call" | custom-call | tf_op jit(solution)/shard_map/pallas_call | solution.py:523
  1.0 3.3 %collective-permute-start = (bf16[192,128]{1,0:T(8,128)(2,1)S(1)}, bf16[192,128]{1,0:T(8,128)(2,1)S(1)}, u32[]{:S(2)}, u32[]{:S(2)}) collective-permute-start(bf16[192,128]{1,0:T(8,128)(2,1)S(1)} %get-tuple-element.46), channel_id=1, source_target_pairs={{0,32},{32,64},{64,96},{96,128},{128,160},{160,192},{192,224},{224... | collective-permute-start | bytes 147464 | tf_op jit(solution)/shard_map/ppermute | solution.py:546
  4.3 1.2 %collective-permute-start.1 = (bf16[192,128]{1,0:T(8,128)(2,1)S(1)}, bf16[192,128]{1,0:T(8,128)(2,1)S(1)}, u32[]{:S(2)}, u32[]{:S(2)}) collective-permute-start(bf16[192,128]{1,0:T(8,128)(2,1)S(1)} %get-tuple-element.47), channel_id=1, source_target_pairs={{32,0},{64,32},{96,64},{128,96},{160,128},{192,160},{224,192},{0,2... | collective-permute-start | bytes 147464 | tf_op jit(solution)/shard_map/ppermute | solution.py:546
  5.6 2.7 %shard_map.181 = (bf16[128,256]{1,0:T(8,128)(2,1)S(1)}, bf16[256,256]{1,0:T(8,128)(2,1)S(1)}, bf16[256,256]{1,0:T(8,128)(2,1)S(1)}, bf16[3,1536,256]{2,1,0:T(8,1...) custom-call(bf16[36,128]{1,0:T(8,128)(2,1)} %bitcast.8, ...), custom_call_target="tpu_custom_call" | custom-call | flops 150994944 | bytes 4194304 | tf_op jit(solution)/shard_map/pallas_call | solution.py:523
  8.3 0.0 collective-permute-done.from_upper
  8.3 1.6 %collective-permute-done.1.from_lower = bf16[192,128]{1,0:T(8,128)(2,1)S(1)} collective-permute-done((bf16[192,128]{1,0:T(8,128)(2,1)S(1)}, bf16[192,128]{1,0:T(8,128)(2,1)S(1)}, u32[]{:S(2)}, u32[]{:S(2)}) %collective-permute-start.1) | collective-permute-done | bytes 49184 | tf_op jit(solution)/shard_map/ppermute | solution.py:546
  9.9 0.3 shard_map.183
  10.2 4.6 %collective-permute-start.2 = (bf16[288,128]{1,0:T(8,128)(2,1)S(1)}, bf16[288,128]{1,0:T(8,128)(2,1)S(1)}, u32[]{:S(2)}, u32[]{:S(2)}) collective-permute-start(bf16[288,128]{1,0:T(8,128)(2,1)S(1)} %get-tuple-element.52), channel_id=1, source_target_pairs={{0,31},{1,2},{2,1},{3,4},{4,3},{5,6},{6,5},{7,8},{8,7},{9,10},{10,... | collective-permute-start | bytes 221192 | tf_op jit(solution)/shard_map/ppermute | solution.py:549
  14.8 0.0 collective-permute-start.3
  14.8 2.0 %collective-permute-done.2.from_far = bf16[288,128]{1,0:T(8,128)(2,1)S(1)} collective-permute-done((bf16[288,128]{1,0:T(8,128)(2,1)S(1)}, bf16[288,128]{1,0:T(8,128)(2,1)S(1)}, u32[]{:S(2)}, u32[]{:S(2)}) %collective-permute-start.2) | collective-permute-done | bytes 73760 | tf_op jit(solution)/shard_map/ppermute | solution.py:549
  16.9 0.0 collective-permute-done.3.from_near
  16.9 12.2 %shard_map.184 = (f32[384,128]{1,0:T(8,128)S(1)}, bf16[192,128]{1,0:T(8,128)(2,1)S(1)}, bf16[192,128]{1,0:T(8,128)(2,1)S(1)}, f32[384,128]{1,0:T(8,128)S(1)}, f3...) custom-call(s32[384]{0:T(512)} %row_map.1, f32[384]{0:T(512)} %row_frac.1, f32[8,128]{1,0:T(8,128)S(1)} %get-tuple-element.43.flags, ...), custom_call_target="tpu_custom_call" | custom-call | flops 5000000000 | bytes 8388608 | tf_op jit(solution)/shard_map/pallas_call | solution.py:523
  29.1 3.7 %collective-permute-start.4 = (bf16[192,128]{1,0:T(8,128)(2,1)S(1)}, bf16[192,128]{1,0:T(8,128)(2,1)S(1)}, u32[]{:S(2)}, u32[]{:S(2)}) collective-permute-start(bf16[192,128]{1,0:T(8,128)(2,1)S(1)} %get-tuple-element.66), channel_id=1, source_target_pairs={{0,32},{32,64},{64,96},{96,128},{128,160},{160,192},{192,224},{224... | collective-permute-start | bytes 147464 | tf_op jit(solution)/shard_map/ppermute | solution.py:546
  32.8 1.0 %collective-permute-start.5 = (bf16[192,128]{1,0:T(8,128)(2,1)S(1)}, bf16[192,128]{1,0:T(8,128)(2,1)S(1)}, u32[]{:S(2)}, u32[]{:S(2)}) collective-permute-start(bf16[192,128]{1,0:T(8,128)(2,1)S(1)} %get-tuple-element.67), channel_id=1, source_target_pairs={{32,0},{64,32},{96,64},{128,96},{160,128},{192,160},{224,192},{0,2... | collective-permute-start | bytes 147464 | tf_op jit(solution)/shard_map/ppermute | solution.py:546
  33.8 2.1 %collective-permute-done.4.from_upper = bf16[192,128]{1,0:T(8,128)(2,1)S(1)} collective-permute-done((bf16[192,128]{1,0:T(8,128)(2,1)S(1)}, bf16[192,128]{1,0:T(8,128)(2,1)S(1)}, u32[]{:S(2)}, u32[]{:S(2)}) %collective-permute-start.4) | collective-permute-done | bytes 49184 | tf_op jit(solution)/shard_map/ppermute | solution.py:546
  35.9 2.5 %collective-permute-done.5.from_lower = bf16[192,128]{1,0:T(8,128)(2,1)S(1)} collective-permute-done((bf16[192,128]{1,0:T(8,128)(2,1)S(1)}, bf16[192,128]{1,0:T(8,128)(2,1)S(1)}, u32[]{:S(2)}, u32[]{:S(2)}) %collective-permute-start.5) | collective-permute-done | bytes 49184 | tf_op jit(solution)/shard_map/ppermute | solution.py:546
  38.4 0.1 shard_map.185
  38.5 1.9 %collective-permute-start.6 = (bf16[192,128]{1,0:T(8,128)(2,1)S(1)}, bf16[192,128]{1,0:T(8,128)(2,1)S(1)}, u32[]{:S(2)}, u32[]{:S(2)}) collective-permute-start(bf16[192,128]{1,0:T(8,128)(2,1)S(1)} %get-tuple-element.69), channel_id=1, source_target_pairs={{0,31},{1,2},{2,1},{3,4},{4,3},{5,6},{6,5},{7,8},{8,7},{9,10},{10,... | collective-permute-start | bytes 147464 | tf_op jit(solution)/shard_map/ppermute | solution.py:549
  40.4 0.0 collective-permute-start.7
  40.4 3.8 %collective-permute-done.6.from_far = bf16[192,128]{1,0:T(8,128)(2,1)S(1)} collective-permute-done((bf16[192,128]{1,0:T(8,128)(2,1)S(1)}, bf16[192,128]{1,0:T(8,128)(2,1)S(1)}, u32[]{:S(2)}, u32[]{:S(2)}) %collective-permute-start.6) | collective-permute-done | bytes 49184 | tf_op jit(solution)/shard_map/ppermute | solution.py:549
  44.2 0.0 collective-permute-done.7.from_near
  44.2 10.1 %shard_map.186 = (f32[384,128]{1,0:T(8,128)S(1)}, bf16[96,128]{1,0:T(8,128)(2,1)S(1)}, bf16[96,128]{1,0:T(8,128)(2,1)S(1)}, f32[384,128]{1,0:T(8,128)S(1)}) custom-call(f32[8,128]{1,0:T(8,128)S(1)} %get-tuple-element.43.flags, f32[384,128]{1,0:T(8,128)S(1)} %get-tuple-element.68.total, bf16[192,128]{1,0:T(8,128)(2,1)S(1)} %collective-permute-done.6.from_far, ...), custom_call_target="tpu_custom_call" | custom-call | flops 5000000000 | bytes 8388608 | tf_op jit(solution)/shard_map/pallas_call | solution.py:523
  54.3 3.0 %collective-permute-start.8 = (bf16[96,128]{1,0:T(8,128)(2,1)S(1)}, bf16[96,128]{1,0:T(8,128)(2,1)S(1)}, u32[]{:S(2)}, u32[]{:S(2)}) collective-permute-start(bf16[96,128]{1,0:T(8,128)(2,1)S(1)} %get-tuple-element.75), channel_id=1, source_target_pairs={{0,32},{32,64},{64,96},{96,128},{128,160},{160,192},{192,224},{224... | collective-permute-start | bytes 73736 | tf_op jit(solution)/shard_map/ppermute | solution.py:546
  57.3 1.5 %collective-permute-start.9 = (bf16[96,128]{1,0:T(8,128)(2,1)S(1)}, bf16[96,128]{1,0:T(8,128)(2,1)S(1)}, u32[]{:S(2)}, u32[]{:S(2)}) collective-permute-start(bf16[96,128]{1,0:T(8,128)(2,1)S(1)} %get-tuple-element.76), channel_id=1, source_target_pairs={{32,0},{64,32},{96,64},{128,96},{160,128},{192,160},{224,192},{0,2... | collective-permute-start | bytes 73736 | tf_op jit(solution)/shard_map/ppermute | solution.py:546
  58.8 1.8 %collective-permute-done.8.from_upper = bf16[96,128]{1,0:T(8,128)(2,1)S(1)} collective-permute-done((bf16[96,128]{1,0:T(8,128)(2,1)S(1)}, bf16[96,128]{1,0:T(8,128)(2,1)S(1)}, u32[]{:S(2)}, u32[]{:S(2)}) %collective-permute-start.8) | collective-permute-done | bytes 24608 | tf_op jit(solution)/shard_map/ppermute | solution.py:546
  60.6 2.1 %collective-permute-done.9.from_lower = bf16[96,128]{1,0:T(8,128)(2,1)S(1)} collective-permute-done((bf16[96,128]{1,0:T(8,128)(2,1)S(1)}, bf16[96,128]{1,0:T(8,128)(2,1)S(1)}, u32[]{:S(2)}, u32[]{:S(2)}) %collective-permute-start.9) | collective-permute-done | bytes 24608 | tf_op jit(solution)/shard_map/ppermute | solution.py:546
  62.7 0.1 shard_map.187
  62.8 1.6 %collective-permute-start.10 = (bf16[96,128]{1,0:T(8,128)(2,1)S(1)}, bf16[96,128]{1,0:T(8,128)(2,1)S(1)}, u32[]{:S(2)}, u32[]{:S(2)}) collective-permute-start(bf16[96,128]{1,0:T(8,128)(2,1)S(1)} %get-tuple-element.78), channel_id=1, source_target_pairs={{0,31},{1,2},{2,1},{3,4},{4,3},{5,6},{6,5},{7,8},{8,7},{9,10},{10,... | collective-permute-start | bytes 73736 | tf_op jit(solution)/shard_map/ppermute | solution.py:549
  64.4 0.0 collective-permute-start.11
  64.4 3.8 %collective-permute-done.10.from_far = bf16[96,128]{1,0:T(8,128)(2,1)S(1)} collective-permute-done((bf16[96,128]{1,0:T(8,128)(2,1)S(1)}, bf16[96,128]{1,0:T(8,128)(2,1)S(1)}, u32[]{:S(2)}, u32[]{:S(2)}) %collective-permute-start.10) | collective-permute-done | bytes 24608 | tf_op jit(solution)/shard_map/ppermute | solution.py:549
  68.2 0.0 collective-permute-done.11.from_near
  68.2 0.8 %shard_map.188 = f32[4,48,80]{2,1,0:T(8,128)} custom-call(f32[8,128]{1,0:T(8,128)S(1)} %get-tuple-element.43.flags, f32[192,128]{1,0:T(8,128)S(1)} %get-tuple-element.77.total, bf16[96,128]{1,0:T(8,128)(2,1)S(1)} %collective-permute-done.10.from_far, bf16[96,128]{1,0:T(8,128)(2,1)S(1)} %collective-permute-done.11.from_near, ...), custom_call_target="tpu_custom_call" | custom-call | tf_op jit(solution)/shard_map/pallas_call | solution.py:523
Async XLA Ops:
  1.0 7.2 %collective-permute-start = (bf16[192,128]{1,0:T(8,128)(2,1)S(1)}, bf16[192,128]{1,0:T(8,128)(2,1)S(1)}, u32[]{:S(2)}, u32[]{:S(2)}) collective-permute-start(bf16[192,128]{1,0:T(8,128)(2,1)S(1)} %get-tuple-element.46), channel_id=1, source_target_pairs={{0,32},{32,64},{64,96},{96,128},{128,160},{160,192},{192,224},{224... | collective-permute-start | bytes 147464 | tf_op jit(solution)/shard_map/ppermute | solution.py:546
  4.3 5.6 %collective-permute-start.1 = (bf16[192,128]{1,0:T(8,128)(2,1)S(1)}, bf16[192,128]{1,0:T(8,128)(2,1)S(1)}, u32[]{:S(2)}, u32[]{:S(2)}) collective-permute-start(bf16[192,128]{1,0:T(8,128)(2,1)S(1)} %get-tuple-element.47), channel_id=1, source_target_pairs={{32,0},{64,32},{96,64},{128,96},{160,128},{192,160},{224,192},{0,2... | collective-permute-start | bytes 147464 | tf_op jit(solution)/shard_map/ppermute | solution.py:546
  10.2 6.6 %collective-permute-start.2 = (bf16[288,128]{1,0:T(8,128)(2,1)S(1)}, bf16[288,128]{1,0:T(8,128)(2,1)S(1)}, u32[]{:S(2)}, u32[]{:S(2)}) collective-permute-start(bf16[288,128]{1,0:T(8,128)(2,1)S(1)} %get-tuple-element.52), channel_id=1, source_target_pairs={{0,31},{1,2},{2,1},{3,4},{4,3},{5,6},{6,5},{7,8},{8,7},{9,10},{10,... | collective-permute-start | bytes 221192 | tf_op jit(solution)/shard_map/ppermute | solution.py:549
  14.8 2.0 %collective-permute-start.3 = (bf16[288,128]{1,0:T(8,128)(2,1)S(1)}, bf16[288,128]{1,0:T(8,128)(2,1)S(1)}, u32[]{:S(2)}, u32[]{:S(2)}) collective-permute-start(bf16[288,128]{1,0:T(8,128)(2,1)S(1)} %get-tuple-element.53), channel_id=1, source_target_pairs={{0,1},{1,0},{2,3},{3,2},{4,5},{5,4},{6,7},{7,6},{8,9},{9,8},{10,11... | collective-permute-start | bytes 221192 | tf_op jit(solution)/shard_map/ppermute | solution.py:550
  29.1 6.8 %collective-permute-start.4 = (bf16[192,128]{1,0:T(8,128)(2,1)S(1)}, bf16[192,128]{1,0:T(8,128)(2,1)S(1)}, u32[]{:S(2)}, u32[]{:S(2)}) collective-permute-start(bf16[192,128]{1,0:T(8,128)(2,1)S(1)} %get-tuple-element.66), channel_id=1, source_target_pairs={{0,32},{32,64},{64,96},{96,128},{128,160},{160,192},{192,224},{224... | collective-permute-start | bytes 147464 | tf_op jit(solution)/shard_map/ppermute | solution.py:546
  32.8 5.6 %collective-permute-start.5 = (bf16[192,128]{1,0:T(8,128)(2,1)S(1)}, bf16[192,128]{1,0:T(8,128)(2,1)S(1)}, u32[]{:S(2)}, u32[]{:S(2)}) collective-permute-start(bf16[192,128]{1,0:T(8,128)(2,1)S(1)} %get-tuple-element.67), channel_id=1, source_target_pairs={{32,0},{64,32},{96,64},{128,96},{160,128},{192,160},{224,192},{0,2... | collective-permute-start | bytes 147464 | tf_op jit(solution)/shard_map/ppermute | solution.py:546
  38.5 5.7 %collective-permute-start.6 = (bf16[192,128]{1,0:T(8,128)(2,1)S(1)}, bf16[192,128]{1,0:T(8,128)(2,1)S(1)}, u32[]{:S(2)}, u32[]{:S(2)}) collective-permute-start(bf16[192,128]{1,0:T(8,128)(2,1)S(1)} %get-tuple-element.69), channel_id=1, source_target_pairs={{0,31},{1,2},{2,1},{3,4},{4,3},{5,6},{6,5},{7,8},{8,7},{9,10},{10,... | collective-permute-start | bytes 147464 | tf_op jit(solution)/shard_map/ppermute | solution.py:549
  40.4 3.8 %collective-permute-start.7 = (bf16[192,128]{1,0:T(8,128)(2,1)S(1)}, bf16[192,128]{1,0:T(8,128)(2,1)S(1)}, u32[]{:S(2)}, u32[]{:S(2)}) collective-permute-start(bf16[192,128]{1,0:T(8,128)(2,1)S(1)} %get-tuple-element.70), channel_id=1, source_target_pairs={{0,1},{1,0},{2,3},{3,2},{4,5},{5,4},{6,7},{7,6},{8,9},{9,8},{10,11... | collective-permute-start | bytes 147464 | tf_op jit(solution)/shard_map/ppermute | solution.py:550
  54.3 6.3 %collective-permute-start.8 = (bf16[96,128]{1,0:T(8,128)(2,1)S(1)}, bf16[96,128]{1,0:T(8,128)(2,1)S(1)}, u32[]{:S(2)}, u32[]{:S(2)}) collective-permute-start(bf16[96,128]{1,0:T(8,128)(2,1)S(1)} %get-tuple-element.75), channel_id=1, source_target_pairs={{0,32},{32,64},{64,96},{96,128},{128,160},{160,192},{192,224},{224... | collective-permute-start | bytes 73736 | tf_op jit(solution)/shard_map/ppermute | solution.py:546
  57.3 5.3 %collective-permute-start.9 = (bf16[96,128]{1,0:T(8,128)(2,1)S(1)}, bf16[96,128]{1,0:T(8,128)(2,1)S(1)}, u32[]{:S(2)}, u32[]{:S(2)}) collective-permute-start(bf16[96,128]{1,0:T(8,128)(2,1)S(1)} %get-tuple-element.76), channel_id=1, source_target_pairs={{32,0},{64,32},{96,64},{128,96},{160,128},{192,160},{224,192},{0,2... | collective-permute-start | bytes 73736 | tf_op jit(solution)/shard_map/ppermute | solution.py:546
  62.8 5.4 %collective-permute-start.10 = (bf16[96,128]{1,0:T(8,128)(2,1)S(1)}, bf16[96,128]{1,0:T(8,128)(2,1)S(1)}, u32[]{:S(2)}, u32[]{:S(2)}) collective-permute-start(bf16[96,128]{1,0:T(8,128)(2,1)S(1)} %get-tuple-element.78), channel_id=1, source_target_pairs={{0,31},{1,2},{2,1},{3,4},{4,3},{5,6},{6,5},{7,8},{8,7},{9,10},{10,... | collective-permute-start | bytes 73736 | tf_op jit(solution)/shard_map/ppermute | solution.py:549
  64.4 3.8 %collective-permute-start.11 = (bf16[96,128]{1,0:T(8,128)(2,1)S(1)}, bf16[96,128]{1,0:T(8,128)(2,1)S(1)}, u32[]{:S(2)}, u32[]{:S(2)}) collective-permute-start(bf16[96,128]{1,0:T(8,128)(2,1)S(1)} %get-tuple-element.79), channel_id=1, source_target_pairs={{0,1},{1,0},{2,3},{3,2},{4,5},{5,4},{6,7},{7,6},{8,9},{9,8},{10,11... | collective-permute-start | bytes 73736 | tf_op jit(solution)/shard_map/ppermute | solution.py:550

commit v4 on v3

--- a/solution.py
+++ b/solution.py
@@ -14,8 +14,8 @@
 CH = 128
 ROWS = 4 * PATCH_ROWS
 PAIRS = PATCH_ROWS // 2
-FIRST_BATCH, LAST_BATCH = 48, 48
-LEVEL1_BATCH, COND_BATCH = 12, 8
+FIRST_BATCH, LAST_BATCH = 16, 48
+LEVEL1_BATCH, COND_BATCH = 12, 24
 SIDE = 16
 COARSE_SLOTS = 48
 
@@ -275,7 +275,7 @@
         pad_store(pooled1, FIRST_BATCH * c, 0.25 * (summed[:, :, 0] + summed[:, :, 1]), 4)
         return carry
 
-    lax.fori_loop(0, PAIRS // FIRST_BATCH, first, 0)
+    lax.fori_loop(0, PAIRS // FIRST_BATCH, first, 0, unroll=True)
 
     def one(c, carry):
         act = norm_silu(conv_rows(pooled1, level_w[0], LEVEL1_BATCH * c, LEVEL1_BATCH, 4), mean_w[...])
@@ -283,7 +283,7 @@
         pad_store(pooled2, LEVEL1_BATCH * c, halve(act, LEVEL1_BATCH, 4), 2)
         return carry
 
-    lax.fori_loop(0, 24 // LEVEL1_BATCH, one, 0)
+    lax.fori_loop(0, 24 // LEVEL1_BATCH, one, 0, unroll=True)
 
     act = norm_silu(conv_rows(pooled2, level_w[1], 0, 12, 2), mean_w[...])
     level2[...] = act.reshape(12, 32, 256)

time: 69.2 us -> 68.1 us (0.984)
  Pallas kernels: 27.4 us -> 26.5 us
    pallas_call x8, Pallas kernels: 27.4 us -> 26.5 us  [call(): pl.pallas_call(kernel, out_shape=outs, in_specs=[pl.BlockSpec(memory_spac...]
where the time goes in v4:
time: 68.1 us; the launch traced here: 68 us
  Pallas kernels  26.5 us (39%)
  starting transfers between devices  21.6 us (32%)
  waiting for transfers between devices  19.7 us (29%)
    pallas_call x8, Pallas kernels, call(): pl.pallas_call(kernel, out_shape=outs, in_specs=[pl.BlockSpec(memory_spac...  26.5 us
    ppermute x3, starting transfers between devices, swap_rows(): lax.ppermute(to_lower, 'lat', up)  9.83 us
    ppermute x3, waiting for transfers between devices, swap_cols(): from_far = lax.ppermute(to_far, 'lon', far)  9.66 us
    ppermute x3, starting transfers between devices, swap_cols(): from_far = lax.ppermute(to_far, 'lon', far)  8.12 us
    ppermute x3, waiting for transfers between devices, swap_rows(): lax.ppermute(to_upper, 'lat', down)  6.2 us
    ppermute x3, waiting for transfers between devices, swap_rows(): lax.ppermute(to_lower, 'lat', up)  3.88 us
    ppermute x3, starting transfers between devices, swap_rows(): lax.ppermute(to_upper, 'lat', down)  3.69 us
  transfers between devices with their start and end apart: 12, of which 8 were waited for; matrix products, arithmetic and copies ran while one was open for 0% of the time, Pallas kernels for 4%

profile of v4, /device:TPU:6, one launch (start us, length us, event | category | flops | bytes accessed | tf_op | source)
XLA Modules:
  0.0 68.0 jit_solution(9193072767919329282)
XLA Ops:
  0.0 1.0 %shard_map.182 = (bf16[192,128]{1,0:T(8,128)(2,1)S(1)}, bf16[192,128]{1,0:T(8,128)(2,1)S(1)}, f32[2,192,128]{2,1,0:T(8,128)S(1)}, f32[96,128]{1,0:T(8,128)S(1)}) custom-call(f32[4,48,80]{2,1,0:T(8,128)} %noise_init.1, f32[4,48,80]{2,1,0:T(8,128)} %noise_churn.1, bf16[10,6,40]{2,1,0:T(8,128)(2,1)} %bitcast.5), custom_call_target="tpu_custom_call" | custom-call | tf_op jit(solution)/shard_map/pallas_call | solution.py:523
  1.0 3.3 %collective-permute-start = (bf16[192,128]{1,0:T(8,128)(2,1)S(1)}, bf16[192,128]{1,0:T(8,128)(2,1)S(1)}, u32[]{:S(2)}, u32[]{:S(2)}) collective-permute-start(bf16[192,128]{1,0:T(8,128)(2,1)S(1)} %get-tuple-element.46), channel_id=1, source_target_pairs={{0,32},{32,64},{64,96},{96,128},{128,160},{160,192},{192,224},{224... | collective-permute-start | bytes 147464 | tf_op jit(solution)/shard_map/ppermute | solution.py:546
  4.3 1.2 %collective-permute-start.1 = (bf16[192,128]{1,0:T(8,128)(2,1)S(1)}, bf16[192,128]{1,0:T(8,128)(2,1)S(1)}, u32[]{:S(2)}, u32[]{:S(2)}) collective-permute-start(bf16[192,128]{1,0:T(8,128)(2,1)S(1)} %get-tuple-element.47), channel_id=1, source_target_pairs={{32,0},{64,32},{96,64},{128,96},{160,128},{192,160},{224,192},{0,2... | collective-permute-start | bytes 147464 | tf_op jit(solution)/shard_map/ppermute | solution.py:546
  5.6 2.7 %shard_map.181 = (bf16[128,256]{1,0:T(8,128)(2,1)S(1)}, bf16[256,256]{1,0:T(8,128)(2,1)S(1)}, bf16[256,256]{1,0:T(8,128)(2,1)S(1)}, bf16[3,1536,256]{2,1,0:T(8,1...) custom-call(bf16[36,128]{1,0:T(8,128)(2,1)} %bitcast.8, ...), custom_call_target="tpu_custom_call" | custom-call | flops 150994944 | bytes 4194304 | tf_op jit(solution)/shard_map/pallas_call | solution.py:523
  8.3 0.0 collective-permute-done.from_upper
  8.3 1.6 %collective-permute-done.1.from_lower = bf16[192,128]{1,0:T(8,128)(2,1)S(1)} collective-permute-done((bf16[192,128]{1,0:T(8,128)(2,1)S(1)}, bf16[192,128]{1,0:T(8,128)(2,1)S(1)}, u32[]{:S(2)}, u32[]{:S(2)}) %collective-permute-start.1) | collective-permute-done | bytes 49184 | tf_op jit(solution)/shard_map/ppermute | solution.py:546
  9.9 0.3 shard_map.183
  10.2 4.6 %collective-permute-start.2 = (bf16[288,128]{1,0:T(8,128)(2,1)S(1)}, bf16[288,128]{1,0:T(8,128)(2,1)S(1)}, u32[]{:S(2)}, u32[]{:S(2)}) collective-permute-start(bf16[288,128]{1,0:T(8,128)(2,1)S(1)} %get-tuple-element.52), channel_id=1, source_target_pairs={{0,31},{1,2},{2,1},{3,4},{4,3},{5,6},{6,5},{7,8},{8,7},{9,10},{10,... | collective-permute-start | bytes 221192 | tf_op jit(solution)/shard_map/ppermute | solution.py:549
  14.8 0.0 collective-permute-start.3
  14.8 2.0 %collective-permute-done.2.from_far = bf16[288,128]{1,0:T(8,128)(2,1)S(1)} collective-permute-done((bf16[288,128]{1,0:T(8,128)(2,1)S(1)}, bf16[288,128]{1,0:T(8,128)(2,1)S(1)}, u32[]{:S(2)}, u32[]{:S(2)}) %collective-permute-start.2) | collective-permute-done | bytes 73760 | tf_op jit(solution)/shard_map/ppermute | solution.py:549
  16.9 0.0 collective-permute-done.3.from_near
  16.9 11.6 %shard_map.184 = (f32[384,128]{1,0:T(8,128)S(1)}, bf16[192,128]{1,0:T(8,128)(2,1)S(1)}, bf16[192,128]{1,0:T(8,128)(2,1)S(1)}, f32[384,128]{1,0:T(8,128)S(1)}, f3...) custom-call(s32[384]{0:T(512)} %row_map.1, f32[384]{0:T(512)} %row_frac.1, f32[8,128]{1,0:T(8,128)S(1)} %get-tuple-element.43.flags, ...), custom_call_target="tpu_custom_call" | custom-call | flops 5000000000 | bytes 8388608 | tf_op jit(solution)/shard_map/pallas_call | solution.py:523
  28.4 3.5 %collective-permute-start.4 = (bf16[192,128]{1,0:T(8,128)(2,1)S(1)}, bf16[192,128]{1,0:T(8,128)(2,1)S(1)}, u32[]{:S(2)}, u32[]{:S(2)}) collective-permute-start(bf16[192,128]{1,0:T(8,128)(2,1)S(1)} %get-tuple-element.66), channel_id=1, source_target_pairs={{0,32},{32,64},{64,96},{96,128},{128,160},{160,192},{192,224},{224... | collective-permute-start | bytes 147464 | tf_op jit(solution)/shard_map/ppermute | solution.py:546
  32.0 1.0 %collective-permute-start.5 = (bf16[192,128]{1,0:T(8,128)(2,1)S(1)}, bf16[192,128]{1,0:T(8,128)(2,1)S(1)}, u32[]{:S(2)}, u32[]{:S(2)}) collective-permute-start(bf16[192,128]{1,0:T(8,128)(2,1)S(1)} %get-tuple-element.67), channel_id=1, source_target_pairs={{32,0},{64,32},{96,64},{128,96},{160,128},{192,160},{224,192},{0,2... | collective-permute-start | bytes 147464 | tf_op jit(solution)/shard_map/ppermute | solution.py:546
  33.0 2.1 %collective-permute-done.4.from_upper = bf16[192,128]{1,0:T(8,128)(2,1)S(1)} collective-permute-done((bf16[192,128]{1,0:T(8,128)(2,1)S(1)}, bf16[192,128]{1,0:T(8,128)(2,1)S(1)}, u32[]{:S(2)}, u32[]{:S(2)}) %collective-permute-start.4) | collective-permute-done | bytes 49184 | tf_op jit(solution)/shard_map/ppermute | solution.py:546
  35.0 2.5 %collective-permute-done.5.from_lower = bf16[192,128]{1,0:T(8,128)(2,1)S(1)} collective-permute-done((bf16[192,128]{1,0:T(8,128)(2,1)S(1)}, bf16[192,128]{1,0:T(8,128)(2,1)S(1)}, u32[]{:S(2)}, u32[]{:S(2)}) %collective-permute-start.5) | collective-permute-done | bytes 49184 | tf_op jit(solution)/shard_map/ppermute | solution.py:546
  37.6 0.1 shard_map.185
  37.7 1.9 %collective-permute-start.6 = (bf16[192,128]{1,0:T(8,128)(2,1)S(1)}, bf16[192,128]{1,0:T(8,128)(2,1)S(1)}, u32[]{:S(2)}, u32[]{:S(2)}) collective-permute-start(bf16[192,128]{1,0:T(8,128)(2,1)S(1)} %get-tuple-element.69), channel_id=1, source_target_pairs={{0,31},{1,2},{2,1},{3,4},{4,3},{5,6},{6,5},{7,8},{8,7},{9,10},{10,... | collective-permute-start | bytes 147464 | tf_op jit(solution)/shard_map/ppermute | solution.py:549
  39.6 0.0 collective-permute-start.7
  39.6 3.8 %collective-permute-done.6.from_far = bf16[192,128]{1,0:T(8,128)(2,1)S(1)} collective-permute-done((bf16[192,128]{1,0:T(8,128)(2,1)S(1)}, bf16[192,128]{1,0:T(8,128)(2,1)S(1)}, u32[]{:S(2)}, u32[]{:S(2)}) %collective-permute-start.6) | collective-permute-done | bytes 49184 | tf_op jit(solution)/shard_map/ppermute | solution.py:549
  43.4 0.0 collective-permute-done.7.from_near
  43.4 9.8 %shard_map.186 = (f32[384,128]{1,0:T(8,128)S(1)}, bf16[96,128]{1,0:T(8,128)(2,1)S(1)}, bf16[96,128]{1,0:T(8,128)(2,1)S(1)}, f32[384,128]{1,0:T(8,128)S(1)}) custom-call(f32[8,128]{1,0:T(8,128)S(1)} %get-tuple-element.43.flags, f32[384,128]{1,0:T(8,128)S(1)} %get-tuple-element.68.total, bf16[192,128]{1,0:T(8,128)(2,1)S(1)} %collective-permute-done.6.from_far, ...), custom_call_target="tpu_custom_call" | custom-call | flops 5000000000 | bytes 8388608 | tf_op jit(solution)/shard_map/pallas_call | solution.py:523
  53.2 3.0 %collective-permute-start.8 = (bf16[96,128]{1,0:T(8,128)(2,1)S(1)}, bf16[96,128]{1,0:T(8,128)(2,1)S(1)}, u32[]{:S(2)}, u32[]{:S(2)}) collective-permute-start(bf16[96,128]{1,0:T(8,128)(2,1)S(1)} %get-tuple-element.75), channel_id=1, source_target_pairs={{0,32},{32,64},{64,96},{96,128},{128,160},{160,192},{192,224},{224... | collective-permute-start | bytes 73736 | tf_op jit(solution)/shard_map/ppermute | solution.py:546
  56.3 1.5 %collective-permute-start.9 = (bf16[96,128]{1,0:T(8,128)(2,1)S(1)}, bf16[96,128]{1,0:T(8,128)(2,1)S(1)}, u32[]{:S(2)}, u32[]{:S(2)}) collective-permute-start(bf16[96,128]{1,0:T(8,128)(2,1)S(1)} %get-tuple-element.76), channel_id=1, source_target_pairs={{32,0},{64,32},{96,64},{128,96},{160,128},{192,160},{224,192},{0,2... | collective-permute-start | bytes 73736 | tf_op jit(solution)/shard_map/ppermute | solution.py:546
  57.7 1.8 %collective-permute-done.8.from_upper = bf16[96,128]{1,0:T(8,128)(2,1)S(1)} collective-permute-done((bf16[96,128]{1,0:T(8,128)(2,1)S(1)}, bf16[96,128]{1,0:T(8,128)(2,1)S(1)}, u32[]{:S(2)}, u32[]{:S(2)}) %collective-permute-start.8) | collective-permute-done | bytes 24608 | tf_op jit(solution)/shard_map/ppermute | solution.py:546
  59.5 2.0 %collective-permute-done.9.from_lower = bf16[96,128]{1,0:T(8,128)(2,1)S(1)} collective-permute-done((bf16[96,128]{1,0:T(8,128)(2,1)S(1)}, bf16[96,128]{1,0:T(8,128)(2,1)S(1)}, u32[]{:S(2)}, u32[]{:S(2)}) %collective-permute-start.9) | collective-permute-done | bytes 24608 | tf_op jit(solution)/shard_map/ppermute | solution.py:546
  61.6 0.1 shard_map.187
  61.7 1.6 %collective-permute-start.10 = (bf16[96,128]{1,0:T(8,128)(2,1)S(1)}, bf16[96,128]{1,0:T(8,128)(2,1)S(1)}, u32[]{:S(2)}, u32[]{:S(2)}) collective-permute-start(bf16[96,128]{1,0:T(8,128)(2,1)S(1)} %get-tuple-element.78), channel_id=1, source_target_pairs={{0,31},{1,2},{2,1},{3,4},{4,3},{5,6},{6,5},{7,8},{8,7},{9,10},{10,... | collective-permute-start | bytes 73736 | tf_op jit(solution)/shard_map/ppermute | solution.py:549
  63.3 0.0 collective-permute-start.11
  63.3 3.8 %collective-permute-done.10.from_far = bf16[96,128]{1,0:T(8,128)(2,1)S(1)} collective-permute-done((bf16[96,128]{1,0:T(8,128)(2,1)S(1)}, bf16[96,128]{1,0:T(8,128)(2,1)S(1)}, u32[]{:S(2)}, u32[]{:S(2)}) %collective-permute-start.10) | collective-permute-done | bytes 24608 | tf_op jit(solution)/shard_map/ppermute | solution.py:549
  67.1 0.0 collective-permute-done.11.from_near
  67.1 0.8 %shard_map.188 = f32[4,48,80]{2,1,0:T(8,128)} custom-call(f32[8,128]{1,0:T(8,128)S(1)} %get-tuple-element.43.flags, f32[192,128]{1,0:T(8,128)S(1)} %get-tuple-element.77.total, bf16[96,128]{1,0:T(8,128)(2,1)S(1)} %collective-permute-done.10.from_far, bf16[96,128]{1,0:T(8,128)(2,1)S(1)} %collective-permute-done.11.from_near, ...), custom_call_target="tpu_custom_call" | custom-call | tf_op jit(solution)/shard_map/pallas_call | solution.py:523
Async XLA Ops:
  1.0 7.2 %collective-permute-start = (bf16[192,128]{1,0:T(8,128)(2,1)S(1)}, bf16[192,128]{1,0:T(8,128)(2,1)S(1)}, u32[]{:S(2)}, u32[]{:S(2)}) collective-permute-start(bf16[192,128]{1,0:T(8,128)(2,1)S(1)} %get-tuple-element.46), channel_id=1, source_target_pairs={{0,32},{32,64},{64,96},{96,128},{128,160},{160,192},{192,224},{224... | collective-permute-start | bytes 147464 | tf_op jit(solution)/shard_map/ppermute | solution.py:546
  4.3 5.6 %collective-permute-start.1 = (bf16[192,128]{1,0:T(8,128)(2,1)S(1)}, bf16[192,128]{1,0:T(8,128)(2,1)S(1)}, u32[]{:S(2)}, u32[]{:S(2)}) collective-permute-start(bf16[192,128]{1,0:T(8,128)(2,1)S(1)} %get-tuple-element.47), channel_id=1, source_target_pairs={{32,0},{64,32},{96,64},{128,96},{160,128},{192,160},{224,192},{0,2... | collective-permute-start | bytes 147464 | tf_op jit(solution)/shard_map/ppermute | solution.py:546
  10.2 6.6 %collective-permute-start.2 = (bf16[288,128]{1,0:T(8,128)(2,1)S(1)}, bf16[288,128]{1,0:T(8,128)(2,1)S(1)}, u32[]{:S(2)}, u32[]{:S(2)}) collective-permute-start(bf16[288,128]{1,0:T(8,128)(2,1)S(1)} %get-tuple-element.52), channel_id=1, source_target_pairs={{0,31},{1,2},{2,1},{3,4},{4,3},{5,6},{6,5},{7,8},{8,7},{9,10},{10,... | collective-permute-start | bytes 221192 | tf_op jit(solution)/shard_map/ppermute | solution.py:549
  14.8 2.0 %collective-permute-start.3 = (bf16[288,128]{1,0:T(8,128)(2,1)S(1)}, bf16[288,128]{1,0:T(8,128)(2,1)S(1)}, u32[]{:S(2)}, u32[]{:S(2)}) collective-permute-start(bf16[288,128]{1,0:T(8,128)(2,1)S(1)} %get-tuple-element.53), channel_id=1, source_target_pairs={{0,1},{1,0},{2,3},{3,2},{4,5},{5,4},{6,7},{7,6},{8,9},{9,8},{10,11... | collective-permute-start | bytes 221192 | tf_op jit(solution)/shard_map/ppermute | solution.py:550
  28.4 6.6 %collective-permute-start.4 = (bf16[192,128]{1,0:T(8,128)(2,1)S(1)}, bf16[192,128]{1,0:T(8,128)(2,1)S(1)}, u32[]{:S(2)}, u32[]{:S(2)}) collective-permute-start(bf16[192,128]{1,0:T(8,128)(2,1)S(1)} %get-tuple-element.66), channel_id=1, source_target_pairs={{0,32},{32,64},{64,96},{96,128},{128,160},{160,192},{192,224},{224... | collective-permute-start | bytes 147464 | tf_op jit(solution)/shard_map/ppermute | solution.py:546
  32.0 5.6 %collective-permute-start.5 = (bf16[192,128]{1,0:T(8,128)(2,1)S(1)}, bf16[192,128]{1,0:T(8,128)(2,1)S(1)}, u32[]{:S(2)}, u32[]{:S(2)}) collective-permute-start(bf16[192,128]{1,0:T(8,128)(2,1)S(1)} %get-tuple-element.67), channel_id=1, source_target_pairs={{32,0},{64,32},{96,64},{128,96},{160,128},{192,160},{224,192},{0,2... | collective-permute-start | bytes 147464 | tf_op jit(solution)/shard_map/ppermute | solution.py:546
  37.7 5.7 %collective-permute-start.6 = (bf16[192,128]{1,0:T(8,128)(2,1)S(1)}, bf16[192,128]{1,0:T(8,128)(2,1)S(1)}, u32[]{:S(2)}, u32[]{:S(2)}) collective-permute-start(bf16[192,128]{1,0:T(8,128)(2,1)S(1)} %get-tuple-element.69), channel_id=1, source_target_pairs={{0,31},{1,2},{2,1},{3,4},{4,3},{5,6},{6,5},{7,8},{8,7},{9,10},{10,... | collective-permute-start | bytes 147464 | tf_op jit(solution)/shard_map/ppermute | solution.py:549
  39.6 3.8 %collective-permute-start.7 = (bf16[192,128]{1,0:T(8,128)(2,1)S(1)}, bf16[192,128]{1,0:T(8,128)(2,1)S(1)}, u32[]{:S(2)}, u32[]{:S(2)}) collective-permute-start(bf16[192,128]{1,0:T(8,128)(2,1)S(1)} %get-tuple-element.70), channel_id=1, source_target_pairs={{0,1},{1,0},{2,3},{3,2},{4,5},{5,4},{6,7},{7,6},{8,9},{9,8},{10,11... | collective-permute-start | bytes 147464 | tf_op jit(solution)/shard_map/ppermute | solution.py:550
  53.2 6.3 %collective-permute-start.8 = (bf16[96,128]{1,0:T(8,128)(2,1)S(1)}, bf16[96,128]{1,0:T(8,128)(2,1)S(1)}, u32[]{:S(2)}, u32[]{:S(2)}) collective-permute-start(bf16[96,128]{1,0:T(8,128)(2,1)S(1)} %get-tuple-element.75), channel_id=1, source_target_pairs={{0,32},{32,64},{64,96},{96,128},{128,160},{160,192},{192,224},{224... | collective-permute-start | bytes 73736 | tf_op jit(solution)/shard_map/ppermute | solution.py:546
  56.3 5.3 %collective-permute-start.9 = (bf16[96,128]{1,0:T(8,128)(2,1)S(1)}, bf16[96,128]{1,0:T(8,128)(2,1)S(1)}, u32[]{:S(2)}, u32[]{:S(2)}) collective-permute-start(bf16[96,128]{1,0:T(8,128)(2,1)S(1)} %get-tuple-element.76), channel_id=1, source_target_pairs={{32,0},{64,32},{96,64},{128,96},{160,128},{192,160},{224,192},{0,2... | collective-permute-start | bytes 73736 | tf_op jit(solution)/shard_map/ppermute | solution.py:546
  61.7 5.4 %collective-permute-start.10 = (bf16[96,128]{1,0:T(8,128)(2,1)S(1)}, bf16[96,128]{1,0:T(8,128)(2,1)S(1)}, u32[]{:S(2)}, u32[]{:S(2)}) collective-permute-start(bf16[96,128]{1,0:T(8,128)(2,1)S(1)} %get-tuple-element.78), channel_id=1, source_target_pairs={{0,31},{1,2},{2,1},{3,4},{4,3},{5,6},{6,5},{7,8},{8,7},{9,10},{10,... | collective-permute-start | bytes 73736 | tf_op jit(solution)/shard_map/ppermute | solution.py:549
  63.3 3.8 %collective-permute-start.11 = (bf16[96,128]{1,0:T(8,128)(2,1)S(1)}, bf16[96,128]{1,0:T(8,128)(2,1)S(1)}, u32[]{:S(2)}, u32[]{:S(2)}) collective-permute-start(bf16[96,128]{1,0:T(8,128)(2,1)S(1)} %get-tuple-element.79), channel_id=1, source_target_pairs={{0,1},{1,0},{2,3},{3,2},{4,5},{5,4},{6,7},{7,6},{8,9},{9,8},{10,11... | collective-permute-start | bytes 73736 | tf_op jit(solution)/shard_map/ppermute | solution.py:550

commit v5 on v4

--- a/solution.py
+++ b/solution.py
@@ -15,7 +15,7 @@
 ROWS = 4 * PATCH_ROWS
 PAIRS = PATCH_ROWS // 2
 FIRST_BATCH, LAST_BATCH = 16, 48
-LEVEL1_BATCH, COND_BATCH = 12, 24
+LEVEL1_BATCH, COND_BATCH = 12, 48
 SIDE = 16
 COARSE_SLOTS = 48
 
@@ -327,7 +327,7 @@
                 taps_b[shift, pl.ds(row + 8, 8), :] = taps[16 * shift + 8 : 16 * shift + 16]
         return carry
 
-    lax.fori_loop(0, PAIRS // LAST_BATCH, last, 0)
+    lax.fori_loop(0, PAIRS // LAST_BATCH, last, 0, unroll=True)
 
     parts = []
     for shift in range(3):
@@ -430,7 +430,7 @@
         cond_rows[pl.ds(COND_BATCH * c, COND_BATCH)] = fine.astype(BF16).reshape(COND_BATCH, 80, 128)
         return carry
 
-    lax.fori_loop(0, PAIRS // COND_BATCH, interpolate, 0)
+    lax.fori_loop(0, PAIRS // COND_BATCH, interpolate, 0, unroll=True)
 
     denoise(
         state, cond_rows, (first_w, expand_w, project_w, level_w, last_level_w, final_w),

time: 68.1 us -> 67.8 us (level)
  no operation moved by 1% of the time
where the time goes in v5:
time: 67.8 us; the launch traced here: 67.7 us
  Pallas kernels  26.2 us (39%)
  starting transfers between devices  21.6 us (32%)
  waiting for transfers between devices  19.8 us (29%)
    pallas_call x8, Pallas kernels, call(): pl.pallas_call(kernel, out_shape=outs, in_specs=[pl.BlockSpec(memory_spac...  26.2 us
    ppermute x3, starting transfers between devices, swap_rows(): lax.ppermute(to_lower, 'lat', up)  9.84 us
    ppermute x3, waiting for transfers between devices, swap_cols(): from_far = lax.ppermute(to_far, 'lon', far)  9.7 us
    ppermute x3, starting transfers between devices, swap_cols(): from_far = lax.ppermute(to_far, 'lon', far)  8.07 us
    ppermute x3, waiting for transfers between devices, swap_rows(): lax.ppermute(to_upper, 'lat', down)  6.21 us
    ppermute x3, waiting for transfers between devices, swap_rows(): lax.ppermute(to_lower, 'lat', up)  3.88 us
    ppermute x3, starting transfers between devices, swap_rows(): lax.ppermute(to_upper, 'lat', down)  3.68 us
  transfers between devices with their start and end apart: 12, of which 8 were waited for; matrix products, arithmetic and copies ran while one was open for 0% of the time, Pallas kernels for 4%

profile of v5, /device:TPU:6, one launch (start us, length us, event | category | flops | bytes accessed | tf_op | source)
XLA Modules:
  0.0 67.7 jit_solution(1428619675394479574)
XLA Ops:
  0.0 1.0 %shard_map.182 = (bf16[192,128]{1,0:T(8,128)(2,1)S(1)}, bf16[192,128]{1,0:T(8,128)(2,1)S(1)}, f32[2,192,128]{2,1,0:T(8,128)S(1)}, f32[96,128]{1,0:T(8,128)S(1)}) custom-call(f32[4,48,80]{2,1,0:T(8,128)} %noise_init.1, f32[4,48,80]{2,1,0:T(8,128)} %noise_churn.1, bf16[10,6,40]{2,1,0:T(8,128)(2,1)} %bitcast.5), custom_call_target="tpu_custom_call" | custom-call | tf_op jit(solution)/shard_map/pallas_call | solution.py:523
  1.0 3.3 %collective-permute-start = (bf16[192,128]{1,0:T(8,128)(2,1)S(1)}, bf16[192,128]{1,0:T(8,128)(2,1)S(1)}, u32[]{:S(2)}, u32[]{:S(2)}) collective-permute-start(bf16[192,128]{1,0:T(8,128)(2,1)S(1)} %get-tuple-element.46), channel_id=1, source_target_pairs={{0,32},{32,64},{64,96},{96,128},{128,160},{160,192},{192,224},{224... | collective-permute-start | bytes 147464 | tf_op jit(solution)/shard_map/ppermute | solution.py:546
  4.3 1.2 %collective-permute-start.1 = (bf16[192,128]{1,0:T(8,128)(2,1)S(1)}, bf16[192,128]{1,0:T(8,128)(2,1)S(1)}, u32[]{:S(2)}, u32[]{:S(2)}) collective-permute-start(bf16[192,128]{1,0:T(8,128)(2,1)S(1)} %get-tuple-element.47), channel_id=1, source_target_pairs={{32,0},{64,32},{96,64},{128,96},{160,128},{192,160},{224,192},{0,2... | collective-permute-start | bytes 147464 | tf_op jit(solution)/shard_map/ppermute | solution.py:546
  5.6 2.7 %shard_map.181 = (bf16[128,256]{1,0:T(8,128)(2,1)S(1)}, bf16[256,256]{1,0:T(8,128)(2,1)S(1)}, bf16[256,256]{1,0:T(8,128)(2,1)S(1)}, bf16[3,1536,256]{2,1,0:T(8,1...) custom-call(bf16[36,128]{1,0:T(8,128)(2,1)} %bitcast.8, ...), custom_call_target="tpu_custom_call" | custom-call | flops 150994944 | bytes 4194304 | tf_op jit(solution)/shard_map/pallas_call | solution.py:523
  8.3 0.0 collective-permute-done.from_upper
  8.3 1.6 %collective-permute-done.1.from_lower = bf16[192,128]{1,0:T(8,128)(2,1)S(1)} collective-permute-done((bf16[192,128]{1,0:T(8,128)(2,1)S(1)}, bf16[192,128]{1,0:T(8,128)(2,1)S(1)}, u32[]{:S(2)}, u32[]{:S(2)}) %collective-permute-start.1) | collective-permute-done | bytes 49184 | tf_op jit(solution)/shard_map/ppermute | solution.py:546
  9.9 0.3 shard_map.183
  10.2 4.6 %collective-permute-start.2 = (bf16[288,128]{1,0:T(8,128)(2,1)S(1)}, bf16[288,128]{1,0:T(8,128)(2,1)S(1)}, u32[]{:S(2)}, u32[]{:S(2)}) collective-permute-start(bf16[288,128]{1,0:T(8,128)(2,1)S(1)} %get-tuple-element.52), channel_id=1, source_target_pairs={{0,31},{1,2},{2,1},{3,4},{4,3},{5,6},{6,5},{7,8},{8,7},{9,10},{10,... | collective-permute-start | bytes 221192 | tf_op jit(solution)/shard_map/ppermute | solution.py:549
  14.8 0.0 collective-permute-start.3
  14.8 2.0 %collective-permute-done.2.from_far = bf16[288,128]{1,0:T(8,128)(2,1)S(1)} collective-permute-done((bf16[288,128]{1,0:T(8,128)(2,1)S(1)}, bf16[288,128]{1,0:T(8,128)(2,1)S(1)}, u32[]{:S(2)}, u32[]{:S(2)}) %collective-permute-start.2) | collective-permute-done | bytes 73760 | tf_op jit(solution)/shard_map/ppermute | solution.py:549
  16.9 0.0 collective-permute-done.3.from_near
  16.9 11.3 %shard_map.184 = (f32[384,128]{1,0:T(8,128)S(1)}, bf16[192,128]{1,0:T(8,128)(2,1)S(1)}, bf16[192,128]{1,0:T(8,128)(2,1)S(1)}, f32[384,128]{1,0:T(8,128)S(1)}, f3...) custom-call(s32[384]{0:T(512)} %row_map.1, f32[384]{0:T(512)} %row_frac.1, f32[8,128]{1,0:T(8,128)S(1)} %get-tuple-element.43.flags, ...), custom_call_target="tpu_custom_call" | custom-call | flops 5000000000 | bytes 8388608 | tf_op jit(solution)/shard_map/pallas_call | solution.py:523
  28.1 3.5 %collective-permute-start.4 = (bf16[192,128]{1,0:T(8,128)(2,1)S(1)}, bf16[192,128]{1,0:T(8,128)(2,1)S(1)}, u32[]{:S(2)}, u32[]{:S(2)}) collective-permute-start(bf16[192,128]{1,0:T(8,128)(2,1)S(1)} %get-tuple-element.66), channel_id=1, source_target_pairs={{0,32},{32,64},{64,96},{96,128},{128,160},{160,192},{192,224},{224... | collective-permute-start | bytes 147464 | tf_op jit(solution)/shard_map/ppermute | solution.py:546
  31.6 1.0 %collective-permute-start.5 = (bf16[192,128]{1,0:T(8,128)(2,1)S(1)}, bf16[192,128]{1,0:T(8,128)(2,1)S(1)}, u32[]{:S(2)}, u32[]{:S(2)}) collective-permute-start(bf16[192,128]{1,0:T(8,128)(2,1)S(1)} %get-tuple-element.67), channel_id=1, source_target_pairs={{32,0},{64,32},{96,64},{128,96},{160,128},{192,160},{224,192},{0,2... | collective-permute-start | bytes 147464 | tf_op jit(solution)/shard_map/ppermute | solution.py:546
  32.6 2.1 %collective-permute-done.4.from_upper = bf16[192,128]{1,0:T(8,128)(2,1)S(1)} collective-permute-done((bf16[192,128]{1,0:T(8,128)(2,1)S(1)}, bf16[192,128]{1,0:T(8,128)(2,1)S(1)}, u32[]{:S(2)}, u32[]{:S(2)}) %collective-permute-start.4) | collective-permute-done | bytes 49184 | tf_op jit(solution)/shard_map/ppermute | solution.py:546
  34.7 2.5 %collective-permute-done.5.from_lower = bf16[192,128]{1,0:T(8,128)(2,1)S(1)} collective-permute-done((bf16[192,128]{1,0:T(8,128)(2,1)S(1)}, bf16[192,128]{1,0:T(8,128)(2,1)S(1)}, u32[]{:S(2)}, u32[]{:S(2)}) %collective-permute-start.5) | collective-permute-done | bytes 49184 | tf_op jit(solution)/shard_map/ppermute | solution.py:546
  37.2 0.1 shard_map.185
  37.4 1.9 %collective-permute-start.6 = (bf16[192,128]{1,0:T(8,128)(2,1)S(1)}, bf16[192,128]{1,0:T(8,128)(2,1)S(1)}, u32[]{:S(2)}, u32[]{:S(2)}) collective-permute-start(bf16[192,128]{1,0:T(8,128)(2,1)S(1)} %get-tuple-element.69), channel_id=1, source_target_pairs={{0,31},{1,2},{2,1},{3,4},{4,3},{5,6},{6,5},{7,8},{8,7},{9,10},{10,... | collective-permute-start | bytes 147464 | tf_op jit(solution)/shard_map/ppermute | solution.py:549
  39.3 0.0 collective-permute-start.7
  39.3 3.8 %collective-permute-done.6.from_far = bf16[192,128]{1,0:T(8,128)(2,1)S(1)} collective-permute-done((bf16[192,128]{1,0:T(8,128)(2,1)S(1)}, bf16[192,128]{1,0:T(8,128)(2,1)S(1)}, u32[]{:S(2)}, u32[]{:S(2)}) %collective-permute-start.6) | collective-permute-done | bytes 49184 | tf_op jit(solution)/shard_map/ppermute | solution.py:549
  43.1 0.0 collective-permute-done.7.from_near
  43.1 9.8 %shard_map.186 = (f32[384,128]{1,0:T(8,128)S(1)}, bf16[96,128]{1,0:T(8,128)(2,1)S(1)}, bf16[96,128]{1,0:T(8,128)(2,1)S(1)}, f32[384,128]{1,0:T(8,128)S(1)}) custom-call(f32[8,128]{1,0:T(8,128)S(1)} %get-tuple-element.43.flags, f32[384,128]{1,0:T(8,128)S(1)} %get-tuple-element.68.total, bf16[192,128]{1,0:T(8,128)(2,1)S(1)} %collective-permute-done.6.from_far, ...), custom_call_target="tpu_custom_call" | custom-call | flops 5000000000 | bytes 8388608 | tf_op jit(solution)/shard_map/pallas_call | solution.py:523
  52.9 3.1 %collective-permute-start.8 = (bf16[96,128]{1,0:T(8,128)(2,1)S(1)}, bf16[96,128]{1,0:T(8,128)(2,1)S(1)}, u32[]{:S(2)}, u32[]{:S(2)}) collective-permute-start(bf16[96,128]{1,0:T(8,128)(2,1)S(1)} %get-tuple-element.75), channel_id=1, source_target_pairs={{0,32},{32,64},{64,96},{96,128},{128,160},{160,192},{192,224},{224... | collective-permute-start | bytes 73736 | tf_op jit(solution)/shard_map/ppermute | solution.py:546
  56.0 1.5 %collective-permute-start.9 = (bf16[96,128]{1,0:T(8,128)(2,1)S(1)}, bf16[96,128]{1,0:T(8,128)(2,1)S(1)}, u32[]{:S(2)}, u32[]{:S(2)}) collective-permute-start(bf16[96,128]{1,0:T(8,128)(2,1)S(1)} %get-tuple-element.76), channel_id=1, source_target_pairs={{32,0},{64,32},{96,64},{128,96},{160,128},{192,160},{224,192},{0,2... | collective-permute-start | bytes 73736 | tf_op jit(solution)/shard_map/ppermute | solution.py:546
  57.4 1.8 %collective-permute-done.8.from_upper = bf16[96,128]{1,0:T(8,128)(2,1)S(1)} collective-permute-done((bf16[96,128]{1,0:T(8,128)(2,1)S(1)}, bf16[96,128]{1,0:T(8,128)(2,1)S(1)}, u32[]{:S(2)}, u32[]{:S(2)}) %collective-permute-start.8) | collective-permute-done | bytes 24608 | tf_op jit(solution)/shard_map/ppermute | solution.py:546
  59.2 2.1 %collective-permute-done.9.from_lower = bf16[96,128]{1,0:T(8,128)(2,1)S(1)} collective-permute-done((bf16[96,128]{1,0:T(8,128)(2,1)S(1)}, bf16[96,128]{1,0:T(8,128)(2,1)S(1)}, u32[]{:S(2)}, u32[]{:S(2)}) %collective-permute-start.9) | collective-permute-done | bytes 24608 | tf_op jit(solution)/shard_map/ppermute | solution.py:546
  61.3 0.1 shard_map.187
  61.4 1.6 %collective-permute-start.10 = (bf16[96,128]{1,0:T(8,128)(2,1)S(1)}, bf16[96,128]{1,0:T(8,128)(2,1)S(1)}, u32[]{:S(2)}, u32[]{:S(2)}) collective-permute-start(bf16[96,128]{1,0:T(8,128)(2,1)S(1)} %get-tuple-element.78), channel_id=1, source_target_pairs={{0,31},{1,2},{2,1},{3,4},{4,3},{5,6},{6,5},{7,8},{8,7},{9,10},{10,... | collective-permute-start | bytes 73736 | tf_op jit(solution)/shard_map/ppermute | solution.py:549
  63.0 0.0 collective-permute-start.11
  63.0 3.9 %collective-permute-done.10.from_far = bf16[96,128]{1,0:T(8,128)(2,1)S(1)} collective-permute-done((bf16[96,128]{1,0:T(8,128)(2,1)S(1)}, bf16[96,128]{1,0:T(8,128)(2,1)S(1)}, u32[]{:S(2)}, u32[]{:S(2)}) %collective-permute-start.10) | collective-permute-done | bytes 24608 | tf_op jit(solution)/shard_map/ppermute | solution.py:549
  66.8 0.0 collective-permute-done.11.from_near
  66.8 0.8 %shard_map.188 = f32[4,48,80]{2,1,0:T(8,128)} custom-call(f32[8,128]{1,0:T(8,128)S(1)} %get-tuple-element.43.flags, f32[192,128]{1,0:T(8,128)S(1)} %get-tuple-element.77.total, bf16[96,128]{1,0:T(8,128)(2,1)S(1)} %collective-permute-done.10.from_far, bf16[96,128]{1,0:T(8,128)(2,1)S(1)} %collective-permute-done.11.from_near, ...), custom_call_target="tpu_custom_call" | custom-call | tf_op jit(solution)/shard_map/pallas_call | solution.py:523
Async XLA Ops:
  1.0 7.2 %collective-permute-start = (bf16[192,128]{1,0:T(8,128)(2,1)S(1)}, bf16[192,128]{1,0:T(8,128)(2,1)S(1)}, u32[]{:S(2)}, u32[]{:S(2)}) collective-permute-start(bf16[192,128]{1,0:T(8,128)(2,1)S(1)} %get-tuple-element.46), channel_id=1, source_target_pairs={{0,32},{32,64},{64,96},{96,128},{128,160},{160,192},{192,224},{224... | collective-permute-start | bytes 147464 | tf_op jit(solution)/shard_map/ppermute | solution.py:546
  4.3 5.6 %collective-permute-start.1 = (bf16[192,128]{1,0:T(8,128)(2,1)S(1)}, bf16[192,128]{1,0:T(8,128)(2,1)S(1)}, u32[]{:S(2)}, u32[]{:S(2)}) collective-permute-start(bf16[192,128]{1,0:T(8,128)(2,1)S(1)} %get-tuple-element.47), channel_id=1, source_target_pairs={{32,0},{64,32},{96,64},{128,96},{160,128},{192,160},{224,192},{0,2... | collective-permute-start | bytes 147464 | tf_op jit(solution)/shard_map/ppermute | solution.py:546
  10.2 6.6 %collective-permute-start.2 = (bf16[288,128]{1,0:T(8,128)(2,1)S(1)}, bf16[288,128]{1,0:T(8,128)(2,1)S(1)}, u32[]{:S(2)}, u32[]{:S(2)}) collective-permute-start(bf16[288,128]{1,0:T(8,128)(2,1)S(1)} %get-tuple-element.52), channel_id=1, source_target_pairs={{0,31},{1,2},{2,1},{3,4},{4,3},{5,6},{6,5},{7,8},{8,7},{9,10},{10,... | collective-permute-start | bytes 221192 | tf_op jit(solution)/shard_map/ppermute | solution.py:549
  14.8 2.0 %collective-permute-start.3 = (bf16[288,128]{1,0:T(8,128)(2,1)S(1)}, bf16[288,128]{1,0:T(8,128)(2,1)S(1)}, u32[]{:S(2)}, u32[]{:S(2)}) collective-permute-start(bf16[288,128]{1,0:T(8,128)(2,1)S(1)} %get-tuple-element.53), channel_id=1, source_target_pairs={{0,1},{1,0},{2,3},{3,2},{4,5},{5,4},{6,7},{7,6},{8,9},{9,8},{10,11... | collective-permute-start | bytes 221192 | tf_op jit(solution)/shard_map/ppermute | solution.py:550
  28.1 6.6 %collective-permute-start.4 = (bf16[192,128]{1,0:T(8,128)(2,1)S(1)}, bf16[192,128]{1,0:T(8,128)(2,1)S(1)}, u32[]{:S(2)}, u32[]{:S(2)}) collective-permute-start(bf16[192,128]{1,0:T(8,128)(2,1)S(1)} %get-tuple-element.66), channel_id=1, source_target_pairs={{0,32},{32,64},{64,96},{96,128},{128,160},{160,192},{192,224},{224... | collective-permute-start | bytes 147464 | tf_op jit(solution)/shard_map/ppermute | solution.py:546
  31.6 5.6 %collective-permute-start.5 = (bf16[192,128]{1,0:T(8,128)(2,1)S(1)}, bf16[192,128]{1,0:T(8,128)(2,1)S(1)}, u32[]{:S(2)}, u32[]{:S(2)}) collective-permute-start(bf16[192,128]{1,0:T(8,128)(2,1)S(1)} %get-tuple-element.67), channel_id=1, source_target_pairs={{32,0},{64,32},{96,64},{128,96},{160,128},{192,160},{224,192},{0,2... | collective-permute-start | bytes 147464 | tf_op jit(solution)/shard_map/ppermute | solution.py:546
  37.4 5.7 %collective-permute-start.6 = (bf16[192,128]{1,0:T(8,128)(2,1)S(1)}, bf16[192,128]{1,0:T(8,128)(2,1)S(1)}, u32[]{:S(2)}, u32[]{:S(2)}) collective-permute-start(bf16[192,128]{1,0:T(8,128)(2,1)S(1)} %get-tuple-element.69), channel_id=1, source_target_pairs={{0,31},{1,2},{2,1},{3,4},{4,3},{5,6},{6,5},{7,8},{8,7},{9,10},{10,... | collective-permute-start | bytes 147464 | tf_op jit(solution)/shard_map/ppermute | solution.py:549
  39.3 3.8 %collective-permute-start.7 = (bf16[192,128]{1,0:T(8,128)(2,1)S(1)}, bf16[192,128]{1,0:T(8,128)(2,1)S(1)}, u32[]{:S(2)}, u32[]{:S(2)}) collective-permute-start(bf16[192,128]{1,0:T(8,128)(2,1)S(1)} %get-tuple-element.70), channel_id=1, source_target_pairs={{0,1},{1,0},{2,3},{3,2},{4,5},{5,4},{6,7},{7,6},{8,9},{9,8},{10,11... | collective-permute-start | bytes 147464 | tf_op jit(solution)/shard_map/ppermute | solution.py:550
  52.9 6.3 %collective-permute-start.8 = (bf16[96,128]{1,0:T(8,128)(2,1)S(1)}, bf16[96,128]{1,0:T(8,128)(2,1)S(1)}, u32[]{:S(2)}, u32[]{:S(2)}) collective-permute-start(bf16[96,128]{1,0:T(8,128)(2,1)S(1)} %get-tuple-element.75), channel_id=1, source_target_pairs={{0,32},{32,64},{64,96},{96,128},{128,160},{160,192},{192,224},{224... | collective-permute-start | bytes 73736 | tf_op jit(solution)/shard_map/ppermute | solution.py:546
  56.0 5.3 %collective-permute-start.9 = (bf16[96,128]{1,0:T(8,128)(2,1)S(1)}, bf16[96,128]{1,0:T(8,128)(2,1)S(1)}, u32[]{:S(2)}, u32[]{:S(2)}) collective-permute-start(bf16[96,128]{1,0:T(8,128)(2,1)S(1)} %get-tuple-element.76), channel_id=1, source_target_pairs={{32,0},{64,32},{96,64},{128,96},{160,128},{192,160},{224,192},{0,2... | collective-permute-start | bytes 73736 | tf_op jit(solution)/shard_map/ppermute | solution.py:546
  61.4 5.4 %collective-permute-start.10 = (bf16[96,128]{1,0:T(8,128)(2,1)S(1)}, bf16[96,128]{1,0:T(8,128)(2,1)S(1)}, u32[]{:S(2)}, u32[]{:S(2)}) collective-permute-start(bf16[96,128]{1,0:T(8,128)(2,1)S(1)} %get-tuple-element.78), channel_id=1, source_target_pairs={{0,31},{1,2},{2,1},{3,4},{4,3},{5,6},{6,5},{7,8},{8,7},{9,10},{10,... | collective-permute-start | bytes 73736 | tf_op jit(solution)/shard_map/ppermute | solution.py:549
  63.0 3.9 %collective-permute-start.11 = (bf16[96,128]{1,0:T(8,128)(2,1)S(1)}, bf16[96,128]{1,0:T(8,128)(2,1)S(1)}, u32[]{:S(2)}, u32[]{:S(2)}) collective-permute-start(bf16[96,128]{1,0:T(8,128)(2,1)S(1)} %get-tuple-element.79), channel_id=1, source_target_pairs={{0,1},{1,0},{2,3},{3,2},{4,5},{5,4},{6,7},{7,6},{8,9},{9,8},{10,11... | collective-permute-start | bytes 73736 | tf_op jit(solution)/shard_map/ppermute | solution.py:550
